TPU v7x, 32 devices: a whole 2x2x4 slice. The times are simulated.
32 devices in a mesh: branch: 2 (over y), trow: 2 (over x), tcol: 8 (over z, core).
Axes of the slice: x: 2, y: 2, z: 4, core: 2. Of those that a mesh axis runs over, the one named last changes fastest.
Arguments:
- latent: bfloat16 [2, 2, 16, 64, 1152], P('branch', None, 'trow', 'tcol'), may hold values from -6 to 6
- modulation: float32 [2, 3, 1152], replicated, may hold values from -2 to 2
- w_query: bfloat16 [2, 1152, 576], P('branch', None, 'tcol'), may hold values from -0.176776695 to 0.176776695
- w_keyval: bfloat16 [2, 1152, 1152], P('branch', None, 'tcol'), may hold values from -3.8301617 to 3.8301617
- w_out: bfloat16 [2, 576, 1152], P('branch', 'tcol'), may hold values from -0.25 to 0.25
- w_zero: bfloat16 [1152, 1152], P(None, 'tcol'), may hold values from -0.1875 to 0.1875
Outputs:
- hidden_out: bfloat16 [2, 2, 16, 64, 1152], P('branch', None, 'trow', 'tcol')
All inputs are finite; a program needn't handle non-finite values.
Results may differ from a plain program's by a relative error of at most 0.0075.
Values may be sent and summed in bfloat16 or wider, within the bound.
No kernel may reach another device: no remote copies, remote signals or barrier semaphores. Data moves between devices by JAX's collectives and lax.ppermute only.
A program may use at most 128 MiB of HBM per device.

v0:
```python
import math

import jax
import jax.numpy as jnp
from jax import lax
from jax.sharding import PartitionSpec as P

D = 1152
HD = 72
HEADS = 8
WIN = 13
HW = 576


def padded(block, sides, width):
    for axis, dim in sides:
        count = lax.axis_size(axis)
        forward = [(i, i + 1) for i in range(count - 1)]
        backward = [(target, source) for source, target in forward]
        low = lax.ppermute(
            lax.slice_in_dim(block, block.shape[dim] - width, None, axis=dim), axis, forward
        )
        high = lax.ppermute(lax.slice_in_dim(block, 0, width, axis=dim), axis, backward)
        block = jnp.concatenate([low, block, high], axis=dim)
    return block


def shifted(block, axis, distance):
    devices = range(lax.axis_size(axis))
    route = [(i - distance, i) for i in devices if i - distance in devices]
    return lax.ppermute(block, axis, route)


def modulate(hidden, shift_scale):
    average = jnp.mean(hidden, axis=-1, keepdims=True)
    centred = hidden - average
    variance = jnp.mean(centred * centred, axis=-1, keepdims=True)
    return (centred * lax.rsqrt(variance + 1e-06) * (1.0 + shift_scale[1]) + shift_scale[0]).astype(
        jnp.bfloat16
    )


def block_mask(row_first, col_first, total_rows, total_cols, key_count):
    query_edge = 8
    radius = WIN // 2
    key_side = query_edge + 2 * radius
    offsets = jnp.arange(query_edge)
    reaches = jnp.arange(key_side)
    row_starts = jnp.clip(row_first + offsets - radius, 0, total_rows - WIN)
    key_rows = row_first - radius + reaches
    row_inside = (key_rows[None, :] >= row_starts[:, None]) & (
        key_rows[None, :] < row_starts[:, None] + WIN
    )
    col_starts = jnp.clip(col_first + offsets - radius, 0, total_cols - WIN)
    key_cols = col_first - radius + reaches
    col_inside = (key_cols[None, :] >= col_starts[:, None]) & (
        key_cols[None, :] < col_starts[:, None] + WIN
    )
    joined = row_inside[:, None, :, None] & col_inside[None, :, None, :]
    joined = joined.reshape(query_edge * query_edge, key_side * key_side)
    filler = jnp.zeros((query_edge * query_edge, key_count - key_side * key_side), dtype=jnp.bool_)
    return jnp.concatenate([joined, filler], axis=1)


def edge_keys(key_values):
    radius = WIN // 2
    return padded(key_values, (("trow", 1), ("tcol", 2)), radius)


def attend_tile(queries, extended, row_anchor, col_anchor, total_rows, total_cols):
    images, tile_rows, tile_cols = (queries.shape[0], queries.shape[1], queries.shape[2])
    query_edge = 8
    radius = WIN // 2
    key_side = query_edge + 2 * radius
    key_count = (key_side * key_side + 127) // 128 * 128
    across = tile_cols // query_edge
    block_count = tile_rows // query_edge * across
    scaling = 1.0 / math.sqrt(HD)

    def one_block(position):
        row_block = position // across * query_edge
        col_block = position % across * query_edge
        query_block = queries
        query_block = query_block.reshape(images, query_edge * query_edge, HEADS, HD)
        key_block = extended
        key_block = key_block.reshape(images, key_side * key_side, 2 * HW)
        key_block = jnp.pad(key_block, ((0, 0), (0, key_count - key_side * key_side), (0, 0)))
        key_heads = key_block[..., :HW].reshape(images, key_count, HEADS, HD)
        value_heads = key_block[..., HW:].reshape(images, key_count, HEADS, HD)
        allowed = block_mask(
            row_anchor + row_block, col_anchor + col_block, total_rows, total_cols, key_count
        )
        scores = (
            jnp.einsum(
                "iqhd,ikhd->ihqk", query_block, key_heads, preferred_element_type=jnp.float32
            )
            * scaling
        )
        scores = jnp.where(allowed[None, None], scores, -1e30)
        highest = jnp.max(scores, axis=-1, keepdims=True)
        raised = jnp.exp(scores - highest)
        totals = jnp.sum(raised, axis=-1, keepdims=True)
        weights = (raised / totals).astype(jnp.bfloat16)
        blended = jnp.einsum(
            "ihqk,ikhd->iqhd", weights, value_heads, preferred_element_type=jnp.float32
        )
        return blended.astype(jnp.bfloat16).reshape(images, query_edge, query_edge, HW)

    result = lax.map(one_block, jnp.arange(block_count))
    result = result.reshape(tile_rows // query_edge, across, images, query_edge, query_edge, HW)
    return result.transpose(2, 0, 3, 1, 4, 5).reshape(images, tile_rows, tile_cols, HW)


def run_block(active, hidden, shift_scale, weight_q, weight_kv, weight_o):
    images, tile_rows, tile_cols = (hidden.shape[0], hidden.shape[1], hidden.shape[2])
    tokens = images * tile_rows * tile_cols

    def project():
        flattened = modulate(hidden, shift_scale).reshape(tokens, D)
        queries = jnp.dot(flattened, weight_q, preferred_element_type=jnp.float32).astype(
            jnp.bfloat16
        )
        key_values = jnp.dot(flattened, weight_kv, preferred_element_type=jnp.float32).astype(
            jnp.bfloat16
        )
        return (queries, key_values)

    def nothing():
        return (jnp.zeros((tokens, HW), jnp.bfloat16), jnp.zeros((tokens, 2 * HW), jnp.bfloat16))

    queries, key_values = lax.cond(active, project, nothing)
    extended = edge_keys(key_values.reshape(images, tile_rows, tile_cols, 2 * HW))
    row_anchor = lax.axis_index("trow") * tile_rows
    col_anchor = lax.axis_index("tcol") * tile_cols
    total_rows = tile_rows * lax.axis_size("trow")
    total_cols = tile_cols * lax.axis_size("tcol")

    def finish():
        attended = attend_tile(
            queries.reshape(images, tile_rows, tile_cols, HW),
            extended,
            row_anchor,
            col_anchor,
            total_rows,
            total_cols,
        )
        projected = jnp.dot(
            attended.reshape(tokens, HW), weight_o, preferred_element_type=jnp.float32
        )
        return (hidden + shift_scale[2] * projected.reshape(hidden.shape)).astype(jnp.bfloat16)

    def vacant():
        return jnp.zeros(hidden.shape, jnp.bfloat16)

    return lax.cond(active, finish, vacant)


def zero_project(control_out, weight_z):
    flattened = control_out.reshape(-1, D)
    return (
        jnp.dot(flattened, weight_z, preferred_element_type=jnp.float32)
        .astype(jnp.bfloat16)
        .reshape(control_out.shape)
    )


def on_device(latent, modulation, w_query, w_keyval, w_out, w_zero):
    sources = (w_query, w_keyval, w_out)
    weight_q, weight_kv, weight_o, weight_z = (
        lax.all_gather(sources[0], "tcol", axis=2, tiled=True),
        lax.all_gather(sources[1], "tcol", axis=2, tiled=True),
        lax.all_gather(sources[2], "tcol", axis=1, tiled=True),
        lax.all_gather(w_zero, "tcol", axis=1, tiled=True),
    )
    branch_index = lax.axis_index("branch")
    is_control = branch_index == 1
    own_copy = latent[0]
    shift_scale = lax.dynamic_index_in_dim(modulation, branch_index, 0, keepdims=False)
    received = shifted(own_copy, "branch", 1)
    control_in = own_copy.astype(jnp.float32) + received.astype(jnp.float32)
    control_out = run_block(
        is_control, control_in, shift_scale, weight_q[0], weight_kv[0], weight_o[0]
    )

    def with_projection():
        return zero_project(control_out, weight_z)

    def without_projection():
        return jnp.zeros(control_out.shape, jnp.bfloat16)

    residual = lax.cond(is_control, with_projection, without_projection)
    returned = shifted(residual, "branch", -1)
    base_in = own_copy.astype(jnp.float32) + returned.astype(jnp.float32)
    base_out = run_block(
        jnp.logical_not(is_control), base_in, shift_scale, weight_q[0], weight_kv[0], weight_o[0]
    )
    return jnp.where(is_control, control_out, base_out)[None]


def solution(mesh):
    placed = (
        P("branch", None, "trow", "tcol", None),
        P(),
        P("branch", None, "tcol"),
        P("branch", None, "tcol"),
        P("branch", "tcol", None),
        P(None, "tcol"),
    )
    return jax.shard_map(
        on_device,
        mesh=mesh,
        in_specs=placed,
        out_specs=P("branch", None, "trow", "tcol", None),
        check_vma=False,
    )
```

profile of v0, /device:TPU:1, one launch (start us, length us, event | category | flops | bytes accessed | tf_op | source)
XLA Modules:
  0.0 213.8 jit_solution(173536334885373562)
XLA Ops:
  9.3 4.0 %collective-permute-start = (bf16[2,8,8,1152]{3,2,1,0:T(8,128)(2,1)}, bf16[2,8,8,1152]{3,2,1,0:T(8,128)(2,1)S(1)}, u32[]{:S(2)}, u32[]{:S(2)}) collective-permute-start(bf16[2,8,8,1152]{3,2,1,0:T(8,128)(2,1)} %bitcast.92), channel_id=1, source_target_pairs={{0,16},{1,17},{2,18},{3,19},{4,20},{5,21},{6,22},{7,23},{8,24},{9,... | collective-permute-start | bytes 884744 | tf_op jit(solution)/shard_map/ppermute | solution.py:31
  13.4 5.9 %collective-permute-done = bf16[2,8,8,1152]{3,2,1,0:T(8,128)(2,1)S(1)} collective-permute-done((bf16[2,8,8,1152]{3,2,1,0:T(8,128)(2,1)}, bf16[2,8,8,1152]{3,2,1,0:T(8,128)(2,1)S(1)}, u32[]{:S(2)}, u32[]{:S(2)}) %collective-permute-start) | collective-permute-done | bytes 294944 | tf_op jit(solution)/shard_map/ppermute | solution.py:31
  20.3 14.8 %all-gather.5.cloned.1.call-done = bf16[1,1152,576]{1,2,0:T(8,128)(2,1)} async-done(((bf16[1,1152,72]{1,2,0:T(8,128)(2,1)}), bf16[1,1152,576]{1,2,0:T(8,128)(2,1)}) %all-gather.5.cloned.1.call-update) | async-done | bytes 1327120 | tf_op jit(solution)/shard_map/all_gather | solution.py:170
  35.1 35.3 %all-gather.7.cloned.1.call-done = bf16[1,1152,1152]{1,2,0:T(8,128)(2,1)} async-done(((bf16[1,1152,144]{1,2,0:T(8,128)(2,1)}), bf16[1,1152,1152]{1,2,0:T(8,128)(2,1)}) %all-gather.7.cloned.1.call-update) | async-done | bytes 2654224 | tf_op jit(solution)/shard_map/all_gather | solution.py:171
  73.5 4.0 %collective-permute-start.1 = (bf16[2,6,8,1152]{3,2,1,0:T(8,128)(2,1)S(1)}, bf16[2,6,8,1152]{3,2,1,0:T(8,128)(2,1)S(1)}, u32[]{:S(2)}, u32[]{:S(2)}) collective-permute-start(bf16[2,6,8,1152]{3,2,1,0:T(8,128)(2,1)S(1)} %get-tuple-element.208), channel_id=1, source_target_pairs={{0,8},{1,9},{2,10},{3,11},{4,12},{5,13},{6,14},{7,15},{16,24},{17,... | collective-permute-start | bytes 663560 | tf_op jit(solution)/shard_map/ppermute | solution.py:20
  77.5 3.3 %collective-permute-done.2 = bf16[2,6,8,1152]{3,2,1,0:T(8,128)(2,1)S(1)} collective-permute-done((bf16[2,6,8,1152]{3,2,1,0:T(8,128)(2,1)S(1)}, bf16[2,6,8,1152]{3,2,1,0:T(8,128)(2,1)S(1)}, u32[]{:S(2)}, u32[]{:S(2)}) %collective-permute-start.2) | collective-permute-done | bytes 221216 | tf_op jit(solution)/shard_map/ppermute | solution.py:23
  83.4 3.3 %collective-permute-start.4 = (bf16[2,20,6,1152]{3,0,2,1:T(2,128)(2,1)S(1)}, bf16[2,20,6,1152]{3,0,2,1:T(2,128)(2,1)S(1)}, u32[]{:S(2)}, u32[]{:S(2)}) collective-permute-start(bf16[2,20,6,1152]{3,0,2,1:T(2,128)(2,1)S(1)} %copy.40), channel_id=1, source_target_pairs={{1,0},{2,1},{3,2},{4,3},{5,4},{6,5},{7,6},{9,8},{10,9},{11,10},{12... | collective-permute-start | bytes 1658888 | tf_op jit(solution)/shard_map/ppermute | solution.py:23
  87.2 2.3 %collective-permute-start.3 = (bf16[2,20,6,1152]{3,0,2,1:T(2,128)(2,1)S(1)}, bf16[2,20,6,1152]{3,0,2,1:T(2,128)(2,1)S(1)}, u32[]{:S(2)}, u32[]{:S(2)}) collective-permute-start(bf16[2,20,6,1152]{3,0,2,1:T(2,128)(2,1)S(1)} %copy.39), channel_id=1, source_target_pairs={{0,1},{1,2},{2,3},{3,4},{4,5},{5,6},{6,7},{8,9},{9,10},{10,11},{11... | collective-permute-start | bytes 1658888 | tf_op jit(solution)/shard_map/ppermute | solution.py:20
  89.5 8.7 %collective-permute-done.4 = bf16[2,20,6,1152]{3,0,2,1:T(2,128)(2,1)S(1)} collective-permute-done((bf16[2,20,6,1152]{3,0,2,1:T(2,128)(2,1)S(1)}, bf16[2,20,6,1152]{3,0,2,1:T(2,128)(2,1)S(1)}, u32[]{:S(2)}, u32[]{:S(2)}) %collective-permute-start.4) | collective-permute-done | bytes 552992 | tf_op jit(solution)/shard_map/ppermute | solution.py:23
  98.5 2.0 pad_maximum_fusion
  100.5 29.9 %all-gather.11.cloned.1.call-done = bf16[1152,1152]{0,1:T(8,128)(2,1)} async-done(((bf16[1152,144]{0,1:T(8,128)(2,1)}), bf16[1152,1152]{0,1:T(8,128)(2,1)}) %all-gather.11.cloned.1.call-update) | async-done | bytes 2654224 | tf_op jit(solution)/shard_map/all_gather | solution.py:173
  130.4 1.4 collective-permute-start.5
  131.9 11.2 %collective-permute-done.5 = bf16[2,8,8,1152]{3,2,1,0:T(8,128)(2,1)} collective-permute-done((bf16[2,8,8,1152]{3,2,1,0:T(8,128)(2,1)S(1)}, bf16[2,8,8,1152]{3,2,1,0:T(8,128)(2,1)}, u32[]{:S(2)}, u32[]{:S(2)}) %collective-permute-start.5) | collective-permute-done | bytes 294944 | tf_op jit(solution)/shard_map/ppermute | solution.py:31
  144.2 4.2 %conditional.8 = (bf16[128,576]{0,1:T(8,128)(2,1)S(1)}, bf16[128,1152]{1,0:T(8,128)(2,1)}) conditional(s32[]{:T(128)} %convert_element_type.76, () %tuple.48, (f32[2,8,8,1152]{3,2,1,0:T(8,128)S(1)}, f32[3,1152]{1,0:T(4,128)S(1)}, bf16[1152,576]{0,1:T(8,128)(2,1)}, bf16[1152,1152]{0,1:T(8,128)(2,1)S(1)}) %tuple.104), branch_computations={%region_10.11_spmd, %region_11.14_spmd} | conditional | flops 511157504 | bytes 7110164 | solution.py:131
  145.0 1.8 convolution_convert_fusion.5
  146.8 1.6 convolution_convert_fusion.4
  150.9 4.0 %collective-permute-start.6 = (bf16[2,6,8,1152]{3,2,1,0:T(8,128)(2,1)S(1)}, bf16[2,6,8,1152]{3,2,1,0:T(8,128)(2,1)S(1)}, u32[]{:S(2)}, u32[]{:S(2)}) collective-permute-start(bf16[2,6,8,1152]{3,2,1,0:T(8,128)(2,1)S(1)} %get-tuple-element.206), channel_id=1, source_target_pairs={{0,8},{1,9},{2,10},{3,11},{4,12},{5,13},{6,14},{7,15},{16,24},{17,... | collective-permute-start | bytes 663560 | tf_op jit(solution)/shard_map/ppermute | solution.py:20
  154.9 2.8 %collective-permute-done.7 = bf16[2,6,8,1152]{3,2,1,0:T(8,128)(2,1)S(1)} collective-permute-done((bf16[2,6,8,1152]{3,2,1,0:T(8,128)(2,1)S(1)}, bf16[2,6,8,1152]{3,2,1,0:T(8,128)(2,1)S(1)}, u32[]{:S(2)}, u32[]{:S(2)}) %collective-permute-start.7) | collective-permute-done | bytes 221216 | tf_op jit(solution)/shard_map/ppermute | solution.py:23
  160.2 3.9 %collective-permute-start.9 = (bf16[2,20,6,1152]{3,0,2,1:T(2,128)(2,1)S(1)}, bf16[2,20,6,1152]{3,0,2,1:T(2,128)(2,1)S(1)}, u32[]{:S(2)}, u32[]{:S(2)}) collective-permute-start(bf16[2,20,6,1152]{3,0,2,1:T(2,128)(2,1)S(1)} %copy.49), channel_id=1, source_target_pairs={{1,0},{2,1},{3,2},{4,3},{5,4},{6,5},{7,6},{9,8},{10,9},{11,10},{12... | collective-permute-start | bytes 1658888 | tf_op jit(solution)/shard_map/ppermute | solution.py:23
  164.6 2.3 %collective-permute-start.8 = (bf16[2,20,6,1152]{3,0,2,1:T(2,128)(2,1)S(1)}, bf16[2,20,6,1152]{3,0,2,1:T(2,128)(2,1)S(1)}, u32[]{:S(2)}, u32[]{:S(2)}) collective-permute-start(bf16[2,20,6,1152]{3,0,2,1:T(2,128)(2,1)S(1)} %copy.48), channel_id=1, source_target_pairs={{0,1},{1,2},{2,3},{3,4},{4,5},{5,6},{6,7},{8,9},{9,10},{10,11},{11... | collective-permute-start | bytes 1658888 | tf_op jit(solution)/shard_map/ppermute | solution.py:20
  166.9 4.8 %collective-permute-done.9 = bf16[2,20,6,1152]{3,0,2,1:T(2,128)(2,1)S(1)} collective-permute-done((bf16[2,20,6,1152]{3,0,2,1:T(2,128)(2,1)S(1)}, bf16[2,20,6,1152]{3,0,2,1:T(2,128)(2,1)S(1)}, u32[]{:S(2)}, u32[]{:S(2)}) %collective-permute-start.9) | collective-permute-done | bytes 552992 | tf_op jit(solution)/shard_map/ppermute | solution.py:23
  171.8 1.5 collective-permute-done.8
  173.4 2.1 pad_maximum_fusion.1
  175.5 30.0 %conditional.9 = (bf16[2,8,8,1152]{3,2,1,0:T(8,128)(2,1)}) conditional(s32[]{:T(128)} %convert_element_type.76, () %tuple.47, (f32[3,1152]{1,0:T(4,128)}, bf16[2,20,20,1152]{3,2,1,0:T(8,128)(2,1)S(1)}, s32[]{:T(128)}, s32[]{:T(128)}, bf16[128,576]{0,1:T(8,128)(2,1)}, /*index=5*/bf16[576,1152]{1,0:T(8,128)(2,1)S(1)}, ...), branch_computations={%region_14.15_spmd, %region_15.18_spmd} | conditional | flops 324553312 | bytes 27609876 | solution.py:155
  177.0 5.6 %pad_slice_fusion.2 = (bf16[2,512,576]{2,0,1:T(2,128)(2,1)S(1)}, bf16[2,512,576]{2,0,1:T(2,128)(2,1)}) fusion(bf16[2,400,1152]{2,0,1:T(2,128)(2,1)S(1)} %bitcast.78), kind=kLoop, calls=%fused_computation.55 | loop fusion | bytes 4202496 | tf_op jit(solution)/shard_map/cond/branch_1_fun/while/body/eval_jaxpr/slice | solution.py:88
  182.6 4.2 %copy.33 = bf16[2,512,576]{1,2,0:T(8,128)(2,1)} copy(bf16[2,512,576]{2,0,1:T(2,128)(2,1)} %get-tuple-element.195) | data formatting | bytes 2359296 | tf_op jit(solution)/shard_map/cond/branch_1_fun/while/body/eval_jaxpr/slice | solution.py:89
  189.4 1.8 and.96
  192.6 3.1 %copy.34 = bf16[2,512,576]{1,2,0:T(8,128)(2,1)} copy(bf16[2,512,576]{2,0,1:T(2,128)(2,1)S(1)} %get-tuple-element.194) | data formatting | bytes 2359296 | tf_op jit(solution)/shard_map/cond/branch_1_fun/while/body/eval_jaxpr/slice | solution.py:88
  195.7 1.8 reshape.397
  197.5 3.6 %fusion.41 = (f32[2,8,64]{2,1,0:T(8,128)S(1)}, f32[2,8,64,512]{3,2,1,0:T(8,128)}) fusion(pred[64,512]{1,0:T(8,128)(4,1)} %concatenate.15, bf16[2,512,8,72]{1,3,2,0:T(8,128)(2,1)} %bitcast.91, bf16[2,64,8,72]{1,0,3,2:T(2,128)(2,1)} %reshape.397), kind=kOutput, calls=%fused_computation.87 | convolution fusion | flops 77595136 | bytes 3461120 | tf_op jit(solution)/shard_map/cond/branch_1_fun/while/body/eval_jaxpr/sub | solution.py:101
  201.1 2.2 %fusion.24 = bf16[2,64,8,72]{3,1,2,0:T(8,128)(2,1)S(1)} fusion(bf16[2,512,8,72]{1,3,2,0:T(8,128)(2,1)S(1)} %bitcast.89, f32[2,8,64,512]{3,2,1,0:T(8,128)} %get-tuple-element.197, f32[2,8,64]{2,1,0:T(8,128)S(1)} %get-tuple-element.196), kind=kOutput, calls=%fused_computation.59 | convolution fusion | flops 76619776 | bytes 3428352 | tf_op jit(solution)/shard_map/cond/branch_1_fun/while/body/eval_jaxpr/ihqk,ikhd->iqhd/dot_general | solution.py:104
  205.5 1.7 select_bitcast_fusion
  (74 shorter events, 25.9 us)
Async XLA Ops:
  6.5 6.8 %copy-start = (f32[2,3,1152]{2,0,1:T(2,128)S(1)}, f32[2,3,1152]{2,0,1:T(2,128)}, u32[]{:S(2)}) copy-start(f32[2,3,1152]{2,0,1:T(2,128)} %param.17) | copy-start | bytes 82948
  6.5 28.5 %all-gather.5.cloned.1.call-start = ((), (), s32[]{:S(2)}) async-start(), calls=%async_computation | async-start | bytes 1492992 | tf_op jit(solution)/shard_map/all_gather | solution.py:170
  7.3 63.1 %all-gather.7.cloned.1.call-start = ((), (), s32[]{:S(2)}) async-start(), calls=%async_computation.1 | async-start | bytes 2985984 | tf_op jit(solution)/shard_map/all_gather | solution.py:171
  8.0 92.5 %all-gather.9.cloned.1.call-start = ((), (), s32[]{:S(2)}) async-start(), calls=%async_computation.2 | async-start | bytes 1492992 | tf_op jit(solution)/shard_map/all_gather | solution.py:172
  8.7 121.7 %all-gather.11.cloned.1.call-start = ((), (), s32[]{:S(2)}) async-start(), calls=%async_computation.3 | async-start | bytes 2985984 | tf_op jit(solution)/shard_map/all_gather | solution.py:173
  9.3 10.0 %collective-permute-start = (bf16[2,8,8,1152]{3,2,1,0:T(8,128)(2,1)}, bf16[2,8,8,1152]{3,2,1,0:T(8,128)(2,1)S(1)}, u32[]{:S(2)}, u32[]{:S(2)}) collective-permute-start(bf16[2,8,8,1152]{3,2,1,0:T(8,128)(2,1)} %bitcast.92), channel_id=1, source_target_pairs={{0,16},{1,17},{2,18},{3,19},{4,20},{5,21},{6,22},{7,23},{8,24},{9,... | collective-permute-start | bytes 884744 | tf_op jit(solution)/shard_map/ppermute | solution.py:31
  13.4 130.8 %copy-start.10 = (f32[1,3,1152]{2,1,0:T(4,128)}, f32[1,3,1152]{2,1,0:T(4,128)S(1)}, u32[]{:S(2)}) copy-start(f32[1,3,1152]{2,1,0:T(4,128)S(1)} %copy.87) | copy-start | bytes 41476
  72.2 8.6 %collective-permute-start.2 = (bf16[2,6,8,1152]{3,2,1,0:T(8,128)(2,1)S(1)}, bf16[2,6,8,1152]{3,2,1,0:T(8,128)(2,1)S(1)}, u32[]{:S(2)}, u32[]{:S(2)}) collective-permute-start(bf16[2,6,8,1152]{3,2,1,0:T(8,128)(2,1)S(1)} %get-tuple-element.209), channel_id=1, source_target_pairs={{8,0},{9,1},{10,2},{11,3},{12,4},{13,5},{14,6},{15,7},{24,16},{25,... | collective-permute-start | bytes 663560 | tf_op jit(solution)/shard_map/ppermute | solution.py:23
  73.5 8.2 %collective-permute-start.1 = (bf16[2,6,8,1152]{3,2,1,0:T(8,128)(2,1)S(1)}, bf16[2,6,8,1152]{3,2,1,0:T(8,128)(2,1)S(1)}, u32[]{:S(2)}, u32[]{:S(2)}) collective-permute-start(bf16[2,6,8,1152]{3,2,1,0:T(8,128)(2,1)S(1)} %get-tuple-element.208), channel_id=1, source_target_pairs={{0,8},{1,9},{2,10},{3,11},{4,12},{5,13},{6,14},{7,15},{16,24},{17,... | collective-permute-start | bytes 663560 | tf_op jit(solution)/shard_map/ppermute | solution.py:20
  83.4 14.8 %collective-permute-start.4 = (bf16[2,20,6,1152]{3,0,2,1:T(2,128)(2,1)S(1)}, bf16[2,20,6,1152]{3,0,2,1:T(2,128)(2,1)S(1)}, u32[]{:S(2)}, u32[]{:S(2)}) collective-permute-start(bf16[2,20,6,1152]{3,0,2,1:T(2,128)(2,1)S(1)} %copy.40), channel_id=1, source_target_pairs={{1,0},{2,1},{3,2},{4,3},{5,4},{6,5},{7,6},{9,8},{10,9},{11,10},{12... | collective-permute-start | bytes 1658888 | tf_op jit(solution)/shard_map/ppermute | solution.py:23
  87.2 11.2 %collective-permute-start.3 = (bf16[2,20,6,1152]{3,0,2,1:T(2,128)(2,1)S(1)}, bf16[2,20,6,1152]{3,0,2,1:T(2,128)(2,1)S(1)}, u32[]{:S(2)}, u32[]{:S(2)}) collective-permute-start(bf16[2,20,6,1152]{3,0,2,1:T(2,128)(2,1)S(1)} %copy.39), channel_id=1, source_target_pairs={{0,1},{1,2},{2,3},{3,4},{4,5},{5,6},{6,7},{8,9},{9,10},{10,11},{11... | collective-permute-start | bytes 1658888 | tf_op jit(solution)/shard_map/ppermute | solution.py:20
  100.5 29.9 %copy-start.5 = (bf16[2,8,8,1152]{3,2,1,0:T(8,128)(2,1)}, bf16[2,8,8,1152]{3,2,1,0:T(8,128)(2,1)S(1)}, u32[]{:S(2)}) copy-start(bf16[2,8,8,1152]{3,2,1,0:T(8,128)(2,1)S(1)} %get-tuple-element.218) | copy-start | bytes 884740
  130.4 13.8 %copy-start.1 = (bf16[1,1152,1152]{1,2,0:T(8,128)(2,1)S(1)}, bf16[1,1152,1152]{1,2,0:T(8,128)(2,1)}, u32[]{:S(2)}) copy-start(bf16[1,1152,1152]{1,2,0:T(8,128)(2,1)} %all-gather.7.cloned.1.call-done) | copy-start | bytes 7962628
  130.4 12.6 %collective-permute-start.5 = (bf16[2,8,8,1152]{3,2,1,0:T(8,128)(2,1)S(1)}, bf16[2,8,8,1152]{3,2,1,0:T(8,128)(2,1)}, u32[]{:S(2)}, u32[]{:S(2)}) collective-permute-start(bf16[2,8,8,1152]{3,2,1,0:T(8,128)(2,1)S(1)} %get-tuple-element.219), channel_id=1, source_target_pairs={{16,0},{17,1},{18,2},{19,3},{20,4},{21,5},{22,6},{23,7},{24,8},{25... | collective-permute-start | bytes 884744 | tf_op jit(solution)/shard_map/ppermute | solution.py:31
  148.4 11.4 %copy-start.9 = (bf16[128,576]{0,1:T(8,128)(2,1)}, bf16[128,576]{0,1:T(8,128)(2,1)S(1)}, u32[]{:S(2)}) copy-start(bf16[128,576]{0,1:T(8,128)(2,1)S(1)} %get-tuple-element.129) | copy-start | bytes 442372
  149.6 8.1 %collective-permute-start.7 = (bf16[2,6,8,1152]{3,2,1,0:T(8,128)(2,1)S(1)}, bf16[2,6,8,1152]{3,2,1,0:T(8,128)(2,1)S(1)}, u32[]{:S(2)}, u32[]{:S(2)}) collective-permute-start(bf16[2,6,8,1152]{3,2,1,0:T(8,128)(2,1)S(1)} %get-tuple-element.207), channel_id=1, source_target_pairs={{8,0},{9,1},{10,2},{11,3},{12,4},{13,5},{14,6},{15,7},{24,16},{25,... | collective-permute-start | bytes 663560 | tf_op jit(solution)/shard_map/ppermute | solution.py:23
  150.9 7.6 %collective-permute-start.6 = (bf16[2,6,8,1152]{3,2,1,0:T(8,128)(2,1)S(1)}, bf16[2,6,8,1152]{3,2,1,0:T(8,128)(2,1)S(1)}, u32[]{:S(2)}, u32[]{:S(2)}) collective-permute-start(bf16[2,6,8,1152]{3,2,1,0:T(8,128)(2,1)S(1)} %get-tuple-element.206), channel_id=1, source_target_pairs={{0,8},{1,9},{2,10},{3,11},{4,12},{5,13},{6,14},{7,15},{16,24},{17,... | collective-permute-start | bytes 663560 | tf_op jit(solution)/shard_map/ppermute | solution.py:20
  160.2 11.5 %collective-permute-start.9 = (bf16[2,20,6,1152]{3,0,2,1:T(2,128)(2,1)S(1)}, bf16[2,20,6,1152]{3,0,2,1:T(2,128)(2,1)S(1)}, u32[]{:S(2)}, u32[]{:S(2)}) collective-permute-start(bf16[2,20,6,1152]{3,0,2,1:T(2,128)(2,1)S(1)} %copy.49), channel_id=1, source_target_pairs={{1,0},{2,1},{3,2},{4,3},{5,4},{6,5},{7,6},{9,8},{10,9},{11,10},{12... | collective-permute-start | bytes 1658888 | tf_op jit(solution)/shard_map/ppermute | solution.py:23
  164.6 8.7 %collective-permute-start.8 = (bf16[2,20,6,1152]{3,0,2,1:T(2,128)(2,1)S(1)}, bf16[2,20,6,1152]{3,0,2,1:T(2,128)(2,1)S(1)}, u32[]{:S(2)}, u32[]{:S(2)}) collective-permute-start(bf16[2,20,6,1152]{3,0,2,1:T(2,128)(2,1)S(1)} %copy.48), channel_id=1, source_target_pairs={{0,1},{1,2},{2,3},{3,4},{4,5},{5,6},{6,7},{8,9},{9,10},{10,11},{11... | collective-permute-start | bytes 1658888 | tf_op jit(solution)/shard_map/ppermute | solution.py:20
  173.4 2.1 copy-start.3
  175.5 30.0 %copy-start.6 = (bf16[2,8,8,1152]{3,2,1,0:T(8,128)(2,1)S(1)}, bf16[2,8,8,1152]{3,2,1,0:T(8,128)(2,1)}, u32[]{:S(2)}) copy-start(bf16[2,8,8,1152]{3,2,1,0:T(8,128)(2,1)} %copy-done.5) | copy-start | bytes 884740
  197.5 3.6 %copy-start.8 = (bf16[2,512,576]{1,2,0:T(8,128)(2,1)S(1)}, bf16[2,512,576]{1,2,0:T(8,128)(2,1)}, u32[]{:S(2)}) copy-start(bf16[2,512,576]{1,2,0:T(8,128)(2,1)} %copy.33) | copy-start | bytes 3538948 | tf_op jit(solution)/shard_map/cond
Sparse Core Ops, SparseCore 0:
  9.0 26.0 all-gather.4
  36.7 33.5 all-gather.6
  72.0 23.3 all-gather.8
  96.9 33.4 all-gather.10
where the time goes:
time: 215 us; the launch traced here: 214 us
  waiting for transfers between devices  123 us (57%)
  starting transfers between devices  28 us (13%)
  local copies, waits for them, and re-layouts  26 us (12%)
  between operations  13.4 us (6%)
  other arithmetic  13.2 us (6%)
  matrix products  10.3 us (5%)
    all_gather x1, waiting for transfers between devices, on_device(): lax.all_gather(sources[1], 'tcol', axis=2, tiled=True)  35.3 us
    all_gather x1, waiting for transfers between devices, on_device(): lax.all_gather(w_zero, 'tcol', axis=1, tiled=True)  29.9 us
    ppermute x4, waiting for transfers between devices, padded(): lax.ppermute(lax.slice_in_dim(block, 0, width, axis=dim), axis, backward)  19.6 us
    ppermute x2, waiting for transfers between devices, shifted(): return lax.ppermute(block, axis, route)  17.1 us
    all_gather x1, waiting for transfers between devices, on_device(): lax.all_gather(sources[0], 'tcol', axis=2, tiled=True)  14.8 us
    ppermute x4, starting transfers between devices, padded(): lax.ppermute(lax.slice_in_dim(block, block.shape[dim] - width, None, axis...  12.7 us
    ppermute x4, starting transfers between devices, padded(): lax.ppermute(lax.slice_in_dim(block, 0, width, axis=dim), axis, backward)  9.79 us
    slice x2, local copies, waits for them, and re-layouts, one_block(): key_heads = key_block[..., :HW].reshape(images, key_count, HEADS, HD)  8.73 us
  transfers between devices with their start and end apart: 14, of which 12 were waited for; matrix products, arithmetic and copies ran while one was open for 4% of the time, Pallas kernels for 0%

commit v1 on v0

--- a/solution.py
+++ b/solution.py
@@ -1,8 +1,11 @@
+import functools
 import math
 
 import jax
 import jax.numpy as jnp
 from jax import lax
+from jax.experimental import pallas as pl
+from jax.experimental.pallas import tpu as pltpu
 from jax.sharding import PartitionSpec as P
 
 D = 1152
@@ -197,6 +200,480 @@
     return jnp.where(is_control, control_out, base_out)[None]
 
 
+AXES = ("branch", "trow", "tcol")
+SLOT = 80
+ORDER = (0, 3, 1, 2)
+
+
+def routes(sizes, move):
+    found = []
+    for b in range(sizes[0]):
+        for r in range(sizes[1]):
+            for t in range(sizes[2]):
+                target = move(b, r, t)
+                if target is not None:
+                    found.append((place_of(sizes, b, r, t), place_of(sizes, *target)))
+    return found
+
+
+def place_of(sizes, b, r, t):
+    return (b * sizes[1] + r) * sizes[2] + t
+
+
+def send(block, sizes, move):
+    return lax.ppermute(block, AXES, routes(sizes, move))
+
+
+def after(block, *earlier):
+    return lax.optimization_barrier((block,) + earlier)[0]
+
+
+def kernel_call(body, outs, args, scratch=(), copies=0, stay=False, micros=0):
+    def space(a):
+        if a.dtype == jnp.int32:
+            return pltpu.SMEM
+        return pltpu.VMEM if a.dtype == jnp.float32 else pl.ANY
+
+    buffers = [pltpu.VMEM(shape, kind) for shape, kind in scratch]
+    return pl.pallas_call(
+        body,
+        out_shape=[jax.ShapeDtypeStruct(shape, kind) for shape, kind in outs],
+        in_specs=[pl.BlockSpec(memory_space=space(a)) for a in args],
+        out_specs=[pl.BlockSpec(memory_space=pl.ANY if stay else pltpu.VMEM) for _ in outs],
+        scratch_shapes=buffers + [pltpu.SemaphoreType.DMA((copies,))],
+        compiler_params=pltpu.CompilerParams(vmem_limit_bytes=32 * 1024 * 1024),
+        cost_estimate=pl.CostEstimate(
+            flops=0, bytes_accessed=1 + 3_700_000 * micros, transcendentals=0
+        ),
+    )(*args)
+
+
+def begin(copies, done, first=0):
+    started = []
+    for n, (source, target) in enumerate(copies):
+        copy = pltpu.make_async_copy(source, target, done.at[first + n])
+        copy.start()
+        started.append(copy)
+    return started
+
+
+def finish(started):
+    for copy in started:
+        copy.wait()
+
+
+def dot_rows(left, right):
+    return lax.dot_general(left, right, (((1,), (1,)), ((), ())), preferred_element_type=jnp.float32)
+
+
+def rows_at(start, count):
+    return pl.ds(pl.multiple_of(start, 16), count)
+
+
+def stack_kernel(*refs):
+    *pieces, stacked, done = refs
+    finish(begin([(piece, stacked.at[n]) for n, piece in enumerate(pieces)], done))
+
+
+def norm_kernel(total_rows, total_cols, spot, own, far, mod, normed, bias, total, first, second, done):
+    copies = [(own, first), (far, second)]
+    started = begin(copies, done)
+    radius = WIN // 2
+    query = lax.broadcasted_iota(jnp.int32, bias.shape, 0)
+    key = lax.broadcasted_iota(jnp.int32, bias.shape, 1)
+    base = spot[4]
+    row_start = jnp.clip((query >> 3) - radius, 0, total_rows - WIN)
+    col_start = jnp.clip(base + (query & 7) - radius, 0, total_cols - WIN)
+    key_row = (key & 127) >> 3
+    outward = 2 * spot[3] - 1
+    key_col = base + (1 - (key >> 7)) * outward * 8 + (key & 7)
+    inside = (
+        (key_row >= row_start)
+        & (key_row < row_start + WIN)
+        & (key_col >= col_start)
+        & (key_col < col_start + WIN)
+    )
+    bias[...] = jnp.where(inside, 0.0, -1e30)
+    finish(started)
+    for image in range(own.shape[0]):
+        hidden = first[image].astype(jnp.float32) + second[image].astype(jnp.float32)
+        total[image] = hidden
+        normed[image] = modulate(hidden, mod)
+
+
+def in_order(origin):
+    return (origin % 2) * 2 + origin // 2
+
+
+def arrange_keyvals(link, stacks, weight):
+    for at in range(2):
+        for step in range(4):
+            origin = link ^ ORDER[step]
+            slot = (1 - origin // 2) * 4 + at * 2 + origin % 2
+            weight[rows_at(slot * SLOT, SLOT), :] = stacks[at, step, :SLOT]
+
+
+def arrange_heads(link, stack, first_row, weight):
+    for step in range(4):
+        start = first_row + in_order(link ^ ORDER[step]) * SLOT
+        weight[rows_at(start, SLOT), :] = stack[step]
+
+
+def arrange_queries(link, stacks, row, weight):
+    start = weight.shape[0] - 4 * SLOT
+    weight[8 * SLOT : start, :] = jnp.zeros((start - 8 * SLOT, weight.shape[1]), weight.dtype)
+    arrange_heads(link, stacks.at[row, :, SLOT:], start, weight)
+
+
+def project_kernel(spot, normed, normed_other, mine, other, keyval, query, stacks, weight, both, done):
+    row, link, core = (spot[1], spot[2], spot[3])
+    copies = [(mine, stacks.at[core]), (other, stacks.at[1 - core])]
+    for image in range(normed.shape[0]):
+        copies.append((normed.at[image], both.at[image, row]))
+        copies.append((normed_other.at[image], both.at[image, 1 - row]))
+    finish(begin(copies, done))
+    arrange_keyvals(link, stacks, weight)
+    arrange_queries(link, stacks, row, weight)
+    tokens = both[...].reshape(-1, both.shape[3])
+    projected = dot_rows(tokens, weight[...]).astype(keyval.dtype)
+    keyval[...] = projected[:, : keyval.shape[1]]
+    query[...] = projected[:, keyval.shape[1] :]
+
+
+def attend_kernel(spot, queries, outer, here, inner, bias, out, query_rows, keyvals, done):
+    scaling = 1.0 / math.sqrt(HD)
+    tokens = bias.shape[0]
+    images = out.shape[0] // tokens
+    copies = [(queries, query_rows)]
+    copies += [(part, keyvals.at[index]) for index, part in enumerate((outer, here, inner))]
+    finish(begin(copies, done))
+    key_lanes = queries.shape[1]
+    first_key = here.shape[1] - key_lanes
+    heads = out.shape[1] // SLOT
+    pad = key_lanes - heads * SLOT
+    value_lanes = (out.shape[1] + 127) // 128 * 128
+    query_lane = lax.broadcasted_iota(jnp.int32, (tokens, key_lanes), 1) - pad
+    value_lane = lax.broadcasted_iota(jnp.int32, (tokens, value_lanes), 1)
+
+    def within(lane, head):
+        return (lane >= head * SLOT) & (lane < (head + 1) * SLOT)
+
+    for image in range(images):
+        rows = slice(image * tokens, (image + 1) * tokens)
+        keys = jnp.concatenate([keyvals[n, rows, first_key:] for n in range(3)], axis=0)
+        values = jnp.concatenate([keyvals[n, rows, :value_lanes] for n in range(3)], axis=0)
+        query = query_rows[rows, :].astype(jnp.float32)
+        split = [jnp.where(within(query_lane, head), query, 0.0) for head in range(heads)]
+        scores = dot_rows(jnp.concatenate(split, axis=0).astype(jnp.bfloat16), keys)
+        raised, sums = ([], [])
+        for head in range(heads):
+            part = scores[head * tokens : (head + 1) * tokens] * scaling + bias[...]
+            part = jnp.exp(part - jnp.max(part, axis=-1, keepdims=True))
+            sums.append(jnp.sum(part, axis=-1, keepdims=True))
+            raised.append(part.astype(jnp.bfloat16))
+        blended = jnp.dot(
+            jnp.concatenate(raised, axis=0), values, preferred_element_type=jnp.float32
+        )
+        total = jnp.zeros((tokens, value_lanes), jnp.float32)
+        for head in range(heads):
+            part = blended[head * tokens : (head + 1) * tokens] / sums[head]
+            total = jnp.where(within(value_lane, head), part, total)
+        out[rows, :] = total[:, : out.shape[1]].astype(out.dtype)
+
+
+def prepare_kernel(
+    spot, first, first_other, zero_side, zero_corner, second, second_other, w_zero, weight,
+    stacks, zeros, keyval_stacks, done,
+):
+    row, link, core = (spot[1], spot[2], spot[3])
+    copies = [(first, stacks.at[core]), (first_other, stacks.at[1 - core])]
+    copies += [(zero_side, zeros.at[core]), (zero_corner, zeros.at[1 - core])]
+    copies += [(second, keyval_stacks.at[core]), (second_other, keyval_stacks.at[1 - core])]
+    started = begin(copies, done)
+    finish(started)
+    shard = w_zero.shape[0] // 8
+    for at in range(2):
+        for step in range(4):
+            start = (2 * (link ^ ORDER[step]) + at) * shard
+            mine = start + row * (shard - SLOT)
+            w_zero[rows_at(mine, SLOT), :] = stacks[at, step, :SLOT]
+            other = start + (1 - row) * (shard - SLOT)
+            w_zero[rows_at(other, SLOT), :] = zeros[at, step]
+    arrange_keyvals(link, keyval_stacks, weight)
+    arrange_queries(link, stacks, row, weight)
+
+
+def middle_kernel(
+    spot, own, far, side, corner, near, cross, out_mine, out_other, zero_rows, projections,
+    mod, mod_base, base_in, keyval, query,
+    base_rows, more_rows, heads, outs, w_out, w_zero, weight, both, done,
+):
+    row, link, core = (spot[1], spot[2], spot[3])
+    images, tokens, _ = own.shape
+    tile = images * tokens
+    width = heads.shape[2]
+    copies = []
+    for image in range(images):
+        for part, slot in ((0, row), (1, 1 - row)):
+            rows = slice(part * tile + image * tokens, part * tile + (image + 1) * tokens)
+            for index, ref in enumerate((near, cross)):
+                copies.append((ref.at[image, slot], heads.at[index, rows]))
+    copies += [(out_mine, outs.at[core]), (out_other, outs.at[1 - core])]
+    copies += [(own, base_rows.at[0]), (side, base_rows.at[1])]
+    copies += [(far, more_rows.at[0]), (corner, more_rows.at[1])]
+    early = begin(copies, done)
+    late = begin([(zero_rows, w_zero), (projections, weight)], done, len(early))
+    finish(early)
+    for at in range(2):
+        arrange_heads(link, outs.at[at], at * width, w_out)
+    projected = jnp.dot(
+        heads[0], w_out[rows_at(row * width, width), :], preferred_element_type=jnp.float32
+    )
+    projected += jnp.dot(
+        heads[1], w_out[rows_at((1 - row) * width, width), :], preferred_element_type=jnp.float32
+    )
+
+    def flat(ref):
+        return ref[...].reshape(2 * tile, ref.shape[3]).astype(jnp.float32)
+
+    base = flat(base_rows)
+    out = (base + flat(more_rows) + mod[2] * projected).astype(jnp.bfloat16)
+    finish(late)
+    residual = dot_rows(out, w_zero[...]).astype(jnp.bfloat16)
+    base = base + residual.astype(jnp.float32)
+    result = modulate(base, mod_base)
+    for image in range(images):
+        rows = slice(image * tokens, (image + 1) * tokens)
+        base_in[image] = base[rows]
+        both[image, row] = result[rows]
+        both[image, 1 - row] = result[tile + image * tokens : tile + (image + 1) * tokens]
+    rows = both[...].reshape(2 * tile, both.shape[3])
+    projected = dot_rows(rows, weight[...]).astype(keyval.dtype)
+    keyval[...] = projected[:, : keyval.shape[1]]
+    query[...] = projected[:, keyval.shape[1] :]
+
+
+def final_kernel(spot, attended, side, mine, other, base, mod, out, near, far, outs, w_out, done):
+    row, link = (spot[1], spot[2])
+    images = out.shape[0]
+    width = near.shape[2]
+    copies = [(side, far)]
+    copies += [(attended.at[image, row], near.at[image]) for image in range(images)]
+    copies += [(mine, outs.at[1 - row]), (other, outs.at[row])]
+    finish(begin(copies, done))
+    for at in range(2):
+        arrange_heads(link, outs.at[at], at * width, w_out)
+
+    def flat(ref):
+        return jnp.concatenate([ref[i] for i in range(images)], axis=0)
+
+    projected = jnp.dot(
+        flat(near), w_out[rows_at(row * width, width), :], preferred_element_type=jnp.float32
+    )
+    projected += jnp.dot(
+        flat(far), w_out[rows_at((1 - row) * width, width), :], preferred_element_type=jnp.float32
+    )
+    tokens = out.shape[1]
+    for image in range(images):
+        rows = slice(image * tokens, (image + 1) * tokens)
+        out[image] = (base[image] + mod[2] * projected[rows]).astype(out.dtype)
+
+
+def paired_rows(sizes, latent, modulation, w_query, w_keyval, w_out, w_zero):
+    branch = lax.axis_index("branch")
+    row = lax.axis_index("trow")
+    column = lax.axis_index("tcol")
+    core = column % 2
+    is_control = branch == 1
+    is_query = core == row
+    _, images, tile_rows, tile_cols, _ = latent.shape
+    tile = tile_rows * tile_cols
+    tokens = images * 2 * tile
+    half = HEADS // 2 * SLOT
+    lanes = half + half % 128
+    spot = jnp.stack([branch, row, column // 2, core, column * tile_cols]).astype(jnp.int32)
+    own = latent.reshape(images, tile, D)
+
+    def everyone(b, r, t):
+        return True
+
+    def base_only(b, r, t):
+        return b == 0
+
+    def control_only(b, r, t):
+        return b == 1
+
+    def swap_cores(block, joins=everyone):
+        return send(block, sizes, lambda b, r, t: (b, r, t ^ 1) if joins(b, r, t) else None)
+
+    def swap_rows(block, joins=everyone):
+        return send(block, sizes, lambda b, r, t: (b, 1 - r, t) if joins(b, r, t) else None)
+
+    def swap_links(block, distance, joins=everyone):
+        return send(
+            block, sizes, lambda b, r, t: (b, r, t ^ (2 * distance)) if joins(b, r, t) else None
+        )
+
+    def padded_rows(block):
+        return jnp.pad(block, ((0, SLOT - HD), (0, 0)))
+
+    def stacked(pieces):
+        shape = (len(pieces),) + pieces[0].shape
+        out = [(shape, jnp.bfloat16)]
+        (stack,) = kernel_call(stack_kernel, out, pieces, copies=len(pieces), stay=True)
+        return stack.reshape((-1,) + shape[-2:])
+
+    def joined(block, other):
+        return jnp.concatenate([block, other], axis=0)
+
+    keyval_piece = padded_rows(lax.dynamic_slice_in_dim(w_keyval[0].T, row * HD, HD, axis=0))
+    zero_piece = lax.dynamic_slice_in_dim(
+        w_zero.T, row * (w_zero.shape[1] - SLOT), SLOT, axis=0
+    )
+    query_or_out = padded_rows(jnp.where(is_query, w_query[0].T, w_out[0]))
+
+    piece = joined(jnp.where(is_control, keyval_piece, zero_piece), query_or_out)
+    first = [piece, swap_links(piece, ORDER[1]), swap_links(piece, ORDER[2])]
+    started = after(own, piece)
+    far = send(started, sizes, lambda b, r, t: (1 - b, r, t))
+    corner = send(started, sizes, lambda b, r, t: (0, 1 - r, t) if b == 1 else None)
+    tile_shape = (images, tile, D)
+    normed, bias, hidden = kernel_call(
+        functools.partial(norm_kernel, 2 * tile_rows, sizes[2] * tile_cols),
+        [
+            (tile_shape, jnp.bfloat16),
+            ((2 * tile, 6 * tile), jnp.float32),
+            (tile_shape, jnp.float32),
+        ],
+        (spot, own, far, modulation[1]),
+        scratch=[(tile_shape, jnp.bfloat16), (tile_shape, jnp.bfloat16)],
+        copies=2,
+    )
+    side = swap_rows(jnp.where(is_control, normed, own))
+    side, corner, *first = lax.optimization_barrier((side, corner, *first))
+    first.append(swap_links(first[1], ORDER[2]))
+    first = stacked(first)
+    first_other = swap_cores(first)
+    zero_side = swap_rows(first[:, :SLOT], base_only)
+    head_stack = jnp.where(is_query, first_other[:, SLOT:], first[:, SLOT:])
+
+    def to_base(b, r, t):
+        if b == 0:
+            return None
+        return (0, 1 - r, t ^ 1) if t % 2 == r else (0, r, t)
+
+    out_mine = send(head_stack, sizes, to_base)
+    projections = [((tokens, 2 * half), jnp.bfloat16), ((tokens, lanes), jnp.bfloat16)]
+    stacks = ((2, 4, 2 * SLOT, D), jnp.bfloat16)
+    half_stacks = ((2, 4, SLOT, D), jnp.bfloat16)
+    projection_scratch = [
+        ((2 * half + lanes, D), jnp.bfloat16),
+        ((images, 2, tile, D), jnp.bfloat16),
+    ]
+
+    def neighborhood(keyval, query, joins):
+        def across(b, r, t):
+            target = t + 1 if t % 2 else t - 1
+            return (b, r, target) if joins(b, r, t) and 0 <= target < sizes[2] else None
+
+        outer = send(keyval, sizes, across)
+        inner = swap_cores(keyval, joins)
+        (attended,) = kernel_call(
+            attend_kernel, [((tokens, half), jnp.bfloat16)],
+            (spot, query, outer, keyval, inner, bias),
+            scratch=[((tokens, lanes), jnp.bfloat16), ((3, tokens, 2 * half), jnp.bfloat16)],
+            copies=4, micros=8,
+        )
+        return attended.reshape(images, 2, tile, half)
+
+    def finished(attended, other_stack, base, mod, joins):
+        theirs = lax.dynamic_index_in_dim(attended, 1 - row, 1, keepdims=False)
+        (out,) = kernel_call(
+            final_kernel, [(tile_shape, jnp.bfloat16)],
+            (spot, attended, swap_rows(theirs, joins), head_stack, other_stack, base, mod),
+            scratch=[
+                ((images, tile, half), jnp.bfloat16),
+                ((images, tile, half), jnp.bfloat16),
+                half_stacks,
+                ((2 * half, D), jnp.bfloat16),
+            ],
+            copies=3 + images,
+        )
+        return out
+
+    def empty(*outs):
+        return tuple(jnp.zeros(shape, kind) for shape, kind in outs)
+
+    head_shape = ((images, 2, tile, half), jnp.bfloat16)
+    stack_shape = ((4, SLOT, D), jnp.bfloat16)
+    piece_shape = ((SLOT, D), jnp.bfloat16)
+
+    def control_attention():
+        keyval, query = kernel_call(
+            project_kernel, projections, (spot, normed, side, first, first_other),
+            scratch=[stacks] + projection_scratch, copies=2 + 2 * images, micros=5,
+        )
+        return (neighborhood(keyval, query, control_only),) + empty(piece_shape, piece_shape)
+
+    def base_weights():
+        one = swap_links(keyval_piece, ORDER[1], base_only)
+        two = swap_links(keyval_piece, ORDER[2], base_only)
+        return empty(head_shape) + (one, two)
+
+    attended, one, two = lax.cond(is_control, control_attention, base_weights)
+    near = send(attended, sizes, lambda b, r, t: (0, r, t) if b == 1 else None)
+    cross = send(attended, sizes, lambda b, r, t: (0, 1 - r, t) if b == 1 else None)
+    prepared = [((D, D), jnp.bfloat16), ((2 * half + lanes, D), jnp.bfloat16), stack_shape]
+
+    def control_finish():
+        other = swap_rows(head_stack, control_only)
+        out = finished(after(attended, other), other, hidden, modulation[1], control_only)
+        return empty(*prepared) + (out,)
+
+    def base_prepare():
+        three = swap_links(one, ORDER[2], base_only)
+        out_other = swap_cores(after(out_mine, three), base_only)
+        zero_corner = swap_cores(after(zero_side, out_other), base_only)
+        second = stacked([keyval_piece, one, two, three])
+        second_other = swap_cores(after(second, zero_corner), base_only)
+        zero_rows, projection_rows = kernel_call(
+            prepare_kernel, prepared[:2],
+            (spot, first, first_other, zero_side, zero_corner, second, second_other),
+            scratch=[stacks, half_stacks, half_stacks], copies=6,
+        )
+        return (zero_rows, projection_rows, out_other) + empty((tile_shape, jnp.bfloat16))
+
+    zero_rows, projection_rows, out_other, control = lax.cond(
+        is_control, control_finish, base_prepare
+    )
+
+    def base_finish():
+        other = swap_rows(head_stack, base_only)
+        base_in, keyval, query = kernel_call(
+            middle_kernel,
+            [(tile_shape, jnp.float32)] + projections,
+            (
+                spot, own, far, side, corner, near, cross, out_mine, out_other, zero_rows,
+                projection_rows, modulation[1], modulation[0],
+            ),
+            scratch=[
+                ((2, images, tile, D), jnp.bfloat16),
+                ((2, images, tile, D), jnp.bfloat16),
+                ((2, 2 * images * tile, half), jnp.bfloat16),
+                half_stacks,
+                ((2 * half, D), jnp.bfloat16),
+                ((D, D), jnp.bfloat16),
+            ]
+            + projection_scratch,
+            copies=4 * images + 8, micros=8,
+        )
+        attended = neighborhood(keyval, query, base_only)
+        return finished(attended, other, base_in, modulation[0], base_only)
+
+    out = lax.cond(is_control, lambda: control, base_finish)
+    return out.reshape(latent.shape)
+
+
 def solution(mesh):
     placed = (
         P("branch", None, "trow", "tcol", None),
@@ -206,8 +683,12 @@
         P("branch", "tcol", None),
         P(None, "tcol"),
     )
+    sizes = (mesh.shape["branch"], mesh.shape["trow"], mesh.shape["tcol"])
+    body = on_device
+    if sizes == (2, 2, HEADS):
+        body = functools.partial(paired_rows, sizes)
     return jax.shard_map(
-        on_device,
+        body,
         mesh=mesh,
         in_specs=placed,
         out_specs=P("branch", None, "trow", "tcol", None),

time: 215 us -> 119 us (0.55)
  waiting for transfers between devices: 123 us -> 45 us
  local copies, waits for them, and re-layouts: 26 us -> 3.97 us
  starting transfers between devices: 28 us -> 47.1 us
  Pallas kernels: 0 us -> 17 us
  between operations: 13.4 us -> 0.2 us
  matrix products: 10.3 us -> 0 us
  other arithmetic: 13.2 us -> 3.97 us
    all_gather x4 -> x0, waiting for transfers between devices: 79.9 us -> none  [the longest x1 35.3 us: on_device(): lax.all_gather(sources[1], 'tcol', axis=2, tiled=True)]
    ppermute x10 -> x21, starting transfers between devices: 27.9 us -> 47.1 us  [send(): return lax.ppermute(block, AXES, routes(sizes, move))]
    slice x12 -> x1, local copies, waits for them, and re-layouts: 18 us -> 0.76 us  [paired_rows(): modulation[1]]
    pallas_call x0 -> x7, Pallas kernels: none -> 17 us  [kernel_call(): pl.pallas_call(body, out_shape=[jax.ShapeDtypeStruct(shape, kind) for sha...]
    dot_general x4 -> x0, matrix products: 6.71 us -> none  [the longest x1 2.15 us: one_block(): jnp.einsum('ihqk,ikhd->iqhd', weights, value_heads, preferred_element_typ...]
    concatenate x4 -> x1, other arithmetic: 6.18 us -> 0.03 us  [joined(): return jnp.concatenate([block, other], axis=0)]
    ppermute x10 -> x21, waiting for transfers between devices: 40 us -> 45 us  [send(): return lax.ppermute(block, AXES, routes(sizes, move))]
    sub x1 -> x0, matrix products: 3.62 us -> none  [one_block(): raised = jnp.exp(scores - highest)]
  transfers between devices with their start and end apart: 14 -> 21, of which waited for: 12 -> 13; matrix products, arithmetic and copies ran while one was open for 4% -> 1% of each run, Pallas kernels for 0% -> 12%
where the time goes in v1:
time: 119 us; the launch traced here: 117 us
  starting transfers between devices  47.1 us (40%)
  waiting for transfers between devices  45 us (38%)
  Pallas kernels  17 us (14%)
  local copies, waits for them, and re-layouts  3.97 us (3%)
  other arithmetic  3.97 us (3%)
    ppermute x21, starting transfers between devices, send(): return lax.ppermute(block, AXES, routes(sizes, move))  47.1 us
    ppermute x21, waiting for transfers between devices, send(): return lax.ppermute(block, AXES, routes(sizes, move))  45 us
    pallas_call x7, Pallas kernels, kernel_call(): pl.pallas_call(body, out_shape=[jax.ShapeDtypeStruct(shape, kind) for sha...  17 us
  transfers between devices with their start and end apart: 21, of which 13 were waited for; matrix products, arithmetic and copies ran while one was open for 1% of the time, Pallas kernels for 12%

profile of v1, /device:TPU:1, one launch (start us, length us, event | category | flops | bytes accessed | tf_op | source)
XLA Modules:
  0.0 117.5 jit_solution(7209167027880899246)
XLA Ops:
  3.7 2.1 %collective-permute-start.14 = (bf16[2,64,1152]{2,1,0:T(8,128)(2,1)}, bf16[2,64,1152]{2,1,0:T(8,128)(2,1)S(1)}, u32[]{:S(2)}, u32[]{:S(2)}) collective-permute-start(bf16[2,64,1152]{2,1,0:T(8,128)(2,1)} %bitcast.39), channel_id=1, source_target_pairs={{0,16},{1,17},{2,18},{3,19},{4,20},{5,21},{6,22},{7,23},{8,24},{9,... | collective-permute-start | bytes 884744 | tf_op jit(solution)/shard_map/ppermute | solution.py:224
  5.8 3.3 %collective-permute-start.17 = (bf16[160,1152]{1,0:T(8,128)(2,1)S(1)}, bf16[160,1152]{1,0:T(8,128)(2,1)S(1)}, u32[]{:S(2)}, u32[]{:S(2)}) collective-permute-start(bf16[160,1152]{1,0:T(8,128)(2,1)S(1)} %fusion.1.refs_0_), channel_id=1, source_target_pairs={{0,6},{1,7},{2,4},{3,5},{4,2},{5,3},{6,0},{7,1},{8,14},{9,15},{10,... | collective-permute-start | bytes 1105928 | tf_op jit(solution)/shard_map/ppermute | solution.py:224
  12.8 1.7 %shard_map.66 = (bf16[2,64,1152]{2,1,0:T(8,128)(2,1)S(1)}, f32[128,384]{1,0:T(8,128)S(1)}, f32[2,64,1152]{2,1,0:T(8,128)}) custom-call(s32[5]{0:T(128)S(1)} %stack.23.spot, bf16[2,64,1152]{2,1,0:T(8,128)(2,1)S(1)} %bitcast.42, bf16[2,64,1152]{2,1,0:T(8,128)(2,1)S(1)} %collective-permute-done.14.far, f32[3,1152]{1,0:T(4,128)S(1)} %bitcast.38), custom_call_target="tpu_custom_call" | custom-call | bytes 1 | tf_op jit(solution)/shard_map/pallas_call | solution.py:238
  15.7 3.8 %collective-permute-done.16 = bf16[2,64,1152]{2,1,0:T(8,128)(2,1)} collective-permute-done((bf16[2,64,1152]{2,1,0:T(8,128)(2,1)}, bf16[2,64,1152]{2,1,0:T(8,128)(2,1)}, u32[]{:S(2)}, u32[]{:S(2)}) %collective-permute-start.16) | collective-permute-done | bytes 294944 | tf_op jit(solution)/shard_map/ppermute | solution.py:224
  19.5 6.7 %collective-permute-done.18.refs_2_ = bf16[160,1152]{1,0:T(8,128)(2,1)S(1)} collective-permute-done((bf16[160,1152]{1,0:T(8,128)(2,1)S(1)}, bf16[160,1152]{1,0:T(8,128)(2,1)S(1)}, u32[]{:S(2)}, u32[]{:S(2)}) %collective-permute-start.18) | collective-permute-done | bytes 368672 | tf_op jit(solution)/shard_map/ppermute | solution.py:224
  26.9 8.9 %collective-permute-done.19.refs_3_ = bf16[160,1152]{1,0:T(8,128)(2,1)S(1)} collective-permute-done((bf16[160,1152]{1,0:T(8,128)(2,1)S(1)}, bf16[160,1152]{1,0:T(8,128)(2,1)S(1)}, u32[]{:S(2)}, u32[]{:S(2)}) %collective-permute-start.19) | collective-permute-done | bytes 368672 | tf_op jit(solution)/shard_map/ppermute | solution.py:224
  37.9 2.9 %collective-permute-done.20 = bf16[4,160,1152]{2,1,0:T(8,128)(2,1)S(1)} collective-permute-done((bf16[4,160,1152]{2,1,0:T(8,128)(2,1)S(1)}, bf16[4,160,1152]{2,1,0:T(8,128)(2,1)S(1)}, u32[]{:S(2)}, u32[]{:S(2)}) %collective-permute-start.20) | collective-permute-done | bytes 1474592 | tf_op jit(solution)/shard_map/ppermute | solution.py:224
  43.4 3.1 %collective-permute-start.24 = (bf16[4,80,1152]{2,1,0:T(8,128)(2,1)}, bf16[4,80,1152]{2,1,0:T(8,128)(2,1)}, u32[]{:S(2)}, u32[]{:S(2)}) collective-permute-start(bf16[4,80,1152]{2,1,0:T(8,128)(2,1)} %get-tuple-element.185), channel_id=1, source_target_pairs={{0,8},{1,9},{2,10},{3,11},{4,12},{5,13},{6,14},{7,15},{8,0},{9,1},... | collective-permute-start | bytes 2211848 | tf_op jit(solution)/shard_map/ppermute | solution.py:224
  46.5 16.3 %conditional.3 = (bf16[2,2,64,320]{3,2,1,0:T(8,128)(2,1)}, bf16[80,1152]{1,0:T(8,128)(2,1)S(1)}, bf16[80,1152]{1,0:T(8,128)(2,1)S(1)}) conditional(s32[]{:T(128)} %convert_element_type.8, bf16[80,1152]{1,0:T(8,128)(2,1)} %get-tuple-element.187, (s32[5]{0:T(128)S(1)}, bf16[2,64,1152]{2,1,0:T(8,128)(2,1)}, bf16[2,64,1152]{2,1,0:T(8,128)(2,1)}, ...), branch_computations={%region_0.1_spmd, %region_1.2_spmd} | conditional | bytes 51090184 | solution.py:623
  46.5 6.8 %collective-permute-start = (bf16[80,1152]{1,0:T(8,128)(2,1)}, bf16[80,1152]{1,0:T(8,128)(2,1)S(1)}, u32[]{:S(2)}, u32[]{:S(2)}) collective-permute-start(bf16[80,1152]{1,0:T(8,128)(2,1)} %param), channel_id=1, source_target_pairs={{0,6},{1,7},{2,4},{3,5},{4,2},{5,3},{6,0},{7,1},{8,14},{9,15},{10,... | collective-permute-start | bytes 552968 | tf_op jit(solution)/shard_map/cond/branch_0_fun/ppermute | solution.py:224
  53.3 1.9 %collective-permute-start.1 = (bf16[80,1152]{1,0:T(8,128)(2,1)}, bf16[80,1152]{1,0:T(8,128)(2,1)S(1)}, u32[]{:S(2)}, u32[]{:S(2)}) collective-permute-start(bf16[80,1152]{1,0:T(8,128)(2,1)} %param), channel_id=1, source_target_pairs={{0,2},{1,3},{2,0},{3,1},{4,6},{5,7},{6,4},{7,5},{8,10},{9,11},{10,... | collective-permute-start | bytes 552968 | tf_op jit(solution)/shard_map/cond/branch_0_fun/ppermute | solution.py:224
  55.2 2.7 %collective-permute-done = bf16[80,1152]{1,0:T(8,128)(2,1)S(1)} collective-permute-done((bf16[80,1152]{1,0:T(8,128)(2,1)}, bf16[80,1152]{1,0:T(8,128)(2,1)S(1)}, u32[]{:S(2)}, u32[]{:S(2)}) %collective-permute-start) | collective-permute-done | bytes 184352 | tf_op jit(solution)/shard_map/cond/branch_0_fun/ppermute | solution.py:224
  57.9 4.2 %collective-permute-done.1 = bf16[80,1152]{1,0:T(8,128)(2,1)S(1)} collective-permute-done((bf16[80,1152]{1,0:T(8,128)(2,1)}, bf16[80,1152]{1,0:T(8,128)(2,1)S(1)}, u32[]{:S(2)}, u32[]{:S(2)}) %collective-permute-start.1) | collective-permute-done | bytes 184352 | tf_op jit(solution)/shard_map/cond/branch_0_fun/ppermute | solution.py:224
  65.4 24.1 %conditional.4 = (bf16[1152,1152]{1,0:T(8,128)(2,1)S(1)}, bf16[1024,1152]{1,0:T(8,128)(2,1)S(1)}, bf16[4,80,1152]{2,1,0:T(8,128)(2,1)S(1)}, bf16[2,64,1152]{2,1,0:T(8,128)(2,1)S(1)}) conditional(s32[]{:T(128)} %convert_element_type.8, (bf16[80,1152]{1,0:T(8,128)(2,1)S(1)}, bf16[4,80,1152]{2,1,0:T(8,128)(2,1)}, bf16[4,80,1152]{2,1,0:T(8,128)(2,1)}, ...), branch_computations={%region_2.3_spmd, %region_3.4_spmd} | conditional | flops 4 | bytes 11354364 | solution.py:646
  65.5 3.0 %collective-permute-start.4 = (bf16[80,1152]{1,0:T(8,128)(2,1)S(1)}, bf16[80,1152]{1,0:T(8,128)(2,1)S(1)}, u32[]{:S(2)}, u32[]{:S(2)}) collective-permute-start(bf16[80,1152]{1,0:T(8,128)(2,1)S(1)} %get-tuple-element.96.refs_1_), channel_id=1, source_target_pairs={{0,2},{1,3},{2,0},{3,1},{4,6},{5,7},{6,4},{7,5},{8,10},{9,11},{10,... | collective-permute-start | bytes 552968 | tf_op jit(solution)/shard_map/cond/branch_0_fun/ppermute | solution.py:224
  68.5 4.1 %collective-permute-done.4.refs_3_ = bf16[80,1152]{1,0:T(8,128)(2,1)S(1)} collective-permute-done((bf16[80,1152]{1,0:T(8,128)(2,1)S(1)}, bf16[80,1152]{1,0:T(8,128)(2,1)S(1)}, u32[]{:S(2)}, u32[]{:S(2)}) %collective-permute-start.4) | collective-permute-done | bytes 184352 | tf_op jit(solution)/shard_map/cond/branch_0_fun/ppermute | solution.py:224
  72.5 3.8 %collective-permute-start.5 = (bf16[4,80,1152]{2,1,0:T(8,128)(2,1)}, bf16[4,80,1152]{2,1,0:T(8,128)(2,1)S(1)}, u32[]{:S(2)}, u32[]{:S(2)}) collective-permute-start(bf16[4,80,1152]{2,1,0:T(8,128)(2,1)} %get-tuple-element.97), channel_id=1, source_target_pairs={{0,1},{1,0},{2,3},{3,2},{4,5},{5,4},{6,7},{7,6},{8,9},{9,8},{10,11... | collective-permute-start | bytes 2211848 | tf_op jit(solution)/shard_map/cond/branch_0_fun/ppermute | solution.py:224
  76.3 2.0 %collective-permute-done.5 = bf16[4,80,1152]{2,1,0:T(8,128)(2,1)S(1)} collective-permute-done((bf16[4,80,1152]{2,1,0:T(8,128)(2,1)}, bf16[4,80,1152]{2,1,0:T(8,128)(2,1)S(1)}, u32[]{:S(2)}, u32[]{:S(2)}) %collective-permute-start.5) | collective-permute-done | bytes 737312 | tf_op jit(solution)/shard_map/cond/branch_0_fun/ppermute | solution.py:224
  78.3 2.3 %collective-permute-start.6 = (bf16[4,80,1152]{2,1,0:T(8,128)(2,1)}, bf16[4,80,1152]{2,1,0:T(8,128)(2,1)S(1)}, u32[]{:S(2)}, u32[]{:S(2)}) collective-permute-start(bf16[4,80,1152]{2,1,0:T(8,128)(2,1)} %get-tuple-element.98.zero_side), channel_id=1, source_target_pairs={{0,1},{1,0},{2,3},{3,2},{4,5},{5,4},{6,7},{7,6},{8,9},{9,8},{10,11... | collective-permute-start | bytes 2211848 | tf_op jit(solution)/shard_map/cond/branch_0_fun/ppermute | solution.py:224
  82.7 2.3 %collective-permute-start.7 = (bf16[4,80,1152]{2,1,0:T(8,128)(2,1)S(1)}, bf16[4,80,1152]{2,1,0:T(8,128)(2,1)S(1)}, u32[]{:S(2)}, u32[]{:S(2)}) collective-permute-start(bf16[4,80,1152]{2,1,0:T(8,128)(2,1)S(1)} %branch_0_fun.5.second), channel_id=1, source_target_pairs={{0,1},{1,0},{2,3},{3,2},{4,5},{5,4},{6,7},{7,6},{8,9},{9,8},{10,11... | collective-permute-start | bytes 2211848 | tf_op jit(solution)/shard_map/cond/branch_0_fun/ppermute | solution.py:224
  84.9 1.8 %collective-permute-done.7.second_other = bf16[4,80,1152]{2,1,0:T(8,128)(2,1)S(1)} collective-permute-done((bf16[4,80,1152]{2,1,0:T(8,128)(2,1)S(1)}, bf16[4,80,1152]{2,1,0:T(8,128)(2,1)S(1)}, u32[]{:S(2)}, u32[]{:S(2)}) %collective-permute-start.7) | collective-permute-done | bytes 737312 | tf_op jit(solution)/shard_map/cond/branch_0_fun/ppermute | solution.py:224
  86.8 2.7 %branch_0_fun.6 = (bf16[1152,1152]{1,0:T(8,128)(2,1)S(1)}, bf16[1024,1152]{1,0:T(8,128)(2,1)S(1)}) custom-call(s32[5]{0:T(128)S(1)} %get-tuple-element.91.spot, bf16[4,160,1152]{2,1,0:T(8,128)(2,1)S(1)} %get-tuple-element.92.first, bf16[4,160,1152]{2,1,0:T(8,128)(2,1)S(1)} %get-tuple-element.93.first_other, ...), custom_call_target="tpu_custom_call" | custom-call | bytes 1 | tf_op jit(solution)/shard_map/cond/branch_0_fun/pallas_call | solution.py:238
  89.5 27.2 %conditional.5 = (bf16[1,2,8,8,1152]{4,3,2,1,0:T(8,128)(2,1)S(1)}) conditional(s32[]{:T(128)} %convert_element_type.8, (f32[2,3,1152]{2,0,1:T(2,128)S(1)}, s32[5]{0:T(128)S(1)}, bf16[2,64,1152]{2,1,0:T(8,128)(2,1)}, bf16[2,64,1152]{2,1,0:T(8,128)(2,1)}, bf16[2,64,1152]{2,1,0:T(8,128)(2,1)}, /*index=5*/bf16[2,64,1152]{2,1,0:T(8,128)(2,1)}, ...), branch_computations={%region_4.5_spmd, %region_5.6_spmd} | conditional | flops 4 | bytes 65372888 | solution.py:673
  89.6 2.2 %collective-permute-start.13 = (bf16[4,80,1152]{2,1,0:T(8,128)(2,1)}, bf16[4,80,1152]{2,1,0:T(8,128)(2,1)S(1)}, u32[]{:S(2)}, u32[]{:S(2)}) collective-permute-start(bf16[4,80,1152]{2,1,0:T(8,128)(2,1)} %get-tuple-element.127.mine), channel_id=1, source_target_pairs={{0,8},{1,9},{2,10},{3,11},{4,12},{5,13},{6,14},{7,15},{8,0},{9,1},... | collective-permute-start | bytes 2211848 | tf_op jit(solution)/shard_map/cond/branch_0_fun/ppermute | solution.py:224
  91.8 5.6 %branch_0_fun.7 = (f32[2,64,1152]{2,1,0:T(8,128)S(1)}, bf16[256,640]{1,0:T(8,128)(2,1)S(1)}, bf16[256,384]{1,0:T(8,128)(2,1)S(1)}) custom-call(s32[5]{0:T(128)S(1)} %get-tuple-element.111.spot, bf16[2,64,1152]{2,1,0:T(8,128)(2,1)} %get-tuple-element.112.own, bf16[2,64,1152]{2,1,0:T(8,128)(2,1)} %get-tuple-element.113.far, ...), custom_call_target="tpu_custom_call" | custom-call | bytes 29600000 | tf_op jit(solution)/shard_map/cond/branch_0_fun/pallas_call | solution.py:238
  97.4 3.5 %collective-permute-start.10 = (bf16[256,640]{1,0:T(8,128)(2,1)S(1)}, bf16[256,640]{1,0:T(8,128)(2,1)S(1)}, u32[]{:S(2)}, u32[]{:S(2)}) collective-permute-start(bf16[256,640]{1,0:T(8,128)(2,1)S(1)} %get-tuple-element.124.here), channel_id=1, source_target_pairs={{1,2},{2,1},{3,4},{4,3},{5,6},{6,5},{9,10},{10,9},{11,12},{12,11},... | collective-permute-start | bytes 983048 | tf_op jit(solution)/shard_map/cond/branch_0_fun/ppermute | solution.py:224
  100.9 1.9 %collective-permute-start.11 = (bf16[256,640]{1,0:T(8,128)(2,1)S(1)}, bf16[256,640]{1,0:T(8,128)(2,1)S(1)}, u32[]{:S(2)}, u32[]{:S(2)}) collective-permute-start(bf16[256,640]{1,0:T(8,128)(2,1)S(1)} %get-tuple-element.124.here), channel_id=1, source_target_pairs={{0,1},{1,0},{2,3},{3,2},{4,5},{5,4},{6,7},{7,6},{8,9},{9,8},{10,11... | collective-permute-start | bytes 983048 | tf_op jit(solution)/shard_map/cond/branch_0_fun/ppermute | solution.py:224
  102.9 3.2 %collective-permute-done.10.outer = bf16[256,640]{1,0:T(8,128)(2,1)S(1)} collective-permute-done((bf16[256,640]{1,0:T(8,128)(2,1)S(1)}, bf16[256,640]{1,0:T(8,128)(2,1)S(1)}, u32[]{:S(2)}, u32[]{:S(2)}) %collective-permute-start.10) | collective-permute-done | bytes 327712 | tf_op jit(solution)/shard_map/cond/branch_0_fun/ppermute | solution.py:224
  106.1 2.7 %branch_0_fun.8 = bf16[256,320]{1,0:T(8,128)(2,1)S(1)} custom-call(s32[5]{0:T(128)S(1)} %get-tuple-element.111.spot, bf16[256,384]{1,0:T(8,128)(2,1)S(1)} %get-tuple-element.123.queries, bf16[256,640]{1,0:T(8,128)(2,1)S(1)} %collective-permute-done.10.outer, bf16[256,640]{1,0:T(8,128)(2,1)S(1)} %get-tuple-element.124.here, ...), custom_call_target="tpu_custom_call" | custom-call | bytes 29600000 | tf_op jit(solution)/shard_map/cond/branch_0_fun/pallas_call | solution.py:238
  108.8 3.1 %collective-permute-start.12 = (bf16[2,64,320]{2,1,0:T(8,128)(2,1)S(1)}, bf16[2,64,320]{2,1,0:T(8,128)(2,1)S(1)}, u32[]{:S(2)}, u32[]{:S(2)}) collective-permute-start(bf16[2,64,320]{2,1,0:T(8,128)(2,1)S(1)} %dynamic-slice_bitcast_fusion.1), channel_id=1, source_target_pairs={{0,8},{1,9},{2,10},{3,11},{4,12},{5,13},{6,14},{7,15},{8,0},{9,1},... | collective-permute-start | bytes 245768 | tf_op jit(solution)/shard_map/cond/branch_0_fun/ppermute | solution.py:224
  111.9 2.2 %collective-permute-done.12.side = bf16[2,64,320]{2,1,0:T(8,128)(2,1)S(1)} collective-permute-done((bf16[2,64,320]{2,1,0:T(8,128)(2,1)S(1)}, bf16[2,64,320]{2,1,0:T(8,128)(2,1)S(1)}, u32[]{:S(2)}, u32[]{:S(2)}) %collective-permute-start.12) | collective-permute-done | bytes 81952 | tf_op jit(solution)/shard_map/cond/branch_0_fun/ppermute | solution.py:224
  114.2 2.6 %branch_0_fun.9 = bf16[2,64,1152]{2,1,0:T(8,128)(2,1)S(1)} custom-call(s32[5]{0:T(128)S(1)} %get-tuple-element.111.spot, bf16[2,2,64,320]{3,2,1,0:T(8,128)(2,1)S(1)} %bitcast.37, bf16[2,64,320]{2,1,0:T(8,128)(2,1)S(1)} %collective-permute-done.12.side, bf16[4,80,1152]{2,1,0:T(8,128)(2,1)} %get-tuple-element.127.mine, ...), custom_call_target="tpu_custom_call" | custom-call | bytes 1 | tf_op jit(solution)/shard_map/cond/branch_0_fun/pallas_call | solution.py:238
  (52 shorter events, 19.9 us)
Async XLA Ops:
  0.0 1.0 copy-start
  0.0 12.8 %copy-start.1 = (bf16[1,2,8,8,1152]{4,3,2,1,0:T(8,128)(2,1)S(1)}, bf16[1,2,8,8,1152]{4,3,2,1,0:T(8,128)(2,1)}, u32[]{:S(2)}) copy-start(bf16[1,2,8,8,1152]{4,3,2,1,0:T(8,128)(2,1)} %param.12) | copy-start | bytes 884740
  3.7 9.1 %collective-permute-start.14 = (bf16[2,64,1152]{2,1,0:T(8,128)(2,1)}, bf16[2,64,1152]{2,1,0:T(8,128)(2,1)S(1)}, u32[]{:S(2)}, u32[]{:S(2)}) collective-permute-start(bf16[2,64,1152]{2,1,0:T(8,128)(2,1)} %bitcast.39), channel_id=1, source_target_pairs={{0,16},{1,17},{2,18},{3,19},{4,20},{5,21},{6,22},{7,23},{8,24},{9,... | collective-permute-start | bytes 884744 | tf_op jit(solution)/shard_map/ppermute | solution.py:224
  5.8 13.7 %collective-permute-start.17 = (bf16[160,1152]{1,0:T(8,128)(2,1)S(1)}, bf16[160,1152]{1,0:T(8,128)(2,1)S(1)}, u32[]{:S(2)}, u32[]{:S(2)}) collective-permute-start(bf16[160,1152]{1,0:T(8,128)(2,1)S(1)} %fusion.1.refs_0_), channel_id=1, source_target_pairs={{0,6},{1,7},{2,4},{3,5},{4,2},{5,3},{6,0},{7,1},{8,14},{9,15},{10,... | collective-permute-start | bytes 1105928 | tf_op jit(solution)/shard_map/ppermute | solution.py:224
  9.2 17.0 %collective-permute-start.18 = (bf16[160,1152]{1,0:T(8,128)(2,1)S(1)}, bf16[160,1152]{1,0:T(8,128)(2,1)S(1)}, u32[]{:S(2)}, u32[]{:S(2)}) collective-permute-start(bf16[160,1152]{1,0:T(8,128)(2,1)S(1)} %fusion.1.refs_0_), channel_id=1, source_target_pairs={{0,2},{1,3},{2,0},{3,1},{4,6},{5,7},{6,4},{7,5},{8,10},{9,11},{10,... | collective-permute-start | bytes 1105928 | tf_op jit(solution)/shard_map/ppermute | solution.py:224
  9.2 10.4 %collective-permute-start.16 = (bf16[2,64,1152]{2,1,0:T(8,128)(2,1)}, bf16[2,64,1152]{2,1,0:T(8,128)(2,1)}, u32[]{:S(2)}, u32[]{:S(2)}) collective-permute-start(bf16[2,64,1152]{2,1,0:T(8,128)(2,1)} %bitcast.40), channel_id=1, source_target_pairs={{16,8},{17,9},{18,10},{19,11},{20,12},{21,13},{22,14},{23,15},{24,... | collective-permute-start | bytes 884744 | tf_op jit(solution)/shard_map/ppermute | solution.py:224
  12.8 13.5 %copy-start.3 = (bf16[2,64,1152]{2,1,0:T(8,128)(2,1)}, bf16[2,64,1152]{2,1,0:T(8,128)(2,1)S(1)}, u32[]{:S(2)}) copy-start(bf16[2,64,1152]{2,1,0:T(8,128)(2,1)S(1)} %collective-permute-done.14.far) | copy-start | bytes 884740
  14.4 11.8 %copy-start.2 = (bf16[2,64,1152]{2,1,0:T(8,128)(2,1)}, bf16[2,64,1152]{2,1,0:T(8,128)(2,1)S(1)}, u32[]{:S(2)}) copy-start(bf16[2,64,1152]{2,1,0:T(8,128)(2,1)S(1)} %get-tuple-element.146) | copy-start | bytes 884740
  14.5 11.7 %collective-permute-start.15 = (bf16[2,64,1152]{2,1,0:T(8,128)(2,1)S(1)}, bf16[2,64,1152]{2,1,0:T(8,128)(2,1)S(1)}, u32[]{:S(2)}, u32[]{:S(2)}) collective-permute-start(bf16[2,64,1152]{2,1,0:T(8,128)(2,1)S(1)} %broadcast_select_fusion), channel_id=1, source_target_pairs={{0,8},{1,9},{2,10},{3,11},{4,12},{5,13},{6,14},{7,15},{8,0},{9,1},... | collective-permute-start | bytes 884744 | tf_op jit(solution)/shard_map/ppermute | solution.py:224
  26.2 0.7 copy-start.4
  26.2 9.7 %collective-permute-start.19 = (bf16[160,1152]{1,0:T(8,128)(2,1)S(1)}, bf16[160,1152]{1,0:T(8,128)(2,1)S(1)}, u32[]{:S(2)}, u32[]{:S(2)}) collective-permute-start(bf16[160,1152]{1,0:T(8,128)(2,1)S(1)} %collective-permute-done.17.refs_1_), channel_id=1, source_target_pairs={{0,2},{1,3},{2,0},{3,1},{4,6},{5,7},{6,4},{7,5},{8,10},{9,11},{10,... | collective-permute-start | bytes 1105928 | tf_op jit(solution)/shard_map/ppermute | solution.py:224
  36.5 4.3 %collective-permute-start.20 = (bf16[4,160,1152]{2,1,0:T(8,128)(2,1)S(1)}, bf16[4,160,1152]{2,1,0:T(8,128)(2,1)S(1)}, u32[]{:S(2)}, u32[]{:S(2)}) collective-permute-start(bf16[4,160,1152]{2,1,0:T(8,128)(2,1)S(1)} %shard_map.67), channel_id=1, source_target_pairs={{0,1},{1,0},{2,3},{3,2},{4,5},{5,4},{6,7},{7,6},{8,9},{9,8},{10,11... | collective-permute-start | bytes 4423688 | tf_op jit(solution)/shard_map/ppermute | solution.py:224
  42.1 23.3 %collective-permute-start.23 = (bf16[4,80,1152]{2,1,0:T(8,128)(2,1)}, bf16[4,80,1152]{2,1,0:T(8,128)(2,1)}, u32[]{:S(2)}, u32[]{:S(2)}) collective-permute-start(bf16[4,80,1152]{2,1,0:T(8,128)(2,1)} %get-tuple-element.186), channel_id=1, source_target_pairs={{16,9},{17,1},{18,11},{19,3},{20,13},{21,5},{22,15},{23,7},{24,8},... | collective-permute-start | bytes 2211848 | tf_op jit(solution)/shard_map/ppermute | solution.py:224
  43.4 22.0 %collective-permute-start.24 = (bf16[4,80,1152]{2,1,0:T(8,128)(2,1)}, bf16[4,80,1152]{2,1,0:T(8,128)(2,1)}, u32[]{:S(2)}, u32[]{:S(2)}) collective-permute-start(bf16[4,80,1152]{2,1,0:T(8,128)(2,1)} %get-tuple-element.185), channel_id=1, source_target_pairs={{0,8},{1,9},{2,10},{3,11},{4,12},{5,13},{6,14},{7,15},{8,0},{9,1},... | collective-permute-start | bytes 2211848 | tf_op jit(solution)/shard_map/ppermute | solution.py:224
  46.5 18.9 %copy-start.8 = (f32[2,3,1152]{2,0,1:T(2,128)S(1)}, f32[2,3,1152]{2,0,1:T(2,128)}, u32[]{:S(2)}) copy-start(f32[2,3,1152]{2,0,1:T(2,128)} %param.13) | copy-start | bytes 82948
  46.5 11.4 %collective-permute-start = (bf16[80,1152]{1,0:T(8,128)(2,1)}, bf16[80,1152]{1,0:T(8,128)(2,1)S(1)}, u32[]{:S(2)}, u32[]{:S(2)}) collective-permute-start(bf16[80,1152]{1,0:T(8,128)(2,1)} %param), channel_id=1, source_target_pairs={{0,6},{1,7},{2,4},{3,5},{4,2},{5,3},{6,0},{7,1},{8,14},{9,15},{10,... | collective-permute-start | bytes 552968 | tf_op jit(solution)/shard_map/cond/branch_0_fun/ppermute | solution.py:224
  53.3 8.8 %collective-permute-start.1 = (bf16[80,1152]{1,0:T(8,128)(2,1)}, bf16[80,1152]{1,0:T(8,128)(2,1)S(1)}, u32[]{:S(2)}, u32[]{:S(2)}) collective-permute-start(bf16[80,1152]{1,0:T(8,128)(2,1)} %param), channel_id=1, source_target_pairs={{0,2},{1,3},{2,0},{3,1},{4,6},{5,7},{6,4},{7,5},{8,10},{9,11},{10,... | collective-permute-start | bytes 552968 | tf_op jit(solution)/shard_map/cond/branch_0_fun/ppermute | solution.py:224
  62.8 26.7 %collective-permute-start.21 = (bf16[2,2,64,320]{3,2,1,0:T(8,128)(2,1)}, bf16[2,2,64,320]{3,2,1,0:T(8,128)(2,1)}, u32[]{:S(2)}, u32[]{:S(2)}) collective-permute-start(bf16[2,2,64,320]{3,2,1,0:T(8,128)(2,1)} %get-tuple-element.153), channel_id=1, source_target_pairs={{16,0},{17,1},{18,2},{19,3},{20,4},{21,5},{22,6},{23,7},{24,8},{25... | collective-permute-start | bytes 491528 | tf_op jit(solution)/shard_map/ppermute | solution.py:224
  64.1 25.4 %collective-permute-start.22 = (bf16[2,2,64,320]{3,2,1,0:T(8,128)(2,1)}, bf16[2,2,64,320]{3,2,1,0:T(8,128)(2,1)}, u32[]{:S(2)}, u32[]{:S(2)}) collective-permute-start(bf16[2,2,64,320]{3,2,1,0:T(8,128)(2,1)} %get-tuple-element.153), channel_id=1, source_target_pairs={{16,8},{17,9},{18,10},{19,11},{20,12},{21,13},{22,14},{23,15},{24,... | collective-permute-start | bytes 491528 | tf_op jit(solution)/shard_map/ppermute | solution.py:224
  65.4 15.2 %copy-start.6 = (bf16[80,1152]{1,0:T(8,128)(2,1)}, bf16[80,1152]{1,0:T(8,128)(2,1)S(1)}, u32[]{:S(2)}) copy-start(bf16[80,1152]{1,0:T(8,128)(2,1)S(1)} %get-tuple-element.96.refs_1_) | copy-start | bytes 552964 | tf_op jit(solution)/shard_map/cond
  65.5 15.2 %copy-start.7 = (bf16[80,1152]{1,0:T(8,128)(2,1)}, bf16[80,1152]{1,0:T(8,128)(2,1)S(1)}, u32[]{:S(2)}) copy-start(bf16[80,1152]{1,0:T(8,128)(2,1)S(1)} %get-tuple-element.100.refs_2_) | copy-start | bytes 552964 | tf_op jit(solution)/shard_map/cond
  65.5 7.1 %collective-permute-start.4 = (bf16[80,1152]{1,0:T(8,128)(2,1)S(1)}, bf16[80,1152]{1,0:T(8,128)(2,1)S(1)}, u32[]{:S(2)}, u32[]{:S(2)}) collective-permute-start(bf16[80,1152]{1,0:T(8,128)(2,1)S(1)} %get-tuple-element.96.refs_1_), channel_id=1, source_target_pairs={{0,2},{1,3},{2,0},{3,1},{4,6},{5,7},{6,4},{7,5},{8,10},{9,11},{10,... | collective-permute-start | bytes 552968 | tf_op jit(solution)/shard_map/cond/branch_0_fun/ppermute | solution.py:224
  72.5 5.8 %collective-permute-start.5 = (bf16[4,80,1152]{2,1,0:T(8,128)(2,1)}, bf16[4,80,1152]{2,1,0:T(8,128)(2,1)S(1)}, u32[]{:S(2)}, u32[]{:S(2)}) collective-permute-start(bf16[4,80,1152]{2,1,0:T(8,128)(2,1)} %get-tuple-element.97), channel_id=1, source_target_pairs={{0,1},{1,0},{2,3},{3,2},{4,5},{5,4},{6,7},{7,6},{8,9},{9,8},{10,11... | collective-permute-start | bytes 2211848 | tf_op jit(solution)/shard_map/cond/branch_0_fun/ppermute | solution.py:224
  78.3 4.3 %collective-permute-start.6 = (bf16[4,80,1152]{2,1,0:T(8,128)(2,1)}, bf16[4,80,1152]{2,1,0:T(8,128)(2,1)S(1)}, u32[]{:S(2)}, u32[]{:S(2)}) collective-permute-start(bf16[4,80,1152]{2,1,0:T(8,128)(2,1)} %get-tuple-element.98.zero_side), channel_id=1, source_target_pairs={{0,1},{1,0},{2,3},{3,2},{4,5},{5,4},{6,7},{7,6},{8,9},{9,8},{10,11... | collective-permute-start | bytes 2211848 | tf_op jit(solution)/shard_map/cond/branch_0_fun/ppermute | solution.py:224
  82.7 4.1 %collective-permute-start.7 = (bf16[4,80,1152]{2,1,0:T(8,128)(2,1)S(1)}, bf16[4,80,1152]{2,1,0:T(8,128)(2,1)S(1)}, u32[]{:S(2)}, u32[]{:S(2)}) collective-permute-start(bf16[4,80,1152]{2,1,0:T(8,128)(2,1)S(1)} %branch_0_fun.5.second), channel_id=1, source_target_pairs={{0,1},{1,0},{2,3},{3,2},{4,5},{5,4},{6,7},{7,6},{8,9},{9,8},{10,11... | collective-permute-start | bytes 2211848 | tf_op jit(solution)/shard_map/cond/branch_0_fun/ppermute | solution.py:224
  89.6 24.6 %collective-permute-start.13 = (bf16[4,80,1152]{2,1,0:T(8,128)(2,1)}, bf16[4,80,1152]{2,1,0:T(8,128)(2,1)S(1)}, u32[]{:S(2)}, u32[]{:S(2)}) collective-permute-start(bf16[4,80,1152]{2,1,0:T(8,128)(2,1)} %get-tuple-element.127.mine), channel_id=1, source_target_pairs={{0,8},{1,9},{2,10},{3,11},{4,12},{5,13},{6,14},{7,15},{8,0},{9,1},... | collective-permute-start | bytes 2211848 | tf_op jit(solution)/shard_map/cond/branch_0_fun/ppermute | solution.py:224
  97.4 8.7 %collective-permute-start.10 = (bf16[256,640]{1,0:T(8,128)(2,1)S(1)}, bf16[256,640]{1,0:T(8,128)(2,1)S(1)}, u32[]{:S(2)}, u32[]{:S(2)}) collective-permute-start(bf16[256,640]{1,0:T(8,128)(2,1)S(1)} %get-tuple-element.124.here), channel_id=1, source_target_pairs={{1,2},{2,1},{3,4},{4,3},{5,6},{6,5},{9,10},{10,9},{11,12},{12,11},... | collective-permute-start | bytes 983048 | tf_op jit(solution)/shard_map/cond/branch_0_fun/ppermute | solution.py:224
  100.9 5.2 %collective-permute-start.11 = (bf16[256,640]{1,0:T(8,128)(2,1)S(1)}, bf16[256,640]{1,0:T(8,128)(2,1)S(1)}, u32[]{:S(2)}, u32[]{:S(2)}) collective-permute-start(bf16[256,640]{1,0:T(8,128)(2,1)S(1)} %get-tuple-element.124.here), channel_id=1, source_target_pairs={{0,1},{1,0},{2,3},{3,2},{4,5},{5,4},{6,7},{7,6},{8,9},{9,8},{10,11... | collective-permute-start | bytes 983048 | tf_op jit(solution)/shard_map/cond/branch_0_fun/ppermute | solution.py:224
  108.8 5.4 %collective-permute-start.12 = (bf16[2,64,320]{2,1,0:T(8,128)(2,1)S(1)}, bf16[2,64,320]{2,1,0:T(8,128)(2,1)S(1)}, u32[]{:S(2)}, u32[]{:S(2)}) collective-permute-start(bf16[2,64,320]{2,1,0:T(8,128)(2,1)S(1)} %dynamic-slice_bitcast_fusion.1), channel_id=1, source_target_pairs={{0,8},{1,9},{2,10},{3,11},{4,12},{5,13},{6,14},{7,15},{8,0},{9,1},... | collective-permute-start | bytes 245768 | tf_op jit(solution)/shard_map/cond/branch_0_fun/ppermute | solution.py:224
  116.8 0.7 copy-start.5

commit v2 on v1

--- a/solution.py
+++ b/solution.py
@@ -202,6 +202,7 @@
 
 AXES = ("branch", "trow", "tcol")
 SLOT = 80
+SHARED = 64
 ORDER = (0, 3, 1, 2)
 
 
@@ -275,9 +276,14 @@
     finish(begin([(piece, stacked.at[n]) for n, piece in enumerate(pieces)], done))
 
 
-def norm_kernel(total_rows, total_cols, spot, own, far, mod, normed, bias, total, first, second, done):
-    copies = [(own, first), (far, second)]
-    started = begin(copies, done)
+def norm_kernel(spot, own, far, mod, normed, first, second, done):
+    finish(begin([(own, first), (far, second)], done))
+    for image in range(own.shape[0]):
+        hidden = first[image].astype(jnp.float32) + second[image].astype(jnp.float32)
+        normed[image] = modulate(hidden, mod)
+
+
+def bias_kernel(total_rows, total_cols, spot, bias, done):
     radius = WIN // 2
     query = lax.broadcasted_iota(jnp.int32, bias.shape, 0)
     key = lax.broadcasted_iota(jnp.int32, bias.shape, 1)
@@ -294,11 +300,10 @@
         & (key_col < col_start + WIN)
     )
     bias[...] = jnp.where(inside, 0.0, -1e30)
-    finish(started)
-    for image in range(own.shape[0]):
-        hidden = first[image].astype(jnp.float32) + second[image].astype(jnp.float32)
-        total[image] = hidden
-        normed[image] = modulate(hidden, mod)
+
+
+def unset_kernel(spot, out, done):
+    pass
 
 
 def in_order(origin):
@@ -319,10 +324,8 @@
         weight[rows_at(start, SLOT), :] = stack[step]
 
 
-def arrange_queries(link, stacks, row, weight):
-    start = weight.shape[0] - 4 * SLOT
-    weight[8 * SLOT : start, :] = jnp.zeros((start - 8 * SLOT, weight.shape[1]), weight.dtype)
-    arrange_heads(link, stacks.at[row, :, SLOT:], start, weight)
+def clear_rows(weight, start, stop):
+    weight[start:stop, :] = jnp.zeros((stop - start, weight.shape[1]), weight.dtype)
 
 
 def project_kernel(spot, normed, normed_other, mine, other, keyval, query, stacks, weight, both, done):
@@ -333,7 +336,9 @@
         copies.append((normed_other.at[image], both.at[image, 1 - row]))
     finish(begin(copies, done))
     arrange_keyvals(link, stacks, weight)
-    arrange_queries(link, stacks, row, weight)
+    start = weight.shape[0] - 4 * SLOT
+    clear_rows(weight, 8 * SLOT, start)
+    arrange_heads(link, stacks.at[row, :, SLOT : 2 * SLOT], start, weight)
     tokens = both[...].reshape(-1, both.shape[3])
     projected = dot_rows(tokens, weight[...]).astype(keyval.dtype)
     keyval[...] = projected[:, : keyval.shape[1]]
@@ -381,32 +386,18 @@
         out[rows, :] = total[:, : out.shape[1]].astype(out.dtype)
 
 
-def prepare_kernel(
-    spot, first, first_other, zero_side, zero_corner, second, second_other, w_zero, weight,
-    stacks, zeros, keyval_stacks, done,
-):
-    row, link, core = (spot[1], spot[2], spot[3])
-    copies = [(first, stacks.at[core]), (first_other, stacks.at[1 - core])]
-    copies += [(zero_side, zeros.at[core]), (zero_corner, zeros.at[1 - core])]
-    copies += [(second, keyval_stacks.at[core]), (second_other, keyval_stacks.at[1 - core])]
-    started = begin(copies, done)
-    finish(started)
-    shard = w_zero.shape[0] // 8
-    for at in range(2):
-        for step in range(4):
-            start = (2 * (link ^ ORDER[step]) + at) * shard
-            mine = start + row * (shard - SLOT)
-            w_zero[rows_at(mine, SLOT), :] = stacks[at, step, :SLOT]
-            other = start + (1 - row) * (shard - SLOT)
-            w_zero[rows_at(other, SLOT), :] = zeros[at, step]
-    arrange_keyvals(link, keyval_stacks, weight)
-    arrange_queries(link, stacks, row, weight)
+def head_rows_kernel(index, spot, mine, other, out, outs, done):
+    at = spot[index]
+    copies = [(mine, outs.at[1 - at]), (other, outs.at[at])]
+    finish(begin(copies, done))
+    for part in range(2):
+        arrange_heads(spot[2], outs.at[part], part * 4 * SLOT, out)
 
 
 def middle_kernel(
-    spot, own, far, side, corner, near, cross, out_mine, out_other, zero_rows, projections,
-    mod, mod_base, base_in, keyval, query,
-    base_rows, more_rows, heads, outs, w_out, w_zero, weight, both, done,
+    spot, own, far, side, corner, near, cross, out_mine, out_other, first, first_other,
+    zero_side, zero_corner, mod, mod_base, residue, keyval, query,
+    base_rows, more_rows, heads, outs, w_out, stacks, zeros, w_zero, weight, both, done,
 ):
     row, link, core = (spot[1], spot[2], spot[3])
     images, tokens, _ = own.shape
@@ -422,7 +413,9 @@
     copies += [(own, base_rows.at[0]), (side, base_rows.at[1])]
     copies += [(far, more_rows.at[0]), (corner, more_rows.at[1])]
     early = begin(copies, done)
-    late = begin([(zero_rows, w_zero), (projections, weight)], done, len(early))
+    copies = [(first, stacks.at[core]), (first_other, stacks.at[1 - core])]
+    copies += [(zero_side, zeros.at[core]), (zero_corner, zeros.at[1 - core])]
+    late = begin(copies, done, len(early))
     finish(early)
     for at in range(2):
         arrange_heads(link, outs.at[at], at * width, w_out)
@@ -439,12 +432,23 @@
     base = flat(base_rows)
     out = (base + flat(more_rows) + mod[2] * projected).astype(jnp.bfloat16)
     finish(late)
+    shard = w_zero.shape[0] // 8
+    kept = shard - SHARED
+    for at in range(2):
+        for step in range(4):
+            start = (2 * (link ^ ORDER[step]) + at) * shard
+            w_zero[rows_at(start + row * SHARED, kept), :] = stacks[at, step, SLOT : 2 * SLOT]
+            w_zero[rows_at(start + (1 - row) * kept, SHARED), :] = zeros[at, step]
+    arrange_keyvals(link, stacks, weight)
+    start = weight.shape[0] - 4 * SLOT
+    clear_rows(weight, 8 * SLOT, start)
+    arrange_heads(link, stacks.at[row, :, 2 * SLOT :], start, weight)
     residual = dot_rows(out, w_zero[...]).astype(jnp.bfloat16)
     base = base + residual.astype(jnp.float32)
     result = modulate(base, mod_base)
     for image in range(images):
         rows = slice(image * tokens, (image + 1) * tokens)
-        base_in[image] = base[rows]
+        residue[image] = residual[rows]
         both[image, row] = result[rows]
         both[image, 1 - row] = result[tile + image * tokens : tile + (image + 1) * tokens]
     rows = both[...].reshape(2 * tile, both.shape[3])
@@ -453,16 +457,15 @@
     query[...] = projected[:, keyval.shape[1] :]
 
 
-def final_kernel(spot, attended, side, mine, other, base, mod, out, near, far, outs, w_out, done):
-    row, link = (spot[1], spot[2])
+def final_kernel(
+    spot, attended, side, head_rows, own, more, mod, out, near, far, w_out, first, second, done
+):
+    row = spot[1]
     images = out.shape[0]
     width = near.shape[2]
-    copies = [(side, far)]
+    copies = [(head_rows, w_out), (own, first), (more, second), (side, far)]
     copies += [(attended.at[image, row], near.at[image]) for image in range(images)]
-    copies += [(mine, outs.at[1 - row]), (other, outs.at[row])]
     finish(begin(copies, done))
-    for at in range(2):
-        arrange_heads(link, outs.at[at], at * width, w_out)
 
     def flat(ref):
         return jnp.concatenate([ref[i] for i in range(images)], axis=0)
@@ -476,7 +479,8 @@
     tokens = out.shape[1]
     for image in range(images):
         rows = slice(image * tokens, (image + 1) * tokens)
-        out[image] = (base[image] + mod[2] * projected[rows]).astype(out.dtype)
+        base = first[image].astype(jnp.float32) + second[image].astype(jnp.float32)
+        out[image] = (base + mod[2] * projected[rows]).astype(out.dtype)
 
 
 def paired_rows(sizes, latent, modulation, w_query, w_keyval, w_out, w_zero):
@@ -526,58 +530,64 @@
     def joined(block, other):
         return jnp.concatenate([block, other], axis=0)
 
+    def unset(*outs):
+        return tuple(kernel_call(unset_kernel, [out], (spot,), copies=1, stay=True)[0] for out in outs)
+
+    tile_shape = (images, tile, D)
+    head_shape = ((images, 2, tile, half), jnp.bfloat16)
+    half_head_shape = ((images, tile, half), jnp.bfloat16)
+    stack_shape = ((4, SLOT, D), jnp.bfloat16)
+    shared_shape = ((4, SHARED, D), jnp.bfloat16)
+    rows_shape = ((2 * half, D), jnp.bfloat16)
+    projections = [((tokens, 2 * half), jnp.bfloat16), ((tokens, lanes), jnp.bfloat16)]
+    shard = w_zero.shape[1]
+    triple_shape = ((4, 3 * SLOT, D), jnp.bfloat16)
+    stacks = ((2,) + triple_shape[0], jnp.bfloat16)
+    shared_stacks = ((2, 4, SHARED, D), jnp.bfloat16)
+    half_stacks = ((2, 4, SLOT, D), jnp.bfloat16)
+    both_shape = ((images, 2, tile, D), jnp.bfloat16)
+
     keyval_piece = padded_rows(lax.dynamic_slice_in_dim(w_keyval[0].T, row * HD, HD, axis=0))
-    zero_piece = lax.dynamic_slice_in_dim(
-        w_zero.T, row * (w_zero.shape[1] - SLOT), SLOT, axis=0
-    )
+    zero_piece = lax.dynamic_slice_in_dim(w_zero.T, row * SHARED, shard - SHARED, axis=0)
     query_or_out = padded_rows(jnp.where(is_query, w_query[0].T, w_out[0]))
 
-    piece = joined(jnp.where(is_control, keyval_piece, zero_piece), query_or_out)
+    out_piece = padded_rows(w_out[0])
+    piece = jnp.concatenate(
+        [
+            keyval_piece,
+            jnp.where(is_control, query_or_out, zero_piece),
+            jnp.where(is_control, out_piece, query_or_out),
+        ],
+        axis=0,
+    )
     first = [piece, swap_links(piece, ORDER[1]), swap_links(piece, ORDER[2])]
     started = after(own, piece)
     far = send(started, sizes, lambda b, r, t: (1 - b, r, t))
     corner = send(started, sizes, lambda b, r, t: (0, 1 - r, t) if b == 1 else None)
-    tile_shape = (images, tile, D)
-    normed, bias, hidden = kernel_call(
-        functools.partial(norm_kernel, 2 * tile_rows, sizes[2] * tile_cols),
-        [
-            (tile_shape, jnp.bfloat16),
-            ((2 * tile, 6 * tile), jnp.float32),
-            (tile_shape, jnp.float32),
-        ],
-        (spot, own, far, modulation[1]),
-        scratch=[(tile_shape, jnp.bfloat16), (tile_shape, jnp.bfloat16)],
-        copies=2,
+    (normed,) = kernel_call(
+        norm_kernel, [(tile_shape, jnp.bfloat16)], (spot, own, far, modulation[1]),
+        scratch=[(tile_shape, jnp.bfloat16), (tile_shape, jnp.bfloat16)], copies=2,
     )
     side = swap_rows(jnp.where(is_control, normed, own))
     side, corner, *first = lax.optimization_barrier((side, corner, *first))
     first.append(swap_links(first[1], ORDER[2]))
     first = stacked(first)
     first_other = swap_cores(first)
-    zero_side = swap_rows(first[:, :SLOT], base_only)
-    head_stack = jnp.where(is_query, first_other[:, SLOT:], first[:, SLOT:])
-
-    def to_base(b, r, t):
-        if b == 0:
-            return None
-        return (0, 1 - r, t ^ 1) if t % 2 == r else (0, r, t)
-
-    out_mine = send(head_stack, sizes, to_base)
-    projections = [((tokens, 2 * half), jnp.bfloat16), ((tokens, lanes), jnp.bfloat16)]
-    stacks = ((2, 4, 2 * SLOT, D), jnp.bfloat16)
-    half_stacks = ((2, 4, SLOT, D), jnp.bfloat16)
-    projection_scratch = [
-        ((2 * half + lanes, D), jnp.bfloat16),
-        ((images, 2, tile, D), jnp.bfloat16),
-    ]
-
-    def neighborhood(keyval, query, joins):
+    head_stack = jnp.where(is_query, first[:, 2 * SLOT :], first[:, SLOT : 2 * SLOT])
+    out_mine = send(head_stack, sizes, lambda b, r, t: (0, r, t) if b == 1 else None)
+
+    def halos(keyval, joins):
         def across(b, r, t):
             target = t + 1 if t % 2 else t - 1
             return (b, r, target) if joins(b, r, t) and 0 <= target < sizes[2] else None
 
-        outer = send(keyval, sizes, across)
-        inner = swap_cores(keyval, joins)
+        return send(keyval, sizes, across), swap_cores(keyval, joins)
+
+    def neighborhood(query, keyval, outer, inner):
+        (bias,) = kernel_call(
+            functools.partial(bias_kernel, 2 * tile_rows, sizes[2] * tile_cols),
+            [((2 * tile, 6 * tile), jnp.float32)], (spot,), copies=1,
+        )
         (attended,) = kernel_call(
             attend_kernel, [((tokens, half), jnp.bfloat16)],
             (spot, query, outer, keyval, inner, bias),
@@ -586,89 +596,95 @@
         )
         return attended.reshape(images, 2, tile, half)
 
-    def finished(attended, other_stack, base, mod, joins):
+    def their_heads(attended, joins):
         theirs = lax.dynamic_index_in_dim(attended, 1 - row, 1, keepdims=False)
+        return swap_rows(theirs, joins)
+
+    def head_rows(index, mine, other):
+        (rows,) = kernel_call(
+            functools.partial(head_rows_kernel, index), [rows_shape], (spot, mine, other),
+            scratch=[half_stacks], copies=2,
+        )
+        return rows
+
+    def finished(attended, side_heads, rows, more, mod):
         (out,) = kernel_call(
             final_kernel, [(tile_shape, jnp.bfloat16)],
-            (spot, attended, swap_rows(theirs, joins), head_stack, other_stack, base, mod),
-            scratch=[
-                ((images, tile, half), jnp.bfloat16),
-                ((images, tile, half), jnp.bfloat16),
-                half_stacks,
-                ((2 * half, D), jnp.bfloat16),
-            ],
-            copies=3 + images,
+            (spot, attended, side_heads, rows, own, more, mod),
+            scratch=[half_head_shape, half_head_shape, rows_shape]
+            + [(tile_shape, jnp.bfloat16), (tile_shape, jnp.bfloat16)],
+            copies=4 + images,
         )
         return out
-
-    def empty(*outs):
-        return tuple(jnp.zeros(shape, kind) for shape, kind in outs)
-
-    head_shape = ((images, 2, tile, half), jnp.bfloat16)
-    stack_shape = ((4, SLOT, D), jnp.bfloat16)
-    piece_shape = ((SLOT, D), jnp.bfloat16)
 
     def control_attention():
         keyval, query = kernel_call(
             project_kernel, projections, (spot, normed, side, first, first_other),
-            scratch=[stacks] + projection_scratch, copies=2 + 2 * images, micros=5,
-        )
-        return (neighborhood(keyval, query, control_only),) + empty(piece_shape, piece_shape)
-
-    def base_weights():
-        one = swap_links(keyval_piece, ORDER[1], base_only)
-        two = swap_links(keyval_piece, ORDER[2], base_only)
-        return empty(head_shape) + (one, two)
-
-    attended, one, two = lax.cond(is_control, control_attention, base_weights)
+            scratch=[stacks, ((2 * half + lanes, D), jnp.bfloat16), both_shape],
+            copies=2 + 2 * images, micros=5,
+        )
+        attended = neighborhood(query, keyval, *halos(keyval, control_only))
+        return attended
+
+    attended = lax.cond(is_control, control_attention, lambda: unset(head_shape)[0])
     near = send(attended, sizes, lambda b, r, t: (0, r, t) if b == 1 else None)
     cross = send(attended, sizes, lambda b, r, t: (0, 1 - r, t) if b == 1 else None)
-    prepared = [((D, D), jnp.bfloat16), ((2 * half + lanes, D), jnp.bfloat16), stack_shape]
+
+    def base_exchange():
+        shared = lax.dynamic_slice_in_dim(
+            after(first, attended), SLOT + row * (SLOT - SHARED), SHARED, axis=1
+        )
+        third = jnp.where(
+            is_query, first_other[:, 2 * SLOT :], after(first, attended)[:, 2 * SLOT :]
+        )
+        return swap_rows(shared, base_only), third
+
+    zero_side, third = lax.cond(
+        is_control, lambda: unset(shared_shape, stack_shape), base_exchange
+    )
 
     def control_finish():
-        other = swap_rows(head_stack, control_only)
-        out = finished(after(attended, other), other, hidden, modulation[1], control_only)
-        return empty(*prepared) + (out,)
+        rows = head_rows(3, swap_cores(head_stack, control_only), head_stack)
+        side_heads = their_heads(attended, control_only)
+        out = finished(attended, side_heads, rows, far, modulation[1])
+        return unset(shared_shape, stack_shape) + (out,)
 
     def base_prepare():
-        three = swap_links(one, ORDER[2], base_only)
-        out_other = swap_cores(after(out_mine, three), base_only)
-        zero_corner = swap_cores(after(zero_side, out_other), base_only)
-        second = stacked([keyval_piece, one, two, three])
-        second_other = swap_cores(after(second, zero_corner), base_only)
-        zero_rows, projection_rows = kernel_call(
-            prepare_kernel, prepared[:2],
-            (spot, first, first_other, zero_side, zero_corner, second, second_other),
-            scratch=[stacks, half_stacks, half_stacks], copies=6,
-        )
-        return (zero_rows, projection_rows, out_other) + empty((tile_shape, jnp.bfloat16))
-
-    zero_rows, projection_rows, out_other, control = lax.cond(
+        zero_corner = swap_cores(zero_side, base_only)
+        out_other = swap_cores(out_mine, base_only)
+        return (zero_corner, out_other) + unset((tile_shape, jnp.bfloat16))
+
+    zero_corner, out_other, control = lax.cond(
         is_control, control_finish, base_prepare
     )
 
     def base_finish():
-        other = swap_rows(head_stack, base_only)
-        base_in, keyval, query = kernel_call(
+        other = swap_rows(third, base_only)
+        residue, keyval, query = kernel_call(
             middle_kernel,
-            [(tile_shape, jnp.float32)] + projections,
+            [(tile_shape, jnp.bfloat16)] + projections,
             (
-                spot, own, far, side, corner, near, cross, out_mine, out_other, zero_rows,
-                projection_rows, modulation[1], modulation[0],
+                spot, own, far, side, corner, near, cross, out_mine, out_other, first, first_other,
+                zero_side, zero_corner, modulation[1], modulation[0],
             ),
             scratch=[
                 ((2, images, tile, D), jnp.bfloat16),
                 ((2, images, tile, D), jnp.bfloat16),
                 ((2, 2 * images * tile, half), jnp.bfloat16),
                 half_stacks,
-                ((2 * half, D), jnp.bfloat16),
+                rows_shape,
+                stacks,
+                shared_stacks,
                 ((D, D), jnp.bfloat16),
-            ]
-            + projection_scratch,
-            copies=4 * images + 8, micros=8,
-        )
-        attended = neighborhood(keyval, query, base_only)
-        return finished(attended, other, base_in, modulation[0], base_only)
+                ((2 * half + lanes, D), jnp.bfloat16),
+                both_shape,
+            ],
+            copies=4 * images + 10, micros=8,
+        )
+        outer, inner = halos(keyval, base_only)
+        attended = neighborhood(query, keyval, outer, inner)
+        side_heads = their_heads(attended, base_only)
+        return finished(attended, side_heads, head_rows(1, third, other), residue, modulation[0])
 
     out = lax.cond(is_control, lambda: control, base_finish)
     return out.reshape(latent.shape)

time: 119 us -> 113 us (0.950)
  starting transfers between devices: 47.1 us -> 31 us
  waiting for transfers between devices: 45 us -> 54.7 us
  other arithmetic: 3.97 us -> 5.75 us
    ppermute x21 -> x17, starting transfers between devices: 47.1 us -> 31 us  [send(): return lax.ppermute(block, AXES, routes(sizes, move))]
    ppermute x21 -> x17, waiting for transfers between devices: 45 us -> 54.7 us  [send(): return lax.ppermute(block, AXES, routes(sizes, move))]
    select_n x0 -> x3, other arithmetic: none -> 4.64 us  [the longest x1 2.31 us: paired_rows(): jnp.where(is_query, first[:, 2 * SLOT:], first[:, SLOT:2 * SLOT])]
    pad x1 -> x0, other arithmetic: 1.65 us -> none  [padded_rows(): return jnp.pad(block, ((0, SLOT - HD), (0, 0)))]
    slice x1 -> x0, other arithmetic: 1.24 us -> none  [paired_rows(): zero_side = swap_rows(first[:, :SLOT], base_only)]
    pallas_call x7 -> x9, Pallas kernels: 17 us -> 17.3 us  [kernel_call(): pl.pallas_call(body, out_shape=[jax.ShapeDtypeStruct(shape, kind) for sha...]
  transfers between devices with their start and end apart: 21 -> 17, of which waited for: 13 -> 10; matrix products, arithmetic and copies ran while one was open for 1% -> 4% of each run, Pallas kernels for 12% -> 12%
where the time goes in v2:
time: 113 us; the launch traced here: 112 us
  waiting for transfers between devices  54.7 us (48%)
  starting transfers between devices  31 us (27%)
  Pallas kernels  17.3 us (15%)
  other arithmetic  5.75 us (5%)
  local copies, waits for them, and re-layouts  3.14 us (3%)
    ppermute x17, waiting for transfers between devices, send(): return lax.ppermute(block, AXES, routes(sizes, move))  54.7 us
    ppermute x17, starting transfers between devices, send(): return lax.ppermute(block, AXES, routes(sizes, move))  31 us
    pallas_call x9, Pallas kernels, kernel_call(): pl.pallas_call(body, out_shape=[jax.ShapeDtypeStruct(shape, kind) for sha...  17.3 us
    select_n x1, other arithmetic, paired_rows(): jnp.where(is_query, first[:, 2 * SLOT:], first[:, SLOT:2 * SLOT])  2.31 us
  transfers between devices with their start and end apart: 17, of which 10 were waited for; matrix products, arithmetic and copies ran while one was open for 4% of the time, Pallas kernels for 12%

profile of v2, /device:TPU:1, one launch (start us, length us, event | category | flops | bytes accessed | tf_op | source)
XLA Modules:
  0.0 112.3 jit_solution(15240010204088884663)
XLA Ops:
  3.2 2.1 %collective-permute-start.11 = (bf16[2,64,1152]{2,1,0:T(8,128)(2,1)S(1)}, bf16[2,64,1152]{2,1,0:T(8,128)(2,1)S(1)}, u32[]{:S(2)}, u32[]{:S(2)}) collective-permute-start(bf16[2,64,1152]{2,1,0:T(8,128)(2,1)S(1)} %bitcast.39), channel_id=1, source_target_pairs={{0,16},{1,17},{2,18},{3,19},{4,20},{5,21},{6,22},{7,23},{8,24},{9,... | collective-permute-start | bytes 884744 | tf_op jit(solution)/shard_map/ppermute | solution.py:225
  5.3 3.3 %collective-permute-start.14 = (bf16[240,1152]{1,0:T(8,128)(2,1)S(1)}, bf16[240,1152]{1,0:T(8,128)(2,1)S(1)}, u32[]{:S(2)}, u32[]{:S(2)}) collective-permute-start(bf16[240,1152]{1,0:T(8,128)(2,1)S(1)} %fusion.2.refs_0_), channel_id=1, source_target_pairs={{0,6},{1,7},{2,4},{3,5},{4,2},{5,3},{6,0},{7,1},{8,14},{9,15},{10,... | collective-permute-start | bytes 1658888 | tf_op jit(solution)/shard_map/ppermute | solution.py:225
  8.6 1.3 %collective-permute-start.13 = (bf16[2,64,1152]{2,1,0:T(8,128)(2,1)S(1)}, bf16[2,64,1152]{2,1,0:T(8,128)(2,1)S(1)}, u32[]{:S(2)}, u32[]{:S(2)}) collective-permute-start(bf16[2,64,1152]{2,1,0:T(8,128)(2,1)S(1)} %bitcast.40), channel_id=1, source_target_pairs={{16,8},{17,9},{18,10},{19,11},{20,12},{21,13},{22,14},{23,15},{24,... | collective-permute-start | bytes 884744 | tf_op jit(solution)/shard_map/ppermute | solution.py:225
  10.1 2.0 %collective-permute-done.11.far = bf16[2,64,1152]{2,1,0:T(8,128)(2,1)S(1)} collective-permute-done((bf16[2,64,1152]{2,1,0:T(8,128)(2,1)S(1)}, bf16[2,64,1152]{2,1,0:T(8,128)(2,1)S(1)}, u32[]{:S(2)}, u32[]{:S(2)}) %collective-permute-start.11) | collective-permute-done | bytes 294944 | tf_op jit(solution)/shard_map/ppermute | solution.py:225
  14.2 4.4 %collective-permute-done.13 = bf16[2,64,1152]{2,1,0:T(8,128)(2,1)S(1)} collective-permute-done((bf16[2,64,1152]{2,1,0:T(8,128)(2,1)S(1)}, bf16[2,64,1152]{2,1,0:T(8,128)(2,1)S(1)}, u32[]{:S(2)}, u32[]{:S(2)}) %collective-permute-start.13) | collective-permute-done | bytes 294944 | tf_op jit(solution)/shard_map/ppermute | solution.py:225
  18.7 1.8 %collective-permute-done.14.refs_1_ = bf16[240,1152]{1,0:T(8,128)(2,1)S(1)} collective-permute-done((bf16[240,1152]{1,0:T(8,128)(2,1)S(1)}, bf16[240,1152]{1,0:T(8,128)(2,1)S(1)}, u32[]{:S(2)}, u32[]{:S(2)}) %collective-permute-start.14) | collective-permute-done | bytes 552992 | tf_op jit(solution)/shard_map/ppermute | solution.py:225
  20.5 13.1 %collective-permute-done.15.refs_2_ = bf16[240,1152]{1,0:T(8,128)(2,1)S(1)} collective-permute-done((bf16[240,1152]{1,0:T(8,128)(2,1)S(1)}, bf16[240,1152]{1,0:T(8,128)(2,1)S(1)}, u32[]{:S(2)}, u32[]{:S(2)}) %collective-permute-start.15) | collective-permute-done | bytes 552992 | tf_op jit(solution)/shard_map/ppermute | solution.py:225
  33.7 13.5 %collective-permute-done.16.refs_3_ = bf16[240,1152]{1,0:T(8,128)(2,1)S(1)} collective-permute-done((bf16[240,1152]{1,0:T(8,128)(2,1)S(1)}, bf16[240,1152]{1,0:T(8,128)(2,1)S(1)}, u32[]{:S(2)}, u32[]{:S(2)}) %collective-permute-start.16) | collective-permute-done | bytes 552992 | tf_op jit(solution)/shard_map/ppermute | solution.py:225
  47.2 1.4 %shard_map.67 = bf16[4,240,1152]{2,1,0:T(8,128)(2,1)} custom-call(bf16[240,1152]{1,0:T(8,128)(2,1)S(1)} %fusion.2.refs_0_, bf16[240,1152]{1,0:T(8,128)(2,1)S(1)} %collective-permute-done.14.refs_1_, bf16[240,1152]{1,0:T(8,128)(2,1)S(1)} %collective-permute-done.15.refs_2_, bf16[240,1152]{1,0:T(8,128)(2,1)S(1)} %collective-permute-done.16.refs_3_), custom_call_target="tpu_custom_call" | custom-call | bytes 1 | tf_op jit(solution)/shard_map/pallas_call | solution.py:239
  48.6 1.4 %collective-permute-start.17 = (bf16[4,240,1152]{2,1,0:T(8,128)(2,1)}, bf16[4,240,1152]{2,1,0:T(8,128)(2,1)S(1)}, u32[]{:S(2)}, u32[]{:S(2)}) collective-permute-start(bf16[4,240,1152]{2,1,0:T(8,128)(2,1)} %shard_map.67), channel_id=1, source_target_pairs={{0,1},{1,0},{2,3},{3,2},{4,5},{5,4},{6,7},{7,6},{8,9},{9,8},{10,11... | collective-permute-start | bytes 6635528 | tf_op jit(solution)/shard_map/ppermute | solution.py:225
  50.0 2.3 %slice_select_fusion.1 = bf16[4,80,1152]{2,1,0:T(8,128)(2,1)} fusion(bf16[4,240,1152]{2,1,0:T(8,128)(2,1)} %shard_map.67, pred[]{:T(512)} %eq.9), kind=kLoop, calls=%fused_computation.9 | loop fusion | flops 368640 | bytes 2211841 | tf_op jit(solution)/shard_map/jit(_where)/select_n | solution.py:576
  52.3 1.3 %collective-permute-start.20 = (bf16[4,80,1152]{2,1,0:T(8,128)(2,1)}, bf16[4,80,1152]{2,1,0:T(8,128)(2,1)}, u32[]{:S(2)}, u32[]{:S(2)}) collective-permute-start(bf16[4,80,1152]{2,1,0:T(8,128)(2,1)} %slice_select_fusion.1), channel_id=1, source_target_pairs={{16,0},{17,1},{18,2},{19,3},{20,4},{21,5},{22,6},{23,7},{24,8},{25... | collective-permute-start | bytes 2211848 | tf_op jit(solution)/shard_map/ppermute | solution.py:225
  54.8 1.3 %collective-permute-start.18 = (bf16[2,2,64,320]{3,2,1,0:T(8,128)(2,1)}, bf16[2,2,64,320]{3,2,1,0:T(8,128)(2,1)S(1)}, u32[]{:S(2)}, u32[]{:S(2)}) collective-permute-start(bf16[2,2,64,320]{3,2,1,0:T(8,128)(2,1)} %get-tuple-element.190), channel_id=1, source_target_pairs={{16,0},{17,1},{18,2},{19,3},{20,4},{21,5},{22,6},{23,7},{24,8},{25... | collective-permute-start | bytes 491528 | tf_op jit(solution)/shard_map/ppermute | solution.py:225
  56.1 1.3 %collective-permute-start.19 = (bf16[2,2,64,320]{3,2,1,0:T(8,128)(2,1)}, bf16[2,2,64,320]{3,2,1,0:T(8,128)(2,1)}, u32[]{:S(2)}, u32[]{:S(2)}) collective-permute-start(bf16[2,2,64,320]{3,2,1,0:T(8,128)(2,1)} %get-tuple-element.190), channel_id=1, source_target_pairs={{16,8},{17,9},{18,10},{19,11},{20,12},{21,13},{22,14},{23,15},{24,... | collective-permute-start | bytes 491528 | tf_op jit(solution)/shard_map/ppermute | solution.py:225
  57.4 17.7 %conditional.5 = (bf16[4,64,1152]{2,1,0:T(8,128)(2,1)}, bf16[4,80,1152]{2,1,0:T(8,128)(2,1)S(1)}) conditional(s32[]{:T(128)} %convert_element_type.10, (bf16[4,240,1152]{2,1,0:T(8,128)(2,1)}, s32[]{:T(128)}, pred[]{:T(512)}, bf16[4,240,1152]{2,1,0:T(8,128)(2,1)S(1)}) %tuple.45, s32[5]{0:T(128)S(1)} %stack.29.spot), branch_computations={%region_2.3_spmd, %region_3.4_spmd} | conditional | flops 368645 | bytes 5750903 | solution.py:642
  58.5 3.1 %collective-permute-start.4 = (bf16[4,64,1152]{2,1,0:T(8,128)(2,1)S(1)}, bf16[4,64,1152]{2,1,0:T(8,128)(2,1)}, u32[]{:S(2)}, u32[]{:S(2)}) collective-permute-start(bf16[4,64,1152]{2,1,0:T(8,128)(2,1)S(1)} %constant_dynamic-slice_fusion), channel_id=1, source_target_pairs={{0,8},{1,9},{2,10},{3,11},{4,12},{5,13},{6,14},{7,15},{8,0},{9,1},... | collective-permute-start | bytes 1769480 | tf_op jit(solution)/shard_map/cond/branch_0_fun/ppermute | solution.py:225
  62.9 12.2 %collective-permute-done.4 = bf16[4,64,1152]{2,1,0:T(8,128)(2,1)} collective-permute-done((bf16[4,64,1152]{2,1,0:T(8,128)(2,1)S(1)}, bf16[4,64,1152]{2,1,0:T(8,128)(2,1)}, u32[]{:S(2)}, u32[]{:S(2)}) %collective-permute-start.4) | collective-permute-done | bytes 589856 | tf_op jit(solution)/shard_map/cond/branch_0_fun/ppermute | solution.py:225
  75.9 7.2 %conditional.6 = (bf16[4,64,1152]{2,1,0:T(8,128)(2,1)S(1)}, bf16[4,80,1152]{2,1,0:T(8,128)(2,1)S(1)}, bf16[2,64,1152]{2,1,0:T(8,128)(2,1)}) conditional(s32[]{:T(128)} %convert_element_type.10, (bf16[4,64,1152]{2,1,0:T(8,128)(2,1)}, bf16[4,80,1152]{2,1,0:T(8,128)(2,1)}, s32[5]{0:T(128)S(1)}) %tuple.46, (s32[5]{0:T(128)S(1)}, s32[]{:T(128)}, ...), branch_computations={%region_4.5_spmd, %region_5.6_spmd} | conditional | flops 4 | bytes 5308521 | solution.py:657
  75.9 3.1 %collective-permute-start.3 = (bf16[4,80,1152]{2,1,0:T(8,128)(2,1)}, bf16[4,80,1152]{2,1,0:T(8,128)(2,1)S(1)}, u32[]{:S(2)}, u32[]{:S(2)}) collective-permute-start(bf16[4,80,1152]{2,1,0:T(8,128)(2,1)} %get-tuple-element.100), channel_id=1, source_target_pairs={{0,1},{1,0},{2,3},{3,2},{4,5},{5,4},{6,7},{7,6},{8,9},{9,8},{10,11... | collective-permute-start | bytes 2211848 | tf_op jit(solution)/shard_map/cond/branch_0_fun/ppermute | solution.py:225
  79.0 1.9 %collective-permute-start.2 = (bf16[4,64,1152]{2,1,0:T(8,128)(2,1)}, bf16[4,64,1152]{2,1,0:T(8,128)(2,1)S(1)}, u32[]{:S(2)}, u32[]{:S(2)}) collective-permute-start(bf16[4,64,1152]{2,1,0:T(8,128)(2,1)} %get-tuple-element.99), channel_id=1, source_target_pairs={{0,1},{1,0},{2,3},{3,2},{4,5},{5,4},{6,7},{7,6},{8,9},{9,8},{10,11... | collective-permute-start | bytes 1769480 | tf_op jit(solution)/shard_map/cond/branch_0_fun/ppermute | solution.py:225
  81.5 1.6 %collective-permute-done.2 = bf16[4,64,1152]{2,1,0:T(8,128)(2,1)S(1)} collective-permute-done((bf16[4,64,1152]{2,1,0:T(8,128)(2,1)}, bf16[4,64,1152]{2,1,0:T(8,128)(2,1)S(1)}, u32[]{:S(2)}, u32[]{:S(2)}) %collective-permute-start.2) | collective-permute-done | bytes 589856 | tf_op jit(solution)/shard_map/cond/branch_0_fun/ppermute | solution.py:225
  83.2 29.2 %conditional.7 = (bf16[1,2,8,8,1152]{4,3,2,1,0:T(8,128)(2,1)}) conditional(s32[]{:T(128)} %convert_element_type.10, (f32[2,3,1152]{2,0,1:T(2,128)S(1)}, s32[5]{0:T(128)S(1)}, bf16[2,64,1152]{2,1,0:T(8,128)(2,1)S(1)}, bf16[2,64,1152]{2,1,0:T(8,128)(2,1)S(1)}, bf16[2,64,1152]{2,1,0:T(8,128)(2,1)}, /*index=5*/bf16[2,64,1152]{2,1,0:T(8,128)(2,1)}, ...), branch_computations={%region_6.7_spmd, %region_7.8_spmd} | conditional | flops 4 | bytes 70681360 | solution.py:689
  83.2 3.1 %collective-permute-start.10 = (bf16[4,80,1152]{2,1,0:T(8,128)(2,1)}, bf16[4,80,1152]{2,1,0:T(8,128)(2,1)S(1)}, u32[]{:S(2)}, u32[]{:S(2)}) collective-permute-start(bf16[4,80,1152]{2,1,0:T(8,128)(2,1)} %get-tuple-element.126.mine), channel_id=1, source_target_pairs={{0,8},{1,9},{2,10},{3,11},{4,12},{5,13},{6,14},{7,15},{8,0},{9,1},... | collective-permute-start | bytes 2211848 | tf_op jit(solution)/shard_map/cond/branch_0_fun/ppermute | solution.py:225
  86.4 6.7 %branch_0_fun.9 = (bf16[2,64,1152]{2,1,0:T(8,128)(2,1)S(1)}, bf16[256,640]{1,0:T(8,128)(2,1)S(1)}, bf16[256,384]{1,0:T(8,128)(2,1)S(1)}) custom-call(s32[5]{0:T(128)S(1)} %get-tuple-element.109.spot, bf16[2,64,1152]{2,1,0:T(8,128)(2,1)S(1)} %get-tuple-element.110.own, bf16[2,64,1152]{2,1,0:T(8,128)(2,1)S(1)} %get-tuple-element.111.far, ...), custom_call_target="tpu_custom_call" | custom-call | bytes 29600000 | tf_op jit(solution)/shard_map/cond/branch_0_fun/pallas_call | solution.py:239
  93.1 2.4 %collective-permute-start.7 = (bf16[256,640]{1,0:T(8,128)(2,1)S(1)}, bf16[256,640]{1,0:T(8,128)(2,1)S(1)}, u32[]{:S(2)}, u32[]{:S(2)}) collective-permute-start(bf16[256,640]{1,0:T(8,128)(2,1)S(1)} %get-tuple-element.124.here), channel_id=1, source_target_pairs={{1,2},{2,1},{3,4},{4,3},{5,6},{6,5},{9,10},{10,9},{11,12},{12,11},... | collective-permute-start | bytes 983048 | tf_op jit(solution)/shard_map/cond/branch_0_fun/ppermute | solution.py:225
  95.6 1.9 %collective-permute-start.8 = (bf16[256,640]{1,0:T(8,128)(2,1)S(1)}, bf16[256,640]{1,0:T(8,128)(2,1)S(1)}, u32[]{:S(2)}, u32[]{:S(2)}) collective-permute-start(bf16[256,640]{1,0:T(8,128)(2,1)S(1)} %get-tuple-element.124.here), channel_id=1, source_target_pairs={{0,1},{1,0},{2,3},{3,2},{4,5},{5,4},{6,7},{7,6},{8,9},{9,8},{10,11... | collective-permute-start | bytes 983048 | tf_op jit(solution)/shard_map/cond/branch_0_fun/ppermute | solution.py:225
  98.2 3.7 %collective-permute-done.7.outer = bf16[256,640]{1,0:T(8,128)(2,1)S(1)} collective-permute-done((bf16[256,640]{1,0:T(8,128)(2,1)S(1)}, bf16[256,640]{1,0:T(8,128)(2,1)S(1)}, u32[]{:S(2)}, u32[]{:S(2)}) %collective-permute-start.7) | collective-permute-done | bytes 327712 | tf_op jit(solution)/shard_map/cond/branch_0_fun/ppermute | solution.py:225
  101.8 2.6 %branch_0_fun.11 = bf16[256,320]{1,0:T(8,128)(2,1)S(1)} custom-call(s32[5]{0:T(128)S(1)} %get-tuple-element.109.spot, bf16[256,384]{1,0:T(8,128)(2,1)S(1)} %get-tuple-element.123.queries, bf16[256,640]{1,0:T(8,128)(2,1)S(1)} %collective-permute-done.7.outer, bf16[256,640]{1,0:T(8,128)(2,1)S(1)} %get-tuple-element.124.here, ...), custom_call_target="tpu_custom_call" | custom-call | bytes 29600000 | tf_op jit(solution)/shard_map/cond/branch_0_fun/pallas_call | solution.py:239
  104.5 2.2 %collective-permute-start.9 = (bf16[2,64,320]{2,1,0:T(8,128)(2,1)S(1)}, bf16[2,64,320]{2,1,0:T(8,128)(2,1)S(1)}, u32[]{:S(2)}, u32[]{:S(2)}) collective-permute-start(bf16[2,64,320]{2,1,0:T(8,128)(2,1)S(1)} %dynamic-slice_bitcast_fusion.1), channel_id=1, source_target_pairs={{0,8},{1,9},{2,10},{3,11},{4,12},{5,13},{6,14},{7,15},{8,0},{9,1},... | collective-permute-start | bytes 245768 | tf_op jit(solution)/shard_map/cond/branch_0_fun/ppermute | solution.py:225
  106.7 1.3 %branch_0_fun.12.head_rows = bf16[640,1152]{1,0:T(8,128)(2,1)S(1)} custom-call(s32[5]{0:T(128)S(1)} %get-tuple-element.109.spot, bf16[4,80,1152]{2,1,0:T(8,128)(2,1)S(1)} %copy-done.4, bf16[4,80,1152]{2,1,0:T(8,128)(2,1)S(1)} %collective-permute-done.10.other), custom_call_target="tpu_custom_call" | custom-call | bytes 1 | tf_op jit(solution)/shard_map/cond/branch_0_fun/pallas_call | solution.py:239
  108.0 1.8 %collective-permute-done.9.side = bf16[2,64,320]{2,1,0:T(8,128)(2,1)S(1)} collective-permute-done((bf16[2,64,320]{2,1,0:T(8,128)(2,1)S(1)}, bf16[2,64,320]{2,1,0:T(8,128)(2,1)S(1)}, u32[]{:S(2)}, u32[]{:S(2)}) %collective-permute-start.9) | collective-permute-done | bytes 81952 | tf_op jit(solution)/shard_map/cond/branch_0_fun/ppermute | solution.py:225
  109.8 2.5 %branch_0_fun.13 = bf16[2,64,1152]{2,1,0:T(8,128)(2,1)} custom-call(s32[5]{0:T(128)S(1)} %get-tuple-element.109.spot, bf16[2,2,64,320]{3,2,1,0:T(8,128)(2,1)S(1)} %bitcast.37, bf16[2,64,320]{2,1,0:T(8,128)(2,1)S(1)} %collective-permute-done.9.side, bf16[640,1152]{1,0:T(8,128)(2,1)S(1)} %branch_0_fun.12.head_rows, ...), custom_call_target="tpu_custom_call" | custom-call | bytes 1 | tf_op jit(solution)/shard_map/cond/branch_0_fun/pallas_call | solution.py:239
  (47 shorter events, 11.7 us)
Async XLA Ops:
  0.0 1.0 copy-start
  0.0 3.2 %copy-start.2 = (bf16[1,2,8,8,1152]{4,3,2,1,0:T(8,128)(2,1)S(1)}, bf16[1,2,8,8,1152]{4,3,2,1,0:T(8,128)(2,1)}, u32[]{:S(2)}) copy-start(bf16[1,2,8,8,1152]{4,3,2,1,0:T(8,128)(2,1)} %param.14) | copy-start | bytes 884740
  0.0 9.9 %copy-start.8 = (f32[2,3,1152]{2,0,1:T(2,128)S(1)}, f32[2,3,1152]{2,0,1:T(2,128)}, u32[]{:S(2)}) copy-start(f32[2,3,1152]{2,0,1:T(2,128)} %param.15) | copy-start | bytes 82948
  3.2 8.9 %collective-permute-start.11 = (bf16[2,64,1152]{2,1,0:T(8,128)(2,1)S(1)}, bf16[2,64,1152]{2,1,0:T(8,128)(2,1)S(1)}, u32[]{:S(2)}, u32[]{:S(2)}) collective-permute-start(bf16[2,64,1152]{2,1,0:T(8,128)(2,1)S(1)} %bitcast.39), channel_id=1, source_target_pairs={{0,16},{1,17},{2,18},{3,19},{4,20},{5,21},{6,22},{7,23},{8,24},{9,... | collective-permute-start | bytes 884744 | tf_op jit(solution)/shard_map/ppermute | solution.py:225
  5.3 15.1 %collective-permute-start.14 = (bf16[240,1152]{1,0:T(8,128)(2,1)S(1)}, bf16[240,1152]{1,0:T(8,128)(2,1)S(1)}, u32[]{:S(2)}, u32[]{:S(2)}) collective-permute-start(bf16[240,1152]{1,0:T(8,128)(2,1)S(1)} %fusion.2.refs_0_), channel_id=1, source_target_pairs={{0,6},{1,7},{2,4},{3,5},{4,2},{5,3},{6,0},{7,1},{8,14},{9,15},{10,... | collective-permute-start | bytes 1658888 | tf_op jit(solution)/shard_map/ppermute | solution.py:225
  8.6 24.9 %collective-permute-start.15 = (bf16[240,1152]{1,0:T(8,128)(2,1)S(1)}, bf16[240,1152]{1,0:T(8,128)(2,1)S(1)}, u32[]{:S(2)}, u32[]{:S(2)}) collective-permute-start(bf16[240,1152]{1,0:T(8,128)(2,1)S(1)} %fusion.2.refs_0_), channel_id=1, source_target_pairs={{0,2},{1,3},{2,0},{3,1},{4,6},{5,7},{6,4},{7,5},{8,10},{9,11},{10,... | collective-permute-start | bytes 1658888 | tf_op jit(solution)/shard_map/ppermute | solution.py:225
  8.6 10.0 %collective-permute-start.13 = (bf16[2,64,1152]{2,1,0:T(8,128)(2,1)S(1)}, bf16[2,64,1152]{2,1,0:T(8,128)(2,1)S(1)}, u32[]{:S(2)}, u32[]{:S(2)}) collective-permute-start(bf16[2,64,1152]{2,1,0:T(8,128)(2,1)S(1)} %bitcast.40), channel_id=1, source_target_pairs={{16,8},{17,9},{18,10},{19,11},{20,12},{21,13},{22,14},{23,15},{24,... | collective-permute-start | bytes 884744 | tf_op jit(solution)/shard_map/ppermute | solution.py:225
  13.0 34.2 %copy-start.5 = (bf16[2,64,1152]{2,1,0:T(8,128)(2,1)}, bf16[2,64,1152]{2,1,0:T(8,128)(2,1)S(1)}, u32[]{:S(2)}) copy-start(bf16[2,64,1152]{2,1,0:T(8,128)(2,1)S(1)} %shard_map.66) | copy-start | bytes 884740
  13.1 20.5 %collective-permute-start.12 = (bf16[2,64,1152]{2,1,0:T(8,128)(2,1)S(1)}, bf16[2,64,1152]{2,1,0:T(8,128)(2,1)}, u32[]{:S(2)}, u32[]{:S(2)}) collective-permute-start(bf16[2,64,1152]{2,1,0:T(8,128)(2,1)S(1)} %broadcast_select_fusion), channel_id=1, source_target_pairs={{0,8},{1,9},{2,10},{3,11},{4,12},{5,13},{6,14},{7,15},{8,0},{9,1},... | collective-permute-start | bytes 884744 | tf_op jit(solution)/shard_map/ppermute | solution.py:225
  18.7 28.5 %copy-start.7 = (bf16[2,64,1152]{2,1,0:T(8,128)(2,1)}, bf16[2,64,1152]{2,1,0:T(8,128)(2,1)S(1)}, u32[]{:S(2)}) copy-start(bf16[2,64,1152]{2,1,0:T(8,128)(2,1)S(1)} %collective-permute-done.13) | copy-start | bytes 884740
  33.6 13.6 %collective-permute-start.16 = (bf16[240,1152]{1,0:T(8,128)(2,1)S(1)}, bf16[240,1152]{1,0:T(8,128)(2,1)S(1)}, u32[]{:S(2)}, u32[]{:S(2)}) collective-permute-start(bf16[240,1152]{1,0:T(8,128)(2,1)S(1)} %collective-permute-done.14.refs_1_), channel_id=1, source_target_pairs={{0,2},{1,3},{2,0},{3,1},{4,6},{5,7},{6,4},{7,5},{8,10},{9,11},{10,... | collective-permute-start | bytes 1658888 | tf_op jit(solution)/shard_map/ppermute | solution.py:225
  48.6 5.6 %collective-permute-start.17 = (bf16[4,240,1152]{2,1,0:T(8,128)(2,1)}, bf16[4,240,1152]{2,1,0:T(8,128)(2,1)S(1)}, u32[]{:S(2)}, u32[]{:S(2)}) collective-permute-start(bf16[4,240,1152]{2,1,0:T(8,128)(2,1)} %shard_map.67), channel_id=1, source_target_pairs={{0,1},{1,0},{2,3},{3,2},{4,5},{5,4},{6,7},{7,6},{8,9},{9,8},{10,11... | collective-permute-start | bytes 6635528 | tf_op jit(solution)/shard_map/ppermute | solution.py:225
  52.3 22.7 %collective-permute-start.20 = (bf16[4,80,1152]{2,1,0:T(8,128)(2,1)}, bf16[4,80,1152]{2,1,0:T(8,128)(2,1)}, u32[]{:S(2)}, u32[]{:S(2)}) collective-permute-start(bf16[4,80,1152]{2,1,0:T(8,128)(2,1)} %slice_select_fusion.1), channel_id=1, source_target_pairs={{16,0},{17,1},{18,2},{19,3},{20,4},{21,5},{22,6},{23,7},{24,8},{25... | collective-permute-start | bytes 2211848 | tf_op jit(solution)/shard_map/ppermute | solution.py:225
  54.2 3.2 %copy-start.1 = (bf16[4,240,1152]{2,1,0:T(8,128)(2,1)}, bf16[4,240,1152]{2,1,0:T(8,128)(2,1)S(1)}, u32[]{:S(2)}) copy-start(bf16[4,240,1152]{2,1,0:T(8,128)(2,1)S(1)} %collective-permute-done.17) | copy-start | bytes 6635524
  54.8 28.4 %collective-permute-start.18 = (bf16[2,2,64,320]{3,2,1,0:T(8,128)(2,1)}, bf16[2,2,64,320]{3,2,1,0:T(8,128)(2,1)S(1)}, u32[]{:S(2)}, u32[]{:S(2)}) collective-permute-start(bf16[2,2,64,320]{3,2,1,0:T(8,128)(2,1)} %get-tuple-element.190), channel_id=1, source_target_pairs={{16,0},{17,1},{18,2},{19,3},{20,4},{21,5},{22,6},{23,7},{24,8},{25... | collective-permute-start | bytes 491528 | tf_op jit(solution)/shard_map/ppermute | solution.py:225
  56.1 27.1 %collective-permute-start.19 = (bf16[2,2,64,320]{3,2,1,0:T(8,128)(2,1)}, bf16[2,2,64,320]{3,2,1,0:T(8,128)(2,1)}, u32[]{:S(2)}, u32[]{:S(2)}) collective-permute-start(bf16[2,2,64,320]{3,2,1,0:T(8,128)(2,1)} %get-tuple-element.190), channel_id=1, source_target_pairs={{16,8},{17,9},{18,10},{19,11},{20,12},{21,13},{22,14},{23,15},{24,... | collective-permute-start | bytes 491528 | tf_op jit(solution)/shard_map/ppermute | solution.py:225
  58.5 16.5 %collective-permute-start.4 = (bf16[4,64,1152]{2,1,0:T(8,128)(2,1)S(1)}, bf16[4,64,1152]{2,1,0:T(8,128)(2,1)}, u32[]{:S(2)}, u32[]{:S(2)}) collective-permute-start(bf16[4,64,1152]{2,1,0:T(8,128)(2,1)S(1)} %constant_dynamic-slice_fusion), channel_id=1, source_target_pairs={{0,8},{1,9},{2,10},{3,11},{4,12},{5,13},{6,14},{7,15},{8,0},{9,1},... | collective-permute-start | bytes 1769480 | tf_op jit(solution)/shard_map/cond/branch_0_fun/ppermute | solution.py:225
  75.0 0.9 copy-start.3
  75.9 7.2 %collective-permute-start.3 = (bf16[4,80,1152]{2,1,0:T(8,128)(2,1)}, bf16[4,80,1152]{2,1,0:T(8,128)(2,1)S(1)}, u32[]{:S(2)}, u32[]{:S(2)}) collective-permute-start(bf16[4,80,1152]{2,1,0:T(8,128)(2,1)} %get-tuple-element.100), channel_id=1, source_target_pairs={{0,1},{1,0},{2,3},{3,2},{4,5},{5,4},{6,7},{7,6},{8,9},{9,8},{10,11... | collective-permute-start | bytes 2211848 | tf_op jit(solution)/shard_map/cond/branch_0_fun/ppermute | solution.py:225
  79.0 4.1 %collective-permute-start.2 = (bf16[4,64,1152]{2,1,0:T(8,128)(2,1)}, bf16[4,64,1152]{2,1,0:T(8,128)(2,1)S(1)}, u32[]{:S(2)}, u32[]{:S(2)}) collective-permute-start(bf16[4,64,1152]{2,1,0:T(8,128)(2,1)} %get-tuple-element.99), channel_id=1, source_target_pairs={{0,1},{1,0},{2,3},{3,2},{4,5},{5,4},{6,7},{7,6},{8,9},{9,8},{10,11... | collective-permute-start | bytes 1769480 | tf_op jit(solution)/shard_map/cond/branch_0_fun/ppermute | solution.py:225
  83.2 3.1 %copy-start.6 = (bf16[4,64,1152]{2,1,0:T(8,128)(2,1)}, bf16[4,64,1152]{2,1,0:T(8,128)(2,1)S(1)}, u32[]{:S(2)}) copy-start(bf16[4,64,1152]{2,1,0:T(8,128)(2,1)S(1)} %get-tuple-element.121.zero_corner) | copy-start | bytes 1769476 | tf_op jit(solution)/shard_map/cond
  83.2 23.5 %collective-permute-start.10 = (bf16[4,80,1152]{2,1,0:T(8,128)(2,1)}, bf16[4,80,1152]{2,1,0:T(8,128)(2,1)S(1)}, u32[]{:S(2)}, u32[]{:S(2)}) collective-permute-start(bf16[4,80,1152]{2,1,0:T(8,128)(2,1)} %get-tuple-element.126.mine), channel_id=1, source_target_pairs={{0,8},{1,9},{2,10},{3,11},{4,12},{5,13},{6,14},{7,15},{8,0},{9,1},... | collective-permute-start | bytes 2211848 | tf_op jit(solution)/shard_map/cond/branch_0_fun/ppermute | solution.py:225
  93.1 8.7 %collective-permute-start.7 = (bf16[256,640]{1,0:T(8,128)(2,1)S(1)}, bf16[256,640]{1,0:T(8,128)(2,1)S(1)}, u32[]{:S(2)}, u32[]{:S(2)}) collective-permute-start(bf16[256,640]{1,0:T(8,128)(2,1)S(1)} %get-tuple-element.124.here), channel_id=1, source_target_pairs={{1,2},{2,1},{3,4},{4,3},{5,6},{6,5},{9,10},{10,9},{11,12},{12,11},... | collective-permute-start | bytes 983048 | tf_op jit(solution)/shard_map/cond/branch_0_fun/ppermute | solution.py:225
  95.6 6.2 %collective-permute-start.8 = (bf16[256,640]{1,0:T(8,128)(2,1)S(1)}, bf16[256,640]{1,0:T(8,128)(2,1)S(1)}, u32[]{:S(2)}, u32[]{:S(2)}) collective-permute-start(bf16[256,640]{1,0:T(8,128)(2,1)S(1)} %get-tuple-element.124.here), channel_id=1, source_target_pairs={{0,1},{1,0},{2,3},{3,2},{4,5},{5,4},{6,7},{7,6},{8,9},{9,8},{10,11... | collective-permute-start | bytes 983048 | tf_op jit(solution)/shard_map/cond/branch_0_fun/ppermute | solution.py:225
  98.1 8.5 %copy-start.4 = (bf16[4,80,1152]{2,1,0:T(8,128)(2,1)S(1)}, bf16[4,80,1152]{2,1,0:T(8,128)(2,1)}, u32[]{:S(2)}) copy-start(bf16[4,80,1152]{2,1,0:T(8,128)(2,1)} %get-tuple-element.126.mine) | copy-start | bytes 2211844 | tf_op jit(solution)/shard_map/cond
  104.5 5.4 %collective-permute-start.9 = (bf16[2,64,320]{2,1,0:T(8,128)(2,1)S(1)}, bf16[2,64,320]{2,1,0:T(8,128)(2,1)S(1)}, u32[]{:S(2)}, u32[]{:S(2)}) collective-permute-start(bf16[2,64,320]{2,1,0:T(8,128)(2,1)S(1)} %dynamic-slice_bitcast_fusion.1), channel_id=1, source_target_pairs={{0,8},{1,9},{2,10},{3,11},{4,12},{5,13},{6,14},{7,15},{8,0},{9,1},... | collective-permute-start | bytes 245768 | tf_op jit(solution)/shard_map/cond/branch_0_fun/ppermute | solution.py:225

commit v3 on v2

--- a/solution.py
+++ b/solution.py
@@ -229,11 +229,11 @@
     return lax.optimization_barrier((block,) + earlier)[0]
 
 
-def kernel_call(body, outs, args, scratch=(), copies=0, stay=False, micros=0):
+def kernel_call(body, outs, args, scratch=(), copies=0, stay=False, micros=0, near=False):
     def space(a):
         if a.dtype == jnp.int32:
             return pltpu.SMEM
-        return pltpu.VMEM if a.dtype == jnp.float32 else pl.ANY
+        return pltpu.VMEM if near or a.dtype == jnp.float32 else pl.ANY
 
     buffers = [pltpu.VMEM(shape, kind) for shape, kind in scratch]
     return pl.pallas_call(
@@ -241,7 +241,7 @@
         out_shape=[jax.ShapeDtypeStruct(shape, kind) for shape, kind in outs],
         in_specs=[pl.BlockSpec(memory_space=space(a)) for a in args],
         out_specs=[pl.BlockSpec(memory_space=pl.ANY if stay else pltpu.VMEM) for _ in outs],
-        scratch_shapes=buffers + [pltpu.SemaphoreType.DMA((copies,))],
+        scratch_shapes=buffers + ([pltpu.SemaphoreType.DMA((copies,))] if copies else []),
         compiler_params=pltpu.CompilerParams(vmem_limit_bytes=32 * 1024 * 1024),
         cost_estimate=pl.CostEstimate(
             flops=0, bytes_accessed=1 + 3_700_000 * micros, transcendentals=0
@@ -271,9 +271,22 @@
     return pl.ds(pl.multiple_of(start, 16), count)
 
 
-def stack_kernel(*refs):
-    *pieces, stacked, done = refs
-    finish(begin([(piece, stacked.at[n]) for n, piece in enumerate(pieces)], done))
+def stack_kernel(spot, one, two, three, four, stacked, heads, shared, done):
+    pieces = (one, two, three, four)
+    started = begin([(piece, stacked.at[n]) for n, piece in enumerate(pieces)], done)
+
+    def part(first, target):
+        rows = slice(first, first + target.shape[1])
+        finish(begin([(piece.at[rows], target.at[n]) for n, piece in enumerate(pieces)], done, 4))
+
+    is_control = spot[0] == 1
+    is_query = spot[3] == spot[1]
+    low = spot[1] == 0
+    pl.when(is_control & is_query)(lambda: part(2 * SLOT, heads))
+    pl.when(is_control & jnp.logical_not(is_query))(lambda: part(SLOT, heads))
+    pl.when(jnp.logical_not(is_control) & low)(lambda: part(SLOT, shared))
+    pl.when(jnp.logical_not(is_control | low))(lambda: part(2 * SLOT - SHARED, shared))
+    finish(started)
 
 
 def norm_kernel(spot, own, far, mod, normed, first, second, done):
@@ -310,12 +323,12 @@
     return (origin % 2) * 2 + origin // 2
 
 
-def arrange_keyvals(link, stacks, weight):
-    for at in range(2):
+def arrange_keyvals(link, core, mine, other, weight):
+    for block, at in ((mine, core), (other, 1 - core)):
         for step in range(4):
             origin = link ^ ORDER[step]
             slot = (1 - origin // 2) * 4 + at * 2 + origin % 2
-            weight[rows_at(slot * SLOT, SLOT), :] = stacks[at, step, :SLOT]
+            weight[rows_at(slot * SLOT, SLOT), :] = block[step, :SLOT]
 
 
 def arrange_heads(link, stack, first_row, weight):
@@ -328,17 +341,21 @@
     weight[start:stop, :] = jnp.zeros((stop - start, weight.shape[1]), weight.dtype)
 
 
-def project_kernel(spot, normed, normed_other, mine, other, keyval, query, stacks, weight, both, done):
-    row, link, core = (spot[1], spot[2], spot[3])
-    copies = [(mine, stacks.at[core]), (other, stacks.at[1 - core])]
-    for image in range(normed.shape[0]):
-        copies.append((normed.at[image], both.at[image, row]))
-        copies.append((normed_other.at[image], both.at[image, 1 - row]))
-    finish(begin(copies, done))
-    arrange_keyvals(link, stacks, weight)
+def arrange_queries(spot, mine, other, part, weight):
     start = weight.shape[0] - 4 * SLOT
     clear_rows(weight, 8 * SLOT, start)
-    arrange_heads(link, stacks.at[row, :, SLOT : 2 * SLOT], start, weight)
+    rows = slice(part * SLOT, (part + 1) * SLOT)
+    own = spot[3] == spot[1]
+    pl.when(own)(lambda: arrange_heads(spot[2], mine.at[:, rows], start, weight))
+    pl.when(jnp.logical_not(own))(lambda: arrange_heads(spot[2], other.at[:, rows], start, weight))
+
+
+def project_kernel(spot, normed, normed_other, mine, other, keyval, query, weight, both):
+    row, link, core = (spot[1], spot[2], spot[3])
+    arrange_keyvals(link, core, mine, other, weight)
+    arrange_queries(spot, mine, other, 1, weight)
+    both[:, row] = normed[...]
+    both[:, 1 - row] = normed_other[...]
     tokens = both[...].reshape(-1, both.shape[3])
     projected = dot_rows(tokens, weight[...]).astype(keyval.dtype)
     keyval[...] = projected[:, : keyval.shape[1]]
@@ -346,7 +363,7 @@
 
 
 def attend_kernel(spot, queries, outer, here, inner, bias, out, query_rows, keyvals, done):
-    scaling = 1.0 / math.sqrt(HD)
+    scaling = math.log2(math.e) / math.sqrt(HD)
     tokens = bias.shape[0]
     images = out.shape[0] // tokens
     copies = [(queries, query_rows)]
@@ -373,15 +390,15 @@
         raised, sums = ([], [])
         for head in range(heads):
             part = scores[head * tokens : (head + 1) * tokens] * scaling + bias[...]
-            part = jnp.exp(part - jnp.max(part, axis=-1, keepdims=True))
-            sums.append(jnp.sum(part, axis=-1, keepdims=True))
+            part = jnp.exp2(part - jnp.max(part, axis=-1, keepdims=True))
+            sums.append(1.0 / jnp.sum(part, axis=-1, keepdims=True))
             raised.append(part.astype(jnp.bfloat16))
         blended = jnp.dot(
             jnp.concatenate(raised, axis=0), values, preferred_element_type=jnp.float32
         )
         total = jnp.zeros((tokens, value_lanes), jnp.float32)
         for head in range(heads):
-            part = blended[head * tokens : (head + 1) * tokens] / sums[head]
+            part = blended[head * tokens : (head + 1) * tokens] * sums[head]
             total = jnp.where(within(value_lane, head), part, total)
         out[rows, :] = total[:, : out.shape[1]].astype(out.dtype)
 
@@ -397,52 +414,44 @@
 def middle_kernel(
     spot, own, far, side, corner, near, cross, out_mine, out_other, first, first_other,
     zero_side, zero_corner, mod, mod_base, residue, keyval, query,
-    base_rows, more_rows, heads, outs, w_out, stacks, zeros, w_zero, weight, both, done,
+    w_out, w_zero, weight, both,
 ):
     row, link, core = (spot[1], spot[2], spot[3])
     images, tokens, _ = own.shape
     tile = images * tokens
-    width = heads.shape[2]
-    copies = []
-    for image in range(images):
-        for part, slot in ((0, row), (1, 1 - row)):
-            rows = slice(part * tile + image * tokens, part * tile + (image + 1) * tokens)
-            for index, ref in enumerate((near, cross)):
-                copies.append((ref.at[image, slot], heads.at[index, rows]))
-    copies += [(out_mine, outs.at[core]), (out_other, outs.at[1 - core])]
-    copies += [(own, base_rows.at[0]), (side, base_rows.at[1])]
-    copies += [(far, more_rows.at[0]), (corner, more_rows.at[1])]
-    early = begin(copies, done)
-    copies = [(first, stacks.at[core]), (first_other, stacks.at[1 - core])]
-    copies += [(zero_side, zeros.at[core]), (zero_corner, zeros.at[1 - core])]
-    late = begin(copies, done, len(early))
-    finish(early)
-    for at in range(2):
-        arrange_heads(link, outs.at[at], at * width, w_out)
-    projected = jnp.dot(
-        heads[0], w_out[rows_at(row * width, width), :], preferred_element_type=jnp.float32
-    )
-    projected += jnp.dot(
-        heads[1], w_out[rows_at((1 - row) * width, width), :], preferred_element_type=jnp.float32
-    )
-
-    def flat(ref):
-        return ref[...].reshape(2 * tile, ref.shape[3]).astype(jnp.float32)
-
-    base = flat(base_rows)
-    out = (base + flat(more_rows) + mod[2] * projected).astype(jnp.bfloat16)
-    finish(late)
+    width = near.shape[3]
+    for block, at in ((out_mine, core), (out_other, 1 - core)):
+        arrange_heads(link, block, at * width, w_out)
     shard = w_zero.shape[0] // 8
     kept = shard - SHARED
-    for at in range(2):
+    for block, part, at in (
+        (first, zero_side, core),
+        (first_other, zero_corner, 1 - core),
+    ):
         for step in range(4):
             start = (2 * (link ^ ORDER[step]) + at) * shard
-            w_zero[rows_at(start + row * SHARED, kept), :] = stacks[at, step, SLOT : 2 * SLOT]
-            w_zero[rows_at(start + (1 - row) * kept, SHARED), :] = zeros[at, step]
-    arrange_keyvals(link, stacks, weight)
-    start = weight.shape[0] - 4 * SLOT
-    clear_rows(weight, 8 * SLOT, start)
-    arrange_heads(link, stacks.at[row, :, 2 * SLOT :], start, weight)
+            w_zero[rows_at(start + row * SHARED, kept), :] = block[step, SLOT : 2 * SLOT]
+            w_zero[rows_at(start + (1 - row) * kept, SHARED), :] = part[step]
+    arrange_keyvals(link, core, first, first_other, weight)
+    arrange_queries(spot, first, first_other, 2, weight)
+
+    def ordered(ref):
+        return jnp.concatenate([ref[i, s] for s in (row, 1 - row) for i in range(images)], axis=0)
+
+    def stacked(one, two):
+        parts = [ref[i] for ref in (one, two) for i in range(images)]
+        return jnp.concatenate(parts, axis=0).astype(jnp.float32)
+
+    projected = jnp.dot(
+        ordered(near), w_out[rows_at(row * width, width), :], preferred_element_type=jnp.float32
+    )
+    projected += jnp.dot(
+        ordered(cross),
+        w_out[rows_at((1 - row) * width, width), :],
+        preferred_element_type=jnp.float32,
+    )
+    base = stacked(own, side)
+    out = (base + stacked(far, corner) + mod[2] * projected).astype(jnp.bfloat16)
     residual = dot_rows(out, w_zero[...]).astype(jnp.bfloat16)
     base = base + residual.astype(jnp.float32)
     result = modulate(base, mod_base)
@@ -521,12 +530,6 @@
     def padded_rows(block):
         return jnp.pad(block, ((0, SLOT - HD), (0, 0)))
 
-    def stacked(pieces):
-        shape = (len(pieces),) + pieces[0].shape
-        out = [(shape, jnp.bfloat16)]
-        (stack,) = kernel_call(stack_kernel, out, pieces, copies=len(pieces), stay=True)
-        return stack.reshape((-1,) + shape[-2:])
-
     def joined(block, other):
         return jnp.concatenate([block, other], axis=0)
 
@@ -542,8 +545,6 @@
     projections = [((tokens, 2 * half), jnp.bfloat16), ((tokens, lanes), jnp.bfloat16)]
     shard = w_zero.shape[1]
     triple_shape = ((4, 3 * SLOT, D), jnp.bfloat16)
-    stacks = ((2,) + triple_shape[0], jnp.bfloat16)
-    shared_stacks = ((2, 4, SHARED, D), jnp.bfloat16)
     half_stacks = ((2, 4, SLOT, D), jnp.bfloat16)
     both_shape = ((images, 2, tile, D), jnp.bfloat16)
 
@@ -568,13 +569,20 @@
         norm_kernel, [(tile_shape, jnp.bfloat16)], (spot, own, far, modulation[1]),
         scratch=[(tile_shape, jnp.bfloat16), (tile_shape, jnp.bfloat16)], copies=2,
     )
+    (bias,) = kernel_call(
+        functools.partial(bias_kernel, 2 * tile_rows, sizes[2] * tile_cols),
+        [((2 * tile, 6 * tile), jnp.float32)], (spot,), copies=1,
+    )
     side = swap_rows(jnp.where(is_control, normed, own))
-    side, corner, *first = lax.optimization_barrier((side, corner, *first))
+    side, corner, bias, *first = lax.optimization_barrier((side, corner, bias, *first))
     first.append(swap_links(first[1], ORDER[2]))
-    first = stacked(first)
+    first, head_stack, shared = kernel_call(
+        stack_kernel, [triple_shape, stack_shape, shared_shape], (spot, *first),
+        copies=8, stay=True,
+    )
     first_other = swap_cores(first)
-    head_stack = jnp.where(is_query, first[:, 2 * SLOT :], first[:, SLOT : 2 * SLOT])
     out_mine = send(head_stack, sizes, lambda b, r, t: (0, r, t) if b == 1 else None)
+    zero_side = swap_rows(shared, base_only)
 
     def halos(keyval, joins):
         def across(b, r, t):
@@ -584,10 +592,6 @@
         return send(keyval, sizes, across), swap_cores(keyval, joins)
 
     def neighborhood(query, keyval, outer, inner):
-        (bias,) = kernel_call(
-            functools.partial(bias_kernel, 2 * tile_rows, sizes[2] * tile_cols),
-            [((2 * tile, 6 * tile), jnp.float32)], (spot,), copies=1,
-        )
         (attended,) = kernel_call(
             attend_kernel, [((tokens, half), jnp.bfloat16)],
             (spot, query, outer, keyval, inner, bias),
@@ -620,8 +624,7 @@
     def control_attention():
         keyval, query = kernel_call(
             project_kernel, projections, (spot, normed, side, first, first_other),
-            scratch=[stacks, ((2 * half + lanes, D), jnp.bfloat16), both_shape],
-            copies=2 + 2 * images, micros=5,
+            scratch=[((2 * half + lanes, D), jnp.bfloat16), both_shape], micros=5, near=True,
         )
         attended = neighborhood(query, keyval, *halos(keyval, control_only))
         return attended
@@ -629,32 +632,22 @@
     attended = lax.cond(is_control, control_attention, lambda: unset(head_shape)[0])
     near = send(attended, sizes, lambda b, r, t: (0, r, t) if b == 1 else None)
     cross = send(attended, sizes, lambda b, r, t: (0, 1 - r, t) if b == 1 else None)
-
-    def base_exchange():
-        shared = lax.dynamic_slice_in_dim(
-            after(first, attended), SLOT + row * (SLOT - SHARED), SHARED, axis=1
-        )
-        third = jnp.where(
-            is_query, first_other[:, 2 * SLOT :], after(first, attended)[:, 2 * SLOT :]
-        )
-        return swap_rows(shared, base_only), third
-
-    zero_side, third = lax.cond(
-        is_control, lambda: unset(shared_shape, stack_shape), base_exchange
-    )
 
     def control_finish():
         rows = head_rows(3, swap_cores(head_stack, control_only), head_stack)
         side_heads = their_heads(attended, control_only)
         out = finished(attended, side_heads, rows, far, modulation[1])
-        return unset(shared_shape, stack_shape) + (out,)
+        return unset(shared_shape, stack_shape, stack_shape) + (out,)
 
     def base_prepare():
+        third = jnp.where(
+            is_query, first_other[:, 2 * SLOT :], after(first, attended)[:, 2 * SLOT :]
+        )
         zero_corner = swap_cores(zero_side, base_only)
         out_other = swap_cores(out_mine, base_only)
-        return (zero_corner, out_other) + unset((tile_shape, jnp.bfloat16))
-
-    zero_corner, out_other, control = lax.cond(
+        return (zero_corner, out_other, third) + unset((tile_shape, jnp.bfloat16))
+
+    zero_corner, out_other, third, control = lax.cond(
         is_control, control_finish, base_prepare
     )
 
@@ -668,18 +661,12 @@
                 zero_side, zero_corner, modulation[1], modulation[0],
             ),
             scratch=[
-                ((2, images, tile, D), jnp.bfloat16),
-                ((2, images, tile, D), jnp.bfloat16),
-                ((2, 2 * images * tile, half), jnp.bfloat16),
-                half_stacks,
                 rows_shape,
-                stacks,
-                shared_stacks,
                 ((D, D), jnp.bfloat16),
                 ((2 * half + lanes, D), jnp.bfloat16),
                 both_shape,
             ],
-            copies=4 * images + 10, micros=8,
+            micros=8, near=True,
         )
         outer, inner = halos(keyval, base_only)
         attended = neighborhood(query, keyval, outer, inner)

time: 113 us -> 112 us (level)
  waiting for transfers between devices: 54.7 us -> 51.6 us
  starting transfers between devices: 31 us -> 33.7 us
  other arithmetic: 5.75 us -> 4.54 us
    ppermute x17, waiting for transfers between devices: 54.7 us -> 51.6 us  [send(): return lax.ppermute(block, AXES, routes(sizes, move))]
    ppermute x17, starting transfers between devices: 31 us -> 33.7 us  [send(): return lax.ppermute(block, AXES, routes(sizes, move))]
    select_n x2 -> x1, other arithmetic: 3.54 us -> 2.29 us  [base_prepare(): jnp.where(is_query, first_other[:, 2 * SLOT:], after(first, attended)[:,...]
    unnamed x15 -> x21, local copies, waits for them, and re-layouts: 1.86 us -> 2.35 us
  transfers between devices with their start and end apart: 17 -> 17, of which waited for: 10 -> 10; matrix products, arithmetic and copies ran while one was open for 4% -> 2% of each run, Pallas kernels for 12% -> 13%
where the time goes in v3:
time: 112 us; the launch traced here: 111 us
  waiting for transfers between devices  51.6 us (46%)
  starting transfers between devices  33.7 us (30%)
  Pallas kernels  18.1 us (16%)
  other arithmetic  4.54 us (4%)
  local copies, waits for them, and re-layouts  2.52 us (2%)
    ppermute x17, waiting for transfers between devices, send(): return lax.ppermute(block, AXES, routes(sizes, move))  51.6 us
    ppermute x17, starting transfers between devices, send(): return lax.ppermute(block, AXES, routes(sizes, move))  33.7 us
    pallas_call x9, Pallas kernels, kernel_call(): pl.pallas_call(body, out_shape=[jax.ShapeDtypeStruct(shape, kind) for sha...  18.1 us
    unnamed x21, local copies, waits for them, and re-layouts  2.35 us
    select_n x1, other arithmetic, base_prepare(): jnp.where(is_query, first_other[:, 2 * SLOT:], after(first, attended)[:,...  2.29 us
  transfers between devices with their start and end apart: 17, of which 10 were waited for; matrix products, arithmetic and copies ran while one was open for 2% of the time, Pallas kernels for 13%

profile of v3, /device:TPU:1, one launch (start us, length us, event | category | flops | bytes accessed | tf_op | source)
XLA Modules:
  0.0 111.0 jit_solution(7865092339163215656)
XLA Ops:
  3.2 2.1 %collective-permute-start.10 = (bf16[2,64,1152]{2,1,0:T(8,128)(2,1)S(1)}, bf16[2,64,1152]{2,1,0:T(8,128)(2,1)S(1)}, u32[]{:S(2)}, u32[]{:S(2)}) collective-permute-start(bf16[2,64,1152]{2,1,0:T(8,128)(2,1)S(1)} %bitcast.39), channel_id=1, source_target_pairs={{0,16},{1,17},{2,18},{3,19},{4,20},{5,21},{6,22},{7,23},{8,24},{9,... | collective-permute-start | bytes 884744 | tf_op jit(solution)/shard_map/ppermute | solution.py:225
  5.4 3.3 %collective-permute-start.13 = (bf16[240,1152]{1,0:T(8,128)(2,1)S(1)}, bf16[240,1152]{1,0:T(8,128)(2,1)S(1)}, u32[]{:S(2)}, u32[]{:S(2)}) collective-permute-start(bf16[240,1152]{1,0:T(8,128)(2,1)S(1)} %fusion.2.one), channel_id=1, source_target_pairs={{0,6},{1,7},{2,4},{3,5},{4,2},{5,3},{6,0},{7,1},{8,14},{9,15},{10,... | collective-permute-start | bytes 1658888 | tf_op jit(solution)/shard_map/ppermute | solution.py:225
  8.7 1.3 %collective-permute-start.12 = (bf16[2,64,1152]{2,1,0:T(8,128)(2,1)S(1)}, bf16[2,64,1152]{2,1,0:T(8,128)(2,1)S(1)}, u32[]{:S(2)}, u32[]{:S(2)}) collective-permute-start(bf16[2,64,1152]{2,1,0:T(8,128)(2,1)S(1)} %bitcast.40), channel_id=1, source_target_pairs={{16,8},{17,9},{18,10},{19,11},{20,12},{21,13},{22,14},{23,15},{24,... | collective-permute-start | bytes 884744 | tf_op jit(solution)/shard_map/ppermute | solution.py:225
  10.1 2.0 %collective-permute-done.10.far = bf16[2,64,1152]{2,1,0:T(8,128)(2,1)S(1)} collective-permute-done((bf16[2,64,1152]{2,1,0:T(8,128)(2,1)S(1)}, bf16[2,64,1152]{2,1,0:T(8,128)(2,1)S(1)}, u32[]{:S(2)}, u32[]{:S(2)}) %collective-permute-start.10) | collective-permute-done | bytes 294944 | tf_op jit(solution)/shard_map/ppermute | solution.py:225
  14.3 1.3 %shard_map.67 = f32[128,384]{1,0:T(8,128)} custom-call(s32[5]{0:T(128)S(1)} %stack.26.spot), custom_call_target="tpu_custom_call" | custom-call | bytes 1 | tf_op jit(solution)/shard_map/pallas_call | solution.py:239
  15.6 3.1 %collective-permute-done.12 = bf16[2,64,1152]{2,1,0:T(8,128)(2,1)S(1)} collective-permute-done((bf16[2,64,1152]{2,1,0:T(8,128)(2,1)S(1)}, bf16[2,64,1152]{2,1,0:T(8,128)(2,1)S(1)}, u32[]{:S(2)}, u32[]{:S(2)}) %collective-permute-start.12) | collective-permute-done | bytes 294944 | tf_op jit(solution)/shard_map/ppermute | solution.py:225
  18.7 1.8 %collective-permute-done.13.two = bf16[240,1152]{1,0:T(8,128)(2,1)S(1)} collective-permute-done((bf16[240,1152]{1,0:T(8,128)(2,1)S(1)}, bf16[240,1152]{1,0:T(8,128)(2,1)S(1)}, u32[]{:S(2)}, u32[]{:S(2)}) %collective-permute-start.13) | collective-permute-done | bytes 552992 | tf_op jit(solution)/shard_map/ppermute | solution.py:225
  20.5 13.1 %collective-permute-done.14.three = bf16[240,1152]{1,0:T(8,128)(2,1)S(1)} collective-permute-done((bf16[240,1152]{1,0:T(8,128)(2,1)S(1)}, bf16[240,1152]{1,0:T(8,128)(2,1)S(1)}, u32[]{:S(2)}, u32[]{:S(2)}) %collective-permute-start.14) | collective-permute-done | bytes 552992 | tf_op jit(solution)/shard_map/ppermute | solution.py:225
  34.4 12.9 %collective-permute-done.15.four = bf16[240,1152]{1,0:T(8,128)(2,1)S(1)} collective-permute-done((bf16[240,1152]{1,0:T(8,128)(2,1)S(1)}, bf16[240,1152]{1,0:T(8,128)(2,1)S(1)}, u32[]{:S(2)}, u32[]{:S(2)}) %collective-permute-start.15) | collective-permute-done | bytes 552992 | tf_op jit(solution)/shard_map/ppermute | solution.py:225
  47.3 2.0 %shard_map.68 = (bf16[4,240,1152]{2,1,0:T(8,128)(2,1)}, bf16[4,80,1152]{2,1,0:T(8,128)(2,1)}, bf16[4,64,1152]{2,1,0:T(8,128)(2,1)S(1)}) custom-call(s32[5]{0:T(128)S(1)} %stack.26.spot, bf16[240,1152]{1,0:T(8,128)(2,1)S(1)} %fusion.2.one, bf16[240,1152]{1,0:T(8,128)(2,1)S(1)} %collective-permute-done.13.two, ...), custom_call_target="tpu_custom_call" | custom-call | bytes 1 | tf_op jit(solution)/shard_map/pallas_call | solution.py:239
  49.3 1.4 %collective-permute-start.16 = (bf16[4,240,1152]{2,1,0:T(8,128)(2,1)}, bf16[4,240,1152]{2,1,0:T(8,128)(2,1)}, u32[]{:S(2)}, u32[]{:S(2)}) collective-permute-start(bf16[4,240,1152]{2,1,0:T(8,128)(2,1)} %get-tuple-element.150), channel_id=1, source_target_pairs={{0,1},{1,0},{2,3},{3,2},{4,5},{5,4},{6,7},{7,6},{8,9},{9,8},{10,11... | collective-permute-start | bytes 6635528 | tf_op jit(solution)/shard_map/ppermute | solution.py:225
  52.0 3.1 %collective-permute-start.20 = (bf16[4,64,1152]{2,1,0:T(8,128)(2,1)S(1)}, bf16[4,64,1152]{2,1,0:T(8,128)(2,1)}, u32[]{:S(2)}, u32[]{:S(2)}) collective-permute-start(bf16[4,64,1152]{2,1,0:T(8,128)(2,1)S(1)} %get-tuple-element.153), channel_id=1, source_target_pairs={{0,8},{1,9},{2,10},{3,11},{4,12},{5,13},{6,14},{7,15},{8,0},{9,1},... | collective-permute-start | bytes 1769480 | tf_op jit(solution)/shard_map/ppermute | solution.py:225
  55.7 1.3 %collective-permute-start.17 = (bf16[2,2,64,320]{3,2,1,0:T(8,128)(2,1)}, bf16[2,2,64,320]{3,2,1,0:T(8,128)(2,1)S(1)}, u32[]{:S(2)}, u32[]{:S(2)}) collective-permute-start(bf16[2,2,64,320]{3,2,1,0:T(8,128)(2,1)} %get-tuple-element.197), channel_id=1, source_target_pairs={{16,0},{17,1},{18,2},{19,3},{20,4},{21,5},{22,6},{23,7},{24,8},{25... | collective-permute-start | bytes 491528 | tf_op jit(solution)/shard_map/ppermute | solution.py:225
  57.0 1.3 %collective-permute-start.18 = (bf16[2,2,64,320]{3,2,1,0:T(8,128)(2,1)}, bf16[2,2,64,320]{3,2,1,0:T(8,128)(2,1)S(1)}, u32[]{:S(2)}, u32[]{:S(2)}) collective-permute-start(bf16[2,2,64,320]{3,2,1,0:T(8,128)(2,1)} %get-tuple-element.197), channel_id=1, source_target_pairs={{16,8},{17,9},{18,10},{19,11},{20,12},{21,13},{22,14},{23,15},{24,... | collective-permute-start | bytes 491528 | tf_op jit(solution)/shard_map/ppermute | solution.py:225
  58.3 10.6 %collective-permute-done.20 = bf16[4,64,1152]{2,1,0:T(8,128)(2,1)} collective-permute-done((bf16[4,64,1152]{2,1,0:T(8,128)(2,1)S(1)}, bf16[4,64,1152]{2,1,0:T(8,128)(2,1)}, u32[]{:S(2)}, u32[]{:S(2)}) %collective-permute-start.20) | collective-permute-done | bytes 589856 | tf_op jit(solution)/shard_map/ppermute | solution.py:225
  68.9 2.1 %collective-permute-done.19 = bf16[4,80,1152]{2,1,0:T(8,128)(2,1)} collective-permute-done((bf16[4,80,1152]{2,1,0:T(8,128)(2,1)}, bf16[4,80,1152]{2,1,0:T(8,128)(2,1)}, u32[]{:S(2)}, u32[]{:S(2)}) %collective-permute-start.19) | collective-permute-done | bytes 737312 | tf_op jit(solution)/shard_map/ppermute | solution.py:225
  71.0 7.7 %conditional.4 = (bf16[4,64,1152]{2,1,0:T(8,128)(2,1)S(1)}, bf16[4,80,1152]{2,1,0:T(8,128)(2,1)}, bf16[4,80,1152]{2,1,0:T(8,128)(2,1)}, bf16[2,64,1152]{2,1,0:T(8,128)(2,1)S(1)}) conditional(s32[]{:T(128)} %convert_element_type.9, (bf16[4,64,1152]{2,1,0:T(8,128)(2,1)}, bf16[4,80,1152]{2,1,0:T(8,128)(2,1)}, pred[]{:T(512)}, ...), branch_computations={%region_2.3_spmd, %region_3.4_spmd} | conditional | flops 368640 | bytes 7520370 | solution.py:650
  71.0 2.8 %collective-permute-start.3 = (bf16[4,80,1152]{2,1,0:T(8,128)(2,1)}, bf16[4,80,1152]{2,1,0:T(8,128)(2,1)}, u32[]{:S(2)}, u32[]{:S(2)}) collective-permute-start(bf16[4,80,1152]{2,1,0:T(8,128)(2,1)} %get-tuple-element.98), channel_id=1, source_target_pairs={{0,1},{1,0},{2,3},{3,2},{4,5},{5,4},{6,7},{7,6},{8,9},{9,8},{10,11... | collective-permute-start | bytes 2211848 | tf_op jit(solution)/shard_map/cond/branch_0_fun/ppermute | solution.py:225
  73.8 1.9 %collective-permute-start.2 = (bf16[4,64,1152]{2,1,0:T(8,128)(2,1)}, bf16[4,64,1152]{2,1,0:T(8,128)(2,1)S(1)}, u32[]{:S(2)}, u32[]{:S(2)}) collective-permute-start(bf16[4,64,1152]{2,1,0:T(8,128)(2,1)} %get-tuple-element.97), channel_id=1, source_target_pairs={{0,1},{1,0},{2,3},{3,2},{4,5},{5,4},{6,7},{7,6},{8,9},{9,8},{10,11... | collective-permute-start | bytes 1769480 | tf_op jit(solution)/shard_map/cond/branch_0_fun/ppermute | solution.py:225
  76.3 2.3 %slice_select_fusion = bf16[4,80,1152]{2,1,0:T(8,128)(2,1)} fusion(bf16[4,240,1152]{2,1,0:T(8,128)(2,1)} %get-tuple-element.101, bf16[4,240,1152]{2,1,0:T(8,128)(2,1)} %get-tuple-element.100, pred[]{:T(512)} %get-tuple-element.99), kind=kLoop, calls=%fused_computation | loop fusion | flops 368640 | bytes 2211841 | tf_op jit(solution)/shard_map/cond/branch_0_fun/jit(_where)/select_n | solution.py:643
  78.6 1.7 %collective-permute-done.17 = bf16[2,2,64,320]{3,2,1,0:T(8,128)(2,1)S(1)} collective-permute-done((bf16[2,2,64,320]{3,2,1,0:T(8,128)(2,1)}, bf16[2,2,64,320]{3,2,1,0:T(8,128)(2,1)S(1)}, u32[]{:S(2)}, u32[]{:S(2)}) %collective-permute-start.17) | collective-permute-done | bytes 163872 | tf_op jit(solution)/shard_map/ppermute | solution.py:225
  80.4 29.9 %conditional.5 = (bf16[1,2,8,8,1152]{4,3,2,1,0:T(8,128)(2,1)S(1)}) conditional(s32[]{:T(128)} %convert_element_type.9, (f32[2,3,1152]{2,0,1:T(2,128)S(1)}, s32[5]{0:T(128)S(1)}, bf16[2,64,1152]{2,1,0:T(8,128)(2,1)S(1)}, bf16[2,64,1152]{2,1,0:T(8,128)(2,1)S(1)}, bf16[2,64,1152]{2,1,0:T(8,128)(2,1)S(1)}, /*index=5*/bf16[2,64,1152]{2,1,0:T(8,128)(2,1)S(1)}, ...), branch_computations={%region_4.5_spmd, %region_5.6_spmd} | conditional | flops 4 | bytes 68387600 | solution.py:676
  80.4 3.0 %collective-permute-start.9 = (bf16[4,80,1152]{2,1,0:T(8,128)(2,1)}, bf16[4,80,1152]{2,1,0:T(8,128)(2,1)S(1)}, u32[]{:S(2)}, u32[]{:S(2)}) collective-permute-start(bf16[4,80,1152]{2,1,0:T(8,128)(2,1)} %get-tuple-element.128.mine), channel_id=1, source_target_pairs={{0,8},{1,9},{2,10},{3,11},{4,12},{5,13},{6,14},{7,15},{8,0},{9,1},... | collective-permute-start | bytes 2211848 | tf_op jit(solution)/shard_map/cond/branch_0_fun/ppermute | solution.py:225
  83.4 6.6 %branch_0_fun.8 = (bf16[2,64,1152]{2,1,0:T(8,128)(2,1)S(1)}, bf16[256,640]{1,0:T(8,128)(2,1)S(1)}, bf16[256,384]{1,0:T(8,128)(2,1)S(1)}) custom-call(s32[5]{0:T(128)S(1)} %get-tuple-element.110.spot, bf16[2,64,1152]{2,1,0:T(8,128)(2,1)S(1)} %get-tuple-element.111.own, bf16[2,64,1152]{2,1,0:T(8,128)(2,1)S(1)} %get-tuple-element.112.far, ...), custom_call_target="tpu_custom_call" | custom-call | bytes 29600000 | tf_op jit(solution)/shard_map/cond/branch_0_fun/pallas_call | solution.py:239
  90.0 5.2 %collective-permute-start.6 = (bf16[256,640]{1,0:T(8,128)(2,1)S(1)}, bf16[256,640]{1,0:T(8,128)(2,1)S(1)}, u32[]{:S(2)}, u32[]{:S(2)}) collective-permute-start(bf16[256,640]{1,0:T(8,128)(2,1)S(1)} %get-tuple-element.125.here), channel_id=1, source_target_pairs={{1,2},{2,1},{3,4},{4,3},{5,6},{6,5},{9,10},{10,9},{11,12},{12,11},... | collective-permute-start | bytes 983048 | tf_op jit(solution)/shard_map/cond/branch_0_fun/ppermute | solution.py:225
  95.3 1.9 %collective-permute-start.7 = (bf16[256,640]{1,0:T(8,128)(2,1)S(1)}, bf16[256,640]{1,0:T(8,128)(2,1)S(1)}, u32[]{:S(2)}, u32[]{:S(2)}) collective-permute-start(bf16[256,640]{1,0:T(8,128)(2,1)S(1)} %get-tuple-element.125.here), channel_id=1, source_target_pairs={{0,1},{1,0},{2,3},{3,2},{4,5},{5,4},{6,7},{7,6},{8,9},{9,8},{10,11... | collective-permute-start | bytes 983048 | tf_op jit(solution)/shard_map/cond/branch_0_fun/ppermute | solution.py:225
  97.2 2.8 %collective-permute-done.6.outer = bf16[256,640]{1,0:T(8,128)(2,1)S(1)} collective-permute-done((bf16[256,640]{1,0:T(8,128)(2,1)S(1)}, bf16[256,640]{1,0:T(8,128)(2,1)S(1)}, u32[]{:S(2)}, u32[]{:S(2)}) %collective-permute-start.6) | collective-permute-done | bytes 327712 | tf_op jit(solution)/shard_map/cond/branch_0_fun/ppermute | solution.py:225
  100.0 2.6 %branch_0_fun.9 = bf16[256,320]{1,0:T(8,128)(2,1)S(1)} custom-call(s32[5]{0:T(128)S(1)} %get-tuple-element.110.spot, bf16[256,384]{1,0:T(8,128)(2,1)S(1)} %get-tuple-element.124.queries, bf16[256,640]{1,0:T(8,128)(2,1)S(1)} %collective-permute-done.6.outer, bf16[256,640]{1,0:T(8,128)(2,1)S(1)} %get-tuple-element.125.here, ...), custom_call_target="tpu_custom_call" | custom-call | bytes 29600000 | tf_op jit(solution)/shard_map/cond/branch_0_fun/pallas_call | solution.py:239
  102.7 2.4 %collective-permute-start.8 = (bf16[2,64,320]{2,1,0:T(8,128)(2,1)S(1)}, bf16[2,64,320]{2,1,0:T(8,128)(2,1)S(1)}, u32[]{:S(2)}, u32[]{:S(2)}) collective-permute-start(bf16[2,64,320]{2,1,0:T(8,128)(2,1)S(1)} %dynamic-slice_bitcast_fusion.1), channel_id=1, source_target_pairs={{0,8},{1,9},{2,10},{3,11},{4,12},{5,13},{6,14},{7,15},{8,0},{9,1},... | collective-permute-start | bytes 245768 | tf_op jit(solution)/shard_map/cond/branch_0_fun/ppermute | solution.py:225
  105.1 1.8 %branch_0_fun.10.head_rows = bf16[640,1152]{1,0:T(8,128)(2,1)S(1)} custom-call(s32[5]{0:T(128)S(1)} %get-tuple-element.110.spot, bf16[4,80,1152]{2,1,0:T(8,128)(2,1)} %get-tuple-element.128.mine, bf16[4,80,1152]{2,1,0:T(8,128)(2,1)S(1)} %collective-permute-done.9.other), custom_call_target="tpu_custom_call" | custom-call | bytes 1 | tf_op jit(solution)/shard_map/cond/branch_0_fun/pallas_call | solution.py:239
  107.0 1.5 %collective-permute-done.8.side = bf16[2,64,320]{2,1,0:T(8,128)(2,1)S(1)} collective-permute-done((bf16[2,64,320]{2,1,0:T(8,128)(2,1)S(1)}, bf16[2,64,320]{2,1,0:T(8,128)(2,1)S(1)}, u32[]{:S(2)}, u32[]{:S(2)}) %collective-permute-start.8) | collective-permute-done | bytes 81952 | tf_op jit(solution)/shard_map/cond/branch_0_fun/ppermute | solution.py:225
  108.5 1.8 %branch_0_fun.11 = bf16[2,64,1152]{2,1,0:T(8,128)(2,1)S(1)} custom-call(s32[5]{0:T(128)S(1)} %get-tuple-element.110.spot, bf16[2,2,64,320]{3,2,1,0:T(8,128)(2,1)S(1)} %bitcast.37, bf16[2,64,320]{2,1,0:T(8,128)(2,1)S(1)} %collective-permute-done.8.side, bf16[640,1152]{1,0:T(8,128)(2,1)S(1)} %branch_0_fun.10.head_rows, ...), custom_call_target="tpu_custom_call" | custom-call | bytes 1 | tf_op jit(solution)/shard_map/cond/branch_0_fun/pallas_call | solution.py:239
  (50 shorter events, 9.9 us)
Async XLA Ops:
  0.0 1.0 copy-start
  2.0 1.2 %copy-start.1 = (bf16[1,2,8,8,1152]{4,3,2,1,0:T(8,128)(2,1)S(1)}, bf16[1,2,8,8,1152]{4,3,2,1,0:T(8,128)(2,1)}, u32[]{:S(2)}) copy-start(bf16[1,2,8,8,1152]{4,3,2,1,0:T(8,128)(2,1)} %param.12) | copy-start | bytes 884740
  2.0 8.0 %copy-start.11 = (f32[2,3,1152]{2,0,1:T(2,128)S(1)}, f32[2,3,1152]{2,0,1:T(2,128)}, u32[]{:S(2)}) copy-start(f32[2,3,1152]{2,0,1:T(2,128)} %param.13) | copy-start | bytes 82948
  3.2 8.9 %collective-permute-start.10 = (bf16[2,64,1152]{2,1,0:T(8,128)(2,1)S(1)}, bf16[2,64,1152]{2,1,0:T(8,128)(2,1)S(1)}, u32[]{:S(2)}, u32[]{:S(2)}) collective-permute-start(bf16[2,64,1152]{2,1,0:T(8,128)(2,1)S(1)} %bitcast.39), channel_id=1, source_target_pairs={{0,16},{1,17},{2,18},{3,19},{4,20},{5,21},{6,22},{7,23},{8,24},{9,... | collective-permute-start | bytes 884744 | tf_op jit(solution)/shard_map/ppermute | solution.py:225
  5.4 15.1 %collective-permute-start.13 = (bf16[240,1152]{1,0:T(8,128)(2,1)S(1)}, bf16[240,1152]{1,0:T(8,128)(2,1)S(1)}, u32[]{:S(2)}, u32[]{:S(2)}) collective-permute-start(bf16[240,1152]{1,0:T(8,128)(2,1)S(1)} %fusion.2.one), channel_id=1, source_target_pairs={{0,6},{1,7},{2,4},{3,5},{4,2},{5,3},{6,0},{7,1},{8,14},{9,15},{10,... | collective-permute-start | bytes 1658888 | tf_op jit(solution)/shard_map/ppermute | solution.py:225
  8.7 24.9 %collective-permute-start.14 = (bf16[240,1152]{1,0:T(8,128)(2,1)S(1)}, bf16[240,1152]{1,0:T(8,128)(2,1)S(1)}, u32[]{:S(2)}, u32[]{:S(2)}) collective-permute-start(bf16[240,1152]{1,0:T(8,128)(2,1)S(1)} %fusion.2.one), channel_id=1, source_target_pairs={{0,2},{1,3},{2,0},{3,1},{4,6},{5,7},{6,4},{7,5},{8,10},{9,11},{10,... | collective-permute-start | bytes 1658888 | tf_op jit(solution)/shard_map/ppermute | solution.py:225
  8.7 10.0 %collective-permute-start.12 = (bf16[2,64,1152]{2,1,0:T(8,128)(2,1)S(1)}, bf16[2,64,1152]{2,1,0:T(8,128)(2,1)S(1)}, u32[]{:S(2)}, u32[]{:S(2)}) collective-permute-start(bf16[2,64,1152]{2,1,0:T(8,128)(2,1)S(1)} %bitcast.40), channel_id=1, source_target_pairs={{16,8},{17,9},{18,10},{19,11},{20,12},{21,13},{22,14},{23,15},{24,... | collective-permute-start | bytes 884744 | tf_op jit(solution)/shard_map/ppermute | solution.py:225
  13.1 20.5 %collective-permute-start.11 = (bf16[2,64,1152]{2,1,0:T(8,128)(2,1)S(1)}, bf16[2,64,1152]{2,1,0:T(8,128)(2,1)S(1)}, u32[]{:S(2)}, u32[]{:S(2)}) collective-permute-start(bf16[2,64,1152]{2,1,0:T(8,128)(2,1)S(1)} %broadcast_select_fusion), channel_id=1, source_target_pairs={{0,8},{1,9},{2,10},{3,11},{4,12},{5,13},{6,14},{7,15},{8,0},{9,1},... | collective-permute-start | bytes 884744 | tf_op jit(solution)/shard_map/ppermute | solution.py:225
  18.7 15.0 %copy-start.7 = (bf16[2,64,1152]{2,1,0:T(8,128)(2,1)}, bf16[2,64,1152]{2,1,0:T(8,128)(2,1)S(1)}, u32[]{:S(2)}) copy-start(bf16[2,64,1152]{2,1,0:T(8,128)(2,1)S(1)} %collective-permute-done.12) | copy-start | bytes 884740
  33.7 0.7 copy-start.4
  33.7 13.6 %collective-permute-start.15 = (bf16[240,1152]{1,0:T(8,128)(2,1)S(1)}, bf16[240,1152]{1,0:T(8,128)(2,1)S(1)}, u32[]{:S(2)}, u32[]{:S(2)}) collective-permute-start(bf16[240,1152]{1,0:T(8,128)(2,1)S(1)} %collective-permute-done.13.two), channel_id=1, source_target_pairs={{0,2},{1,3},{2,0},{3,1},{4,6},{5,7},{6,4},{7,5},{8,10},{9,11},{10,... | collective-permute-start | bytes 1658888 | tf_op jit(solution)/shard_map/ppermute | solution.py:225
  49.3 5.8 %collective-permute-start.16 = (bf16[4,240,1152]{2,1,0:T(8,128)(2,1)}, bf16[4,240,1152]{2,1,0:T(8,128)(2,1)}, u32[]{:S(2)}, u32[]{:S(2)}) collective-permute-start(bf16[4,240,1152]{2,1,0:T(8,128)(2,1)} %get-tuple-element.150), channel_id=1, source_target_pairs={{0,1},{1,0},{2,3},{3,2},{4,5},{5,4},{6,7},{7,6},{8,9},{9,8},{10,11... | collective-permute-start | bytes 6635528 | tf_op jit(solution)/shard_map/ppermute | solution.py:225
  50.7 20.3 %collective-permute-start.19 = (bf16[4,80,1152]{2,1,0:T(8,128)(2,1)}, bf16[4,80,1152]{2,1,0:T(8,128)(2,1)}, u32[]{:S(2)}, u32[]{:S(2)}) collective-permute-start(bf16[4,80,1152]{2,1,0:T(8,128)(2,1)} %get-tuple-element.152), channel_id=1, source_target_pairs={{16,0},{17,1},{18,2},{19,3},{20,4},{21,5},{22,6},{23,7},{24,8},{25... | collective-permute-start | bytes 2211848 | tf_op jit(solution)/shard_map/ppermute | solution.py:225
  52.0 16.9 %collective-permute-start.20 = (bf16[4,64,1152]{2,1,0:T(8,128)(2,1)S(1)}, bf16[4,64,1152]{2,1,0:T(8,128)(2,1)}, u32[]{:S(2)}, u32[]{:S(2)}) collective-permute-start(bf16[4,64,1152]{2,1,0:T(8,128)(2,1)S(1)} %get-tuple-element.153), channel_id=1, source_target_pairs={{0,8},{1,9},{2,10},{3,11},{4,12},{5,13},{6,14},{7,15},{8,0},{9,1},... | collective-permute-start | bytes 1769480 | tf_op jit(solution)/shard_map/ppermute | solution.py:225
  55.1 15.9 %copy-start.12 = (f32[2,3,1152]{2,0,1:T(2,128)S(1)}, f32[2,3,1152]{2,0,1:T(2,128)}, u32[]{:S(2)}) copy-start(f32[2,3,1152]{2,0,1:T(2,128)} %param.13) | copy-start | bytes 82948
  55.7 24.7 %collective-permute-start.17 = (bf16[2,2,64,320]{3,2,1,0:T(8,128)(2,1)}, bf16[2,2,64,320]{3,2,1,0:T(8,128)(2,1)S(1)}, u32[]{:S(2)}, u32[]{:S(2)}) collective-permute-start(bf16[2,2,64,320]{3,2,1,0:T(8,128)(2,1)} %get-tuple-element.197), channel_id=1, source_target_pairs={{16,0},{17,1},{18,2},{19,3},{20,4},{21,5},{22,6},{23,7},{24,8},{25... | collective-permute-start | bytes 491528 | tf_op jit(solution)/shard_map/ppermute | solution.py:225
  57.0 23.4 %collective-permute-start.18 = (bf16[2,2,64,320]{3,2,1,0:T(8,128)(2,1)}, bf16[2,2,64,320]{3,2,1,0:T(8,128)(2,1)S(1)}, u32[]{:S(2)}, u32[]{:S(2)}) collective-permute-start(bf16[2,2,64,320]{3,2,1,0:T(8,128)(2,1)} %get-tuple-element.197), channel_id=1, source_target_pairs={{16,8},{17,9},{18,10},{19,11},{20,12},{21,13},{22,14},{23,15},{24,... | collective-permute-start | bytes 491528 | tf_op jit(solution)/shard_map/ppermute | solution.py:225
  71.0 9.4 %copy-start.2 = (f32[128,384]{1,0:T(8,128)S(1)}, f32[128,384]{1,0:T(8,128)}, u32[]{:S(2)}) copy-start(f32[128,384]{1,0:T(8,128)} %shard_map.67) | copy-start | bytes 589828
  71.0 9.4 %copy-start.5 = (bf16[2,64,1152]{2,1,0:T(8,128)(2,1)S(1)}, bf16[2,64,1152]{2,1,0:T(8,128)(2,1)}, u32[]{:S(2)}) copy-start(bf16[2,64,1152]{2,1,0:T(8,128)(2,1)} %copy-done.4) | copy-start | bytes 884740
  71.0 9.4 %copy-start.8 = (bf16[2,64,1152]{2,1,0:T(8,128)(2,1)S(1)}, bf16[2,64,1152]{2,1,0:T(8,128)(2,1)}, u32[]{:S(2)}) copy-start(bf16[2,64,1152]{2,1,0:T(8,128)(2,1)} %copy-done.7) | copy-start | bytes 884740
  71.0 7.6 %collective-permute-start.3 = (bf16[4,80,1152]{2,1,0:T(8,128)(2,1)}, bf16[4,80,1152]{2,1,0:T(8,128)(2,1)}, u32[]{:S(2)}, u32[]{:S(2)}) collective-permute-start(bf16[4,80,1152]{2,1,0:T(8,128)(2,1)} %get-tuple-element.98), channel_id=1, source_target_pairs={{0,1},{1,0},{2,3},{3,2},{4,5},{5,4},{6,7},{7,6},{8,9},{9,8},{10,11... | collective-permute-start | bytes 2211848 | tf_op jit(solution)/shard_map/cond/branch_0_fun/ppermute | solution.py:225
  73.8 4.8 %collective-permute-start.2 = (bf16[4,64,1152]{2,1,0:T(8,128)(2,1)}, bf16[4,64,1152]{2,1,0:T(8,128)(2,1)S(1)}, u32[]{:S(2)}, u32[]{:S(2)}) collective-permute-start(bf16[4,64,1152]{2,1,0:T(8,128)(2,1)} %get-tuple-element.97), channel_id=1, source_target_pairs={{0,1},{1,0},{2,3},{3,2},{4,5},{5,4},{6,7},{7,6},{8,9},{9,8},{10,11... | collective-permute-start | bytes 1769480 | tf_op jit(solution)/shard_map/cond/branch_0_fun/ppermute | solution.py:225
  80.4 3.0 %copy-start.6 = (bf16[4,64,1152]{2,1,0:T(8,128)(2,1)}, bf16[4,64,1152]{2,1,0:T(8,128)(2,1)S(1)}, u32[]{:S(2)}) copy-start(bf16[4,64,1152]{2,1,0:T(8,128)(2,1)S(1)} %get-tuple-element.122.zero_corner) | copy-start | bytes 1769476 | tf_op jit(solution)/shard_map/cond
  80.4 3.1 %copy-start.10 = (bf16[2,2,64,320]{3,2,1,0:T(8,128)(2,1)}, bf16[2,2,64,320]{3,2,1,0:T(8,128)(2,1)S(1)}, u32[]{:S(2)}) copy-start(bf16[2,2,64,320]{3,2,1,0:T(8,128)(2,1)S(1)} %get-tuple-element.116.cross) | copy-start | bytes 491524 | tf_op jit(solution)/shard_map/cond
  80.4 24.7 %collective-permute-start.9 = (bf16[4,80,1152]{2,1,0:T(8,128)(2,1)}, bf16[4,80,1152]{2,1,0:T(8,128)(2,1)S(1)}, u32[]{:S(2)}, u32[]{:S(2)}) collective-permute-start(bf16[4,80,1152]{2,1,0:T(8,128)(2,1)} %get-tuple-element.128.mine), channel_id=1, source_target_pairs={{0,8},{1,9},{2,10},{3,11},{4,12},{5,13},{6,14},{7,15},{8,0},{9,1},... | collective-permute-start | bytes 2211848 | tf_op jit(solution)/shard_map/cond/branch_0_fun/ppermute | solution.py:225
  90.0 10.0 %collective-permute-start.6 = (bf16[256,640]{1,0:T(8,128)(2,1)S(1)}, bf16[256,640]{1,0:T(8,128)(2,1)S(1)}, u32[]{:S(2)}, u32[]{:S(2)}) collective-permute-start(bf16[256,640]{1,0:T(8,128)(2,1)S(1)} %get-tuple-element.125.here), channel_id=1, source_target_pairs={{1,2},{2,1},{3,4},{4,3},{5,6},{6,5},{9,10},{10,9},{11,12},{12,11},... | collective-permute-start | bytes 983048 | tf_op jit(solution)/shard_map/cond/branch_0_fun/ppermute | solution.py:225
  95.3 4.7 %collective-permute-start.7 = (bf16[256,640]{1,0:T(8,128)(2,1)S(1)}, bf16[256,640]{1,0:T(8,128)(2,1)S(1)}, u32[]{:S(2)}, u32[]{:S(2)}) collective-permute-start(bf16[256,640]{1,0:T(8,128)(2,1)S(1)} %get-tuple-element.125.here), channel_id=1, source_target_pairs={{0,1},{1,0},{2,3},{3,2},{4,5},{5,4},{6,7},{7,6},{8,9},{9,8},{10,11... | collective-permute-start | bytes 983048 | tf_op jit(solution)/shard_map/cond/branch_0_fun/ppermute | solution.py:225
  102.7 5.8 %collective-permute-start.8 = (bf16[2,64,320]{2,1,0:T(8,128)(2,1)S(1)}, bf16[2,64,320]{2,1,0:T(8,128)(2,1)S(1)}, u32[]{:S(2)}, u32[]{:S(2)}) collective-permute-start(bf16[2,64,320]{2,1,0:T(8,128)(2,1)S(1)} %dynamic-slice_bitcast_fusion.1), channel_id=1, source_target_pairs={{0,8},{1,9},{2,10},{3,11},{4,12},{5,13},{6,14},{7,15},{8,0},{9,1},... | collective-permute-start | bytes 245768 | tf_op jit(solution)/shard_map/cond/branch_0_fun/ppermute | solution.py:225
  110.3 0.7 copy-start.9

commit v4 on v3

--- a/solution.py
+++ b/solution.py
@@ -229,7 +229,7 @@
     return lax.optimization_barrier((block,) + earlier)[0]
 
 
-def kernel_call(body, outs, args, scratch=(), copies=0, stay=False, micros=0, near=False):
+def kernel_call(body, outs, args, scratch=(), copies=0, stay=False, micros=0, near=False, room=16):
     def space(a):
         if a.dtype == jnp.int32:
             return pltpu.SMEM
@@ -242,7 +242,7 @@
         in_specs=[pl.BlockSpec(memory_space=space(a)) for a in args],
         out_specs=[pl.BlockSpec(memory_space=pl.ANY if stay else pltpu.VMEM) for _ in outs],
         scratch_shapes=buffers + ([pltpu.SemaphoreType.DMA((copies,))] if copies else []),
-        compiler_params=pltpu.CompilerParams(vmem_limit_bytes=32 * 1024 * 1024),
+        compiler_params=pltpu.CompilerParams(vmem_limit_bytes=room * 1024 * 1024),
         cost_estimate=pl.CostEstimate(
             flops=0, bytes_accessed=1 + 3_700_000 * micros, transcendentals=0
         ),
@@ -289,10 +289,9 @@
     finish(started)
 
 
-def norm_kernel(spot, own, far, mod, normed, first, second, done):
-    finish(begin([(own, first), (far, second)], done))
+def norm_kernel(spot, own, far, mod, normed):
     for image in range(own.shape[0]):
-        hidden = first[image].astype(jnp.float32) + second[image].astype(jnp.float32)
+        hidden = own[image].astype(jnp.float32) + far[image].astype(jnp.float32)
         normed[image] = modulate(hidden, mod)
 
 
@@ -362,13 +361,11 @@
     query[...] = projected[:, keyval.shape[1] :]
 
 
-def attend_kernel(spot, queries, outer, here, inner, bias, out, query_rows, keyvals, done):
+def attend_kernel(spot, queries, outer, here, inner, bias, out):
     scaling = math.log2(math.e) / math.sqrt(HD)
     tokens = bias.shape[0]
     images = out.shape[0] // tokens
-    copies = [(queries, query_rows)]
-    copies += [(part, keyvals.at[index]) for index, part in enumerate((outer, here, inner))]
-    finish(begin(copies, done))
+    parts = (outer, here, inner)
     key_lanes = queries.shape[1]
     first_key = here.shape[1] - key_lanes
     heads = out.shape[1] // SLOT
@@ -382,9 +379,9 @@
 
     for image in range(images):
         rows = slice(image * tokens, (image + 1) * tokens)
-        keys = jnp.concatenate([keyvals[n, rows, first_key:] for n in range(3)], axis=0)
-        values = jnp.concatenate([keyvals[n, rows, :value_lanes] for n in range(3)], axis=0)
-        query = query_rows[rows, :].astype(jnp.float32)
+        keys = jnp.concatenate([part[rows, first_key:] for part in parts], axis=0)
+        values = jnp.concatenate([part[rows, :value_lanes] for part in parts], axis=0)
+        query = queries[rows, :].astype(jnp.float32)
         split = [jnp.where(within(query_lane, head), query, 0.0) for head in range(heads)]
         scores = dot_rows(jnp.concatenate(split, axis=0).astype(jnp.bfloat16), keys)
         raised, sums = ([], [])
@@ -466,30 +463,24 @@
     query[...] = projected[:, keyval.shape[1] :]
 
 
-def final_kernel(
-    spot, attended, side, head_rows, own, more, mod, out, near, far, w_out, first, second, done
-):
+def final_kernel(spot, attended, side, head_rows, own, more, mod, out, result, done):
     row = spot[1]
     images = out.shape[0]
-    width = near.shape[2]
-    copies = [(head_rows, w_out), (own, first), (more, second), (side, far)]
-    copies += [(attended.at[image, row], near.at[image]) for image in range(images)]
-    finish(begin(copies, done))
-
-    def flat(ref):
-        return jnp.concatenate([ref[i] for i in range(images)], axis=0)
-
+    width = side.shape[2]
+    near = jnp.concatenate([attended[i, row] for i in range(images)], axis=0)
+    far = jnp.concatenate([side[i] for i in range(images)], axis=0)
     projected = jnp.dot(
-        flat(near), w_out[rows_at(row * width, width), :], preferred_element_type=jnp.float32
+        near, head_rows[rows_at(row * width, width), :], preferred_element_type=jnp.float32
     )
     projected += jnp.dot(
-        flat(far), w_out[rows_at((1 - row) * width, width), :], preferred_element_type=jnp.float32
+        far, head_rows[rows_at((1 - row) * width, width), :], preferred_element_type=jnp.float32
     )
     tokens = out.shape[1]
     for image in range(images):
         rows = slice(image * tokens, (image + 1) * tokens)
-        base = first[image].astype(jnp.float32) + second[image].astype(jnp.float32)
-        out[image] = (base + mod[2] * projected[rows]).astype(out.dtype)
+        base = own[image].astype(jnp.float32) + more[image].astype(jnp.float32)
+        result[image] = (base + mod[2] * projected[rows]).astype(out.dtype)
+    finish(begin([(result, out)], done))
 
 
 def paired_rows(sizes, latent, modulation, w_query, w_keyval, w_out, w_zero):
@@ -538,7 +529,6 @@
 
     tile_shape = (images, tile, D)
     head_shape = ((images, 2, tile, half), jnp.bfloat16)
-    half_head_shape = ((images, tile, half), jnp.bfloat16)
     stack_shape = ((4, SLOT, D), jnp.bfloat16)
     shared_shape = ((4, SHARED, D), jnp.bfloat16)
     rows_shape = ((2 * half, D), jnp.bfloat16)
@@ -567,7 +557,7 @@
     corner = send(started, sizes, lambda b, r, t: (0, 1 - r, t) if b == 1 else None)
     (normed,) = kernel_call(
         norm_kernel, [(tile_shape, jnp.bfloat16)], (spot, own, far, modulation[1]),
-        scratch=[(tile_shape, jnp.bfloat16), (tile_shape, jnp.bfloat16)], copies=2,
+        near=True,
     )
     (bias,) = kernel_call(
         functools.partial(bias_kernel, 2 * tile_rows, sizes[2] * tile_cols),
@@ -595,8 +585,7 @@
         (attended,) = kernel_call(
             attend_kernel, [((tokens, half), jnp.bfloat16)],
             (spot, query, outer, keyval, inner, bias),
-            scratch=[((tokens, lanes), jnp.bfloat16), ((3, tokens, 2 * half), jnp.bfloat16)],
-            copies=4, micros=8,
+            micros=8, near=True,
         )
         return attended.reshape(images, 2, tile, half)
 
@@ -615,16 +604,14 @@
         (out,) = kernel_call(
             final_kernel, [(tile_shape, jnp.bfloat16)],
             (spot, attended, side_heads, rows, own, more, mod),
-            scratch=[half_head_shape, half_head_shape, rows_shape]
-            + [(tile_shape, jnp.bfloat16), (tile_shape, jnp.bfloat16)],
-            copies=4 + images,
+            scratch=[(tile_shape, jnp.bfloat16)], copies=1, near=True, stay=True,
         )
         return out
 
     def control_attention():
         keyval, query = kernel_call(
             project_kernel, projections, (spot, normed, side, first, first_other),
-            scratch=[((2 * half + lanes, D), jnp.bfloat16), both_shape], micros=5, near=True,
+            scratch=[((2 * half + lanes, D), jnp.bfloat16), both_shape], micros=5, near=True, room=24,
         )
         attended = neighborhood(query, keyval, *halos(keyval, control_only))
         return attended
@@ -666,7 +653,7 @@
                 ((2 * half + lanes, D), jnp.bfloat16),
                 both_shape,
             ],
-            micros=8, near=True,
+            micros=8, near=True, room=32,
         )
         outer, inner = halos(keyval, base_only)
         attended = neighborhood(query, keyval, outer, inner)

time: 112 us -> 110 us (0.982)
  Pallas kernels: 18.1 us -> 16.7 us
    pallas_call x9, Pallas kernels: 18.1 us -> 16.7 us  [kernel_call(): pl.pallas_call(body, out_shape=[jax.ShapeDtypeStruct(shape, kind) for sha...]
where the time goes in v4:
time: 110 us; the launch traced here: 109 us
  waiting for transfers between devices  51.4 us (47%)
  starting transfers between devices  33.4 us (30%)
  Pallas kernels  16.7 us (15%)
  other arithmetic  4.54 us (4%)
  local copies, waits for them, and re-layouts  2.52 us (2%)
    ppermute x17, waiting for transfers between devices, send(): return lax.ppermute(block, AXES, routes(sizes, move))  51.4 us
    ppermute x17, starting transfers between devices, send(): return lax.ppermute(block, AXES, routes(sizes, move))  33.4 us
    pallas_call x9, Pallas kernels, kernel_call(): pl.pallas_call(body, out_shape=[jax.ShapeDtypeStruct(shape, kind) for sha...  16.7 us
    unnamed x21, local copies, waits for them, and re-layouts  2.35 us
    select_n x1, other arithmetic, base_prepare(): jnp.where(is_query, first_other[:, 2 * SLOT:], after(first, attended)[:,...  2.29 us
  transfers between devices with their start and end apart: 17, of which 10 were waited for; matrix products, arithmetic and copies ran while one was open for 2% of the time, Pallas kernels for 13%

profile of v4, /device:TPU:1, one launch (start us, length us, event | category | flops | bytes accessed | tf_op | source)
XLA Modules:
  0.0 109.1 jit_solution(15811586811731502120)
XLA Ops:
  3.2 2.1 %collective-permute-start.10 = (bf16[2,64,1152]{2,1,0:T(8,128)(2,1)S(1)}, bf16[2,64,1152]{2,1,0:T(8,128)(2,1)S(1)}, u32[]{:S(2)}, u32[]{:S(2)}) collective-permute-start(bf16[2,64,1152]{2,1,0:T(8,128)(2,1)S(1)} %bitcast.39), channel_id=1, source_target_pairs={{0,16},{1,17},{2,18},{3,19},{4,20},{5,21},{6,22},{7,23},{8,24},{9,... | collective-permute-start | bytes 884744 | tf_op jit(solution)/shard_map/ppermute | solution.py:225
  5.4 3.3 %collective-permute-start.13 = (bf16[240,1152]{1,0:T(8,128)(2,1)S(1)}, bf16[240,1152]{1,0:T(8,128)(2,1)S(1)}, u32[]{:S(2)}, u32[]{:S(2)}) collective-permute-start(bf16[240,1152]{1,0:T(8,128)(2,1)S(1)} %fusion.2.one), channel_id=1, source_target_pairs={{0,6},{1,7},{2,4},{3,5},{4,2},{5,3},{6,0},{7,1},{8,14},{9,15},{10,... | collective-permute-start | bytes 1658888 | tf_op jit(solution)/shard_map/ppermute | solution.py:225
  8.7 1.3 %collective-permute-start.12 = (bf16[2,64,1152]{2,1,0:T(8,128)(2,1)S(1)}, bf16[2,64,1152]{2,1,0:T(8,128)(2,1)S(1)}, u32[]{:S(2)}, u32[]{:S(2)}) collective-permute-start(bf16[2,64,1152]{2,1,0:T(8,128)(2,1)S(1)} %bitcast.40), channel_id=1, source_target_pairs={{16,8},{17,9},{18,10},{19,11},{20,12},{21,13},{22,14},{23,15},{24,... | collective-permute-start | bytes 884744 | tf_op jit(solution)/shard_map/ppermute | solution.py:225
  10.1 2.0 %collective-permute-done.10.far = bf16[2,64,1152]{2,1,0:T(8,128)(2,1)S(1)} collective-permute-done((bf16[2,64,1152]{2,1,0:T(8,128)(2,1)S(1)}, bf16[2,64,1152]{2,1,0:T(8,128)(2,1)S(1)}, u32[]{:S(2)}, u32[]{:S(2)}) %collective-permute-start.10) | collective-permute-done | bytes 294944 | tf_op jit(solution)/shard_map/ppermute | solution.py:225
  13.0 1.2 %collective-permute-start.11 = (bf16[2,64,1152]{2,1,0:T(8,128)(2,1)S(1)}, bf16[2,64,1152]{2,1,0:T(8,128)(2,1)S(1)}, u32[]{:S(2)}, u32[]{:S(2)}) collective-permute-start(bf16[2,64,1152]{2,1,0:T(8,128)(2,1)S(1)} %broadcast_select_fusion), channel_id=1, source_target_pairs={{0,8},{1,9},{2,10},{3,11},{4,12},{5,13},{6,14},{7,15},{8,0},{9,1},... | collective-permute-start | bytes 884744 | tf_op jit(solution)/shard_map/ppermute | solution.py:225
  14.2 1.3 %shard_map.67 = f32[128,384]{1,0:T(8,128)} custom-call(s32[5]{0:T(128)S(1)} %stack.26.spot), custom_call_target="tpu_custom_call" | custom-call | bytes 1 | tf_op jit(solution)/shard_map/pallas_call | solution.py:239
  15.5 3.3 %collective-permute-done.12 = bf16[2,64,1152]{2,1,0:T(8,128)(2,1)S(1)} collective-permute-done((bf16[2,64,1152]{2,1,0:T(8,128)(2,1)S(1)}, bf16[2,64,1152]{2,1,0:T(8,128)(2,1)S(1)}, u32[]{:S(2)}, u32[]{:S(2)}) %collective-permute-start.12) | collective-permute-done | bytes 294944 | tf_op jit(solution)/shard_map/ppermute | solution.py:225
  18.7 1.8 %collective-permute-done.13.two = bf16[240,1152]{1,0:T(8,128)(2,1)S(1)} collective-permute-done((bf16[240,1152]{1,0:T(8,128)(2,1)S(1)}, bf16[240,1152]{1,0:T(8,128)(2,1)S(1)}, u32[]{:S(2)}, u32[]{:S(2)}) %collective-permute-start.13) | collective-permute-done | bytes 552992 | tf_op jit(solution)/shard_map/ppermute | solution.py:225
  20.5 13.1 %collective-permute-done.14.three = bf16[240,1152]{1,0:T(8,128)(2,1)S(1)} collective-permute-done((bf16[240,1152]{1,0:T(8,128)(2,1)S(1)}, bf16[240,1152]{1,0:T(8,128)(2,1)S(1)}, u32[]{:S(2)}, u32[]{:S(2)}) %collective-permute-start.14) | collective-permute-done | bytes 552992 | tf_op jit(solution)/shard_map/ppermute | solution.py:225
  34.4 12.9 %collective-permute-done.15.four = bf16[240,1152]{1,0:T(8,128)(2,1)S(1)} collective-permute-done((bf16[240,1152]{1,0:T(8,128)(2,1)S(1)}, bf16[240,1152]{1,0:T(8,128)(2,1)S(1)}, u32[]{:S(2)}, u32[]{:S(2)}) %collective-permute-start.15) | collective-permute-done | bytes 552992 | tf_op jit(solution)/shard_map/ppermute | solution.py:225
  47.3 2.0 %shard_map.68 = (bf16[4,240,1152]{2,1,0:T(8,128)(2,1)}, bf16[4,80,1152]{2,1,0:T(8,128)(2,1)}, bf16[4,64,1152]{2,1,0:T(8,128)(2,1)S(1)}) custom-call(s32[5]{0:T(128)S(1)} %stack.26.spot, bf16[240,1152]{1,0:T(8,128)(2,1)S(1)} %fusion.2.one, bf16[240,1152]{1,0:T(8,128)(2,1)S(1)} %collective-permute-done.13.two, ...), custom_call_target="tpu_custom_call" | custom-call | bytes 1 | tf_op jit(solution)/shard_map/pallas_call | solution.py:239
  49.3 1.4 %collective-permute-start.16 = (bf16[4,240,1152]{2,1,0:T(8,128)(2,1)}, bf16[4,240,1152]{2,1,0:T(8,128)(2,1)}, u32[]{:S(2)}, u32[]{:S(2)}) collective-permute-start(bf16[4,240,1152]{2,1,0:T(8,128)(2,1)} %get-tuple-element.150), channel_id=1, source_target_pairs={{0,1},{1,0},{2,3},{3,2},{4,5},{5,4},{6,7},{7,6},{8,9},{9,8},{10,11... | collective-permute-start | bytes 6635528 | tf_op jit(solution)/shard_map/ppermute | solution.py:225
  50.7 1.3 %collective-permute-start.19 = (bf16[4,80,1152]{2,1,0:T(8,128)(2,1)}, bf16[4,80,1152]{2,1,0:T(8,128)(2,1)}, u32[]{:S(2)}, u32[]{:S(2)}) collective-permute-start(bf16[4,80,1152]{2,1,0:T(8,128)(2,1)} %get-tuple-element.152), channel_id=1, source_target_pairs={{16,0},{17,1},{18,2},{19,3},{20,4},{21,5},{22,6},{23,7},{24,8},{25... | collective-permute-start | bytes 2211848 | tf_op jit(solution)/shard_map/ppermute | solution.py:225
  52.0 3.1 %collective-permute-start.20 = (bf16[4,64,1152]{2,1,0:T(8,128)(2,1)S(1)}, bf16[4,64,1152]{2,1,0:T(8,128)(2,1)}, u32[]{:S(2)}, u32[]{:S(2)}) collective-permute-start(bf16[4,64,1152]{2,1,0:T(8,128)(2,1)S(1)} %get-tuple-element.153), channel_id=1, source_target_pairs={{0,8},{1,9},{2,10},{3,11},{4,12},{5,13},{6,14},{7,15},{8,0},{9,1},... | collective-permute-start | bytes 1769480 | tf_op jit(solution)/shard_map/ppermute | solution.py:225
  55.7 1.3 %collective-permute-start.17 = (bf16[2,2,64,320]{3,2,1,0:T(8,128)(2,1)}, bf16[2,2,64,320]{3,2,1,0:T(8,128)(2,1)S(1)}, u32[]{:S(2)}, u32[]{:S(2)}) collective-permute-start(bf16[2,2,64,320]{3,2,1,0:T(8,128)(2,1)} %get-tuple-element.197), channel_id=1, source_target_pairs={{16,0},{17,1},{18,2},{19,3},{20,4},{21,5},{22,6},{23,7},{24,8},{25... | collective-permute-start | bytes 491528 | tf_op jit(solution)/shard_map/ppermute | solution.py:225
  57.0 1.3 %collective-permute-start.18 = (bf16[2,2,64,320]{3,2,1,0:T(8,128)(2,1)}, bf16[2,2,64,320]{3,2,1,0:T(8,128)(2,1)S(1)}, u32[]{:S(2)}, u32[]{:S(2)}) collective-permute-start(bf16[2,2,64,320]{3,2,1,0:T(8,128)(2,1)} %get-tuple-element.197), channel_id=1, source_target_pairs={{16,8},{17,9},{18,10},{19,11},{20,12},{21,13},{22,14},{23,15},{24,... | collective-permute-start | bytes 491528 | tf_op jit(solution)/shard_map/ppermute | solution.py:225
  58.3 10.6 %collective-permute-done.20 = bf16[4,64,1152]{2,1,0:T(8,128)(2,1)} collective-permute-done((bf16[4,64,1152]{2,1,0:T(8,128)(2,1)S(1)}, bf16[4,64,1152]{2,1,0:T(8,128)(2,1)}, u32[]{:S(2)}, u32[]{:S(2)}) %collective-permute-start.20) | collective-permute-done | bytes 589856 | tf_op jit(solution)/shard_map/ppermute | solution.py:225
  68.9 2.1 %collective-permute-done.19 = bf16[4,80,1152]{2,1,0:T(8,128)(2,1)} collective-permute-done((bf16[4,80,1152]{2,1,0:T(8,128)(2,1)}, bf16[4,80,1152]{2,1,0:T(8,128)(2,1)}, u32[]{:S(2)}, u32[]{:S(2)}) %collective-permute-start.19) | collective-permute-done | bytes 737312 | tf_op jit(solution)/shard_map/ppermute | solution.py:225
  71.0 7.7 %conditional.4 = (bf16[4,64,1152]{2,1,0:T(8,128)(2,1)S(1)}, bf16[4,80,1152]{2,1,0:T(8,128)(2,1)}, bf16[4,80,1152]{2,1,0:T(8,128)(2,1)}, bf16[2,64,1152]{2,1,0:T(8,128)(2,1)S(1)}) conditional(s32[]{:T(128)} %convert_element_type.9, (bf16[4,64,1152]{2,1,0:T(8,128)(2,1)}, bf16[4,80,1152]{2,1,0:T(8,128)(2,1)}, pred[]{:T(512)}, ...), branch_computations={%region_2.3_spmd, %region_3.4_spmd} | conditional | flops 368640 | bytes 7520370 | solution.py:637
  71.0 2.8 %collective-permute-start.3 = (bf16[4,80,1152]{2,1,0:T(8,128)(2,1)}, bf16[4,80,1152]{2,1,0:T(8,128)(2,1)}, u32[]{:S(2)}, u32[]{:S(2)}) collective-permute-start(bf16[4,80,1152]{2,1,0:T(8,128)(2,1)} %get-tuple-element.98), channel_id=1, source_target_pairs={{0,1},{1,0},{2,3},{3,2},{4,5},{5,4},{6,7},{7,6},{8,9},{9,8},{10,11... | collective-permute-start | bytes 2211848 | tf_op jit(solution)/shard_map/cond/branch_0_fun/ppermute | solution.py:225
  73.8 1.9 %collective-permute-start.2 = (bf16[4,64,1152]{2,1,0:T(8,128)(2,1)}, bf16[4,64,1152]{2,1,0:T(8,128)(2,1)S(1)}, u32[]{:S(2)}, u32[]{:S(2)}) collective-permute-start(bf16[4,64,1152]{2,1,0:T(8,128)(2,1)} %get-tuple-element.97), channel_id=1, source_target_pairs={{0,1},{1,0},{2,3},{3,2},{4,5},{5,4},{6,7},{7,6},{8,9},{9,8},{10,11... | collective-permute-start | bytes 1769480 | tf_op jit(solution)/shard_map/cond/branch_0_fun/ppermute | solution.py:225
  76.3 2.3 %slice_select_fusion = bf16[4,80,1152]{2,1,0:T(8,128)(2,1)} fusion(bf16[4,240,1152]{2,1,0:T(8,128)(2,1)} %get-tuple-element.101, bf16[4,240,1152]{2,1,0:T(8,128)(2,1)} %get-tuple-element.100, pred[]{:T(512)} %get-tuple-element.99), kind=kLoop, calls=%fused_computation | loop fusion | flops 368640 | bytes 2211841 | tf_op jit(solution)/shard_map/cond/branch_0_fun/jit(_where)/select_n | solution.py:630
  79.8 28.6 %conditional.5 = (bf16[1,2,8,8,1152]{4,3,2,1,0:T(8,128)(2,1)S(1)}) conditional(s32[]{:T(128)} %convert_element_type.9, (f32[2,3,1152]{2,0,1:T(2,128)S(1)}, s32[5]{0:T(128)S(1)}, bf16[2,64,1152]{2,1,0:T(8,128)(2,1)S(1)}, bf16[2,64,1152]{2,1,0:T(8,128)(2,1)S(1)}, bf16[2,64,1152]{2,1,0:T(8,128)(2,1)S(1)}, /*index=5*/bf16[2,64,1152]{2,1,0:T(8,128)(2,1)S(1)}, ...), branch_computations={%region_4.5_spmd, %region_5.6_spmd} | conditional | flops 4 | bytes 68387600 | solution.py:663
  79.8 3.0 %collective-permute-start.9 = (bf16[4,80,1152]{2,1,0:T(8,128)(2,1)}, bf16[4,80,1152]{2,1,0:T(8,128)(2,1)S(1)}, u32[]{:S(2)}, u32[]{:S(2)}) collective-permute-start(bf16[4,80,1152]{2,1,0:T(8,128)(2,1)} %get-tuple-element.128.mine), channel_id=1, source_target_pairs={{0,8},{1,9},{2,10},{3,11},{4,12},{5,13},{6,14},{7,15},{8,0},{9,1},... | collective-permute-start | bytes 2211848 | tf_op jit(solution)/shard_map/cond/branch_0_fun/ppermute | solution.py:225
  82.8 6.6 %branch_0_fun.8 = (bf16[2,64,1152]{2,1,0:T(8,128)(2,1)S(1)}, bf16[256,640]{1,0:T(8,128)(2,1)S(1)}, bf16[256,384]{1,0:T(8,128)(2,1)S(1)}) custom-call(s32[5]{0:T(128)S(1)} %get-tuple-element.110.spot, bf16[2,64,1152]{2,1,0:T(8,128)(2,1)S(1)} %get-tuple-element.111.own, bf16[2,64,1152]{2,1,0:T(8,128)(2,1)S(1)} %get-tuple-element.112.far, ...), custom_call_target="tpu_custom_call" | custom-call | bytes 29600000 | tf_op jit(solution)/shard_map/cond/branch_0_fun/pallas_call | solution.py:239
  89.4 5.2 %collective-permute-start.6 = (bf16[256,640]{1,0:T(8,128)(2,1)S(1)}, bf16[256,640]{1,0:T(8,128)(2,1)S(1)}, u32[]{:S(2)}, u32[]{:S(2)}) collective-permute-start(bf16[256,640]{1,0:T(8,128)(2,1)S(1)} %get-tuple-element.125.here), channel_id=1, source_target_pairs={{1,2},{2,1},{3,4},{4,3},{5,6},{6,5},{9,10},{10,9},{11,12},{12,11},... | collective-permute-start | bytes 983048 | tf_op jit(solution)/shard_map/cond/branch_0_fun/ppermute | solution.py:225
  94.7 1.9 %collective-permute-start.7 = (bf16[256,640]{1,0:T(8,128)(2,1)S(1)}, bf16[256,640]{1,0:T(8,128)(2,1)S(1)}, u32[]{:S(2)}, u32[]{:S(2)}) collective-permute-start(bf16[256,640]{1,0:T(8,128)(2,1)S(1)} %get-tuple-element.125.here), channel_id=1, source_target_pairs={{0,1},{1,0},{2,3},{3,2},{4,5},{5,4},{6,7},{7,6},{8,9},{9,8},{10,11... | collective-permute-start | bytes 983048 | tf_op jit(solution)/shard_map/cond/branch_0_fun/ppermute | solution.py:225
  96.6 3.1 %collective-permute-done.6.outer = bf16[256,640]{1,0:T(8,128)(2,1)S(1)} collective-permute-done((bf16[256,640]{1,0:T(8,128)(2,1)S(1)}, bf16[256,640]{1,0:T(8,128)(2,1)S(1)}, u32[]{:S(2)}, u32[]{:S(2)}) %collective-permute-start.6) | collective-permute-done | bytes 327712 | tf_op jit(solution)/shard_map/cond/branch_0_fun/ppermute | solution.py:225
  99.7 2.0 %branch_0_fun.9 = bf16[256,320]{1,0:T(8,128)(2,1)S(1)} custom-call(s32[5]{0:T(128)S(1)} %get-tuple-element.110.spot, bf16[256,384]{1,0:T(8,128)(2,1)S(1)} %get-tuple-element.124.queries, bf16[256,640]{1,0:T(8,128)(2,1)S(1)} %collective-permute-done.6.outer, bf16[256,640]{1,0:T(8,128)(2,1)S(1)} %get-tuple-element.125.here, ...), custom_call_target="tpu_custom_call" | custom-call | bytes 29600000 | tf_op jit(solution)/shard_map/cond/branch_0_fun/pallas_call | solution.py:239
  101.8 2.2 %collective-permute-start.8 = (bf16[2,64,320]{2,1,0:T(8,128)(2,1)S(1)}, bf16[2,64,320]{2,1,0:T(8,128)(2,1)S(1)}, u32[]{:S(2)}, u32[]{:S(2)}) collective-permute-start(bf16[2,64,320]{2,1,0:T(8,128)(2,1)S(1)} %dynamic-slice_bitcast_fusion.1), channel_id=1, source_target_pairs={{0,8},{1,9},{2,10},{3,11},{4,12},{5,13},{6,14},{7,15},{8,0},{9,1},... | collective-permute-start | bytes 245768 | tf_op jit(solution)/shard_map/cond/branch_0_fun/ppermute | solution.py:225
  103.9 1.8 %branch_0_fun.10.head_rows = bf16[640,1152]{1,0:T(8,128)(2,1)S(1)} custom-call(s32[5]{0:T(128)S(1)} %get-tuple-element.110.spot, bf16[4,80,1152]{2,1,0:T(8,128)(2,1)} %get-tuple-element.128.mine, bf16[4,80,1152]{2,1,0:T(8,128)(2,1)S(1)} %collective-permute-done.9.other), custom_call_target="tpu_custom_call" | custom-call | bytes 1 | tf_op jit(solution)/shard_map/cond/branch_0_fun/pallas_call | solution.py:239
  105.8 1.5 %collective-permute-done.8.side = bf16[2,64,320]{2,1,0:T(8,128)(2,1)S(1)} collective-permute-done((bf16[2,64,320]{2,1,0:T(8,128)(2,1)S(1)}, bf16[2,64,320]{2,1,0:T(8,128)(2,1)S(1)}, u32[]{:S(2)}, u32[]{:S(2)}) %collective-permute-start.8) | collective-permute-done | bytes 81952 | tf_op jit(solution)/shard_map/cond/branch_0_fun/ppermute | solution.py:225
  (50 shorter events, 9.6 us)
Async XLA Ops:
  0.0 1.0 copy-start
  2.0 1.2 %copy-start.1 = (bf16[1,2,8,8,1152]{4,3,2,1,0:T(8,128)(2,1)S(1)}, bf16[1,2,8,8,1152]{4,3,2,1,0:T(8,128)(2,1)}, u32[]{:S(2)}) copy-start(bf16[1,2,8,8,1152]{4,3,2,1,0:T(8,128)(2,1)} %param.12) | copy-start | bytes 884740
  2.0 8.0 %copy-start.11 = (f32[2,3,1152]{2,0,1:T(2,128)S(1)}, f32[2,3,1152]{2,0,1:T(2,128)}, u32[]{:S(2)}) copy-start(f32[2,3,1152]{2,0,1:T(2,128)} %param.13) | copy-start | bytes 82948
  3.2 8.9 %collective-permute-start.10 = (bf16[2,64,1152]{2,1,0:T(8,128)(2,1)S(1)}, bf16[2,64,1152]{2,1,0:T(8,128)(2,1)S(1)}, u32[]{:S(2)}, u32[]{:S(2)}) collective-permute-start(bf16[2,64,1152]{2,1,0:T(8,128)(2,1)S(1)} %bitcast.39), channel_id=1, source_target_pairs={{0,16},{1,17},{2,18},{3,19},{4,20},{5,21},{6,22},{7,23},{8,24},{9,... | collective-permute-start | bytes 884744 | tf_op jit(solution)/shard_map/ppermute | solution.py:225
  5.4 15.1 %collective-permute-start.13 = (bf16[240,1152]{1,0:T(8,128)(2,1)S(1)}, bf16[240,1152]{1,0:T(8,128)(2,1)S(1)}, u32[]{:S(2)}, u32[]{:S(2)}) collective-permute-start(bf16[240,1152]{1,0:T(8,128)(2,1)S(1)} %fusion.2.one), channel_id=1, source_target_pairs={{0,6},{1,7},{2,4},{3,5},{4,2},{5,3},{6,0},{7,1},{8,14},{9,15},{10,... | collective-permute-start | bytes 1658888 | tf_op jit(solution)/shard_map/ppermute | solution.py:225
  8.7 24.9 %collective-permute-start.14 = (bf16[240,1152]{1,0:T(8,128)(2,1)S(1)}, bf16[240,1152]{1,0:T(8,128)(2,1)S(1)}, u32[]{:S(2)}, u32[]{:S(2)}) collective-permute-start(bf16[240,1152]{1,0:T(8,128)(2,1)S(1)} %fusion.2.one), channel_id=1, source_target_pairs={{0,2},{1,3},{2,0},{3,1},{4,6},{5,7},{6,4},{7,5},{8,10},{9,11},{10,... | collective-permute-start | bytes 1658888 | tf_op jit(solution)/shard_map/ppermute | solution.py:225
  8.7 10.0 %collective-permute-start.12 = (bf16[2,64,1152]{2,1,0:T(8,128)(2,1)S(1)}, bf16[2,64,1152]{2,1,0:T(8,128)(2,1)S(1)}, u32[]{:S(2)}, u32[]{:S(2)}) collective-permute-start(bf16[2,64,1152]{2,1,0:T(8,128)(2,1)S(1)} %bitcast.40), channel_id=1, source_target_pairs={{16,8},{17,9},{18,10},{19,11},{20,12},{21,13},{22,14},{23,15},{24,... | collective-permute-start | bytes 884744 | tf_op jit(solution)/shard_map/ppermute | solution.py:225
  13.0 20.7 %collective-permute-start.11 = (bf16[2,64,1152]{2,1,0:T(8,128)(2,1)S(1)}, bf16[2,64,1152]{2,1,0:T(8,128)(2,1)S(1)}, u32[]{:S(2)}, u32[]{:S(2)}) collective-permute-start(bf16[2,64,1152]{2,1,0:T(8,128)(2,1)S(1)} %broadcast_select_fusion), channel_id=1, source_target_pairs={{0,8},{1,9},{2,10},{3,11},{4,12},{5,13},{6,14},{7,15},{8,0},{9,1},... | collective-permute-start | bytes 884744 | tf_op jit(solution)/shard_map/ppermute | solution.py:225
  18.7 15.0 %copy-start.7 = (bf16[2,64,1152]{2,1,0:T(8,128)(2,1)}, bf16[2,64,1152]{2,1,0:T(8,128)(2,1)S(1)}, u32[]{:S(2)}) copy-start(bf16[2,64,1152]{2,1,0:T(8,128)(2,1)S(1)} %collective-permute-done.12) | copy-start | bytes 884740
  33.7 0.7 copy-start.4
  33.7 13.6 %collective-permute-start.15 = (bf16[240,1152]{1,0:T(8,128)(2,1)S(1)}, bf16[240,1152]{1,0:T(8,128)(2,1)S(1)}, u32[]{:S(2)}, u32[]{:S(2)}) collective-permute-start(bf16[240,1152]{1,0:T(8,128)(2,1)S(1)} %collective-permute-done.13.two), channel_id=1, source_target_pairs={{0,2},{1,3},{2,0},{3,1},{4,6},{5,7},{6,4},{7,5},{8,10},{9,11},{10,... | collective-permute-start | bytes 1658888 | tf_op jit(solution)/shard_map/ppermute | solution.py:225
  49.3 5.8 %collective-permute-start.16 = (bf16[4,240,1152]{2,1,0:T(8,128)(2,1)}, bf16[4,240,1152]{2,1,0:T(8,128)(2,1)}, u32[]{:S(2)}, u32[]{:S(2)}) collective-permute-start(bf16[4,240,1152]{2,1,0:T(8,128)(2,1)} %get-tuple-element.150), channel_id=1, source_target_pairs={{0,1},{1,0},{2,3},{3,2},{4,5},{5,4},{6,7},{7,6},{8,9},{9,8},{10,11... | collective-permute-start | bytes 6635528 | tf_op jit(solution)/shard_map/ppermute | solution.py:225
  50.7 20.3 %collective-permute-start.19 = (bf16[4,80,1152]{2,1,0:T(8,128)(2,1)}, bf16[4,80,1152]{2,1,0:T(8,128)(2,1)}, u32[]{:S(2)}, u32[]{:S(2)}) collective-permute-start(bf16[4,80,1152]{2,1,0:T(8,128)(2,1)} %get-tuple-element.152), channel_id=1, source_target_pairs={{16,0},{17,1},{18,2},{19,3},{20,4},{21,5},{22,6},{23,7},{24,8},{25... | collective-permute-start | bytes 2211848 | tf_op jit(solution)/shard_map/ppermute | solution.py:225
  52.0 16.9 %collective-permute-start.20 = (bf16[4,64,1152]{2,1,0:T(8,128)(2,1)S(1)}, bf16[4,64,1152]{2,1,0:T(8,128)(2,1)}, u32[]{:S(2)}, u32[]{:S(2)}) collective-permute-start(bf16[4,64,1152]{2,1,0:T(8,128)(2,1)S(1)} %get-tuple-element.153), channel_id=1, source_target_pairs={{0,8},{1,9},{2,10},{3,11},{4,12},{5,13},{6,14},{7,15},{8,0},{9,1},... | collective-permute-start | bytes 1769480 | tf_op jit(solution)/shard_map/ppermute | solution.py:225
  55.1 15.9 %copy-start.12 = (f32[2,3,1152]{2,0,1:T(2,128)S(1)}, f32[2,3,1152]{2,0,1:T(2,128)}, u32[]{:S(2)}) copy-start(f32[2,3,1152]{2,0,1:T(2,128)} %param.13) | copy-start | bytes 82948
  55.7 24.0 %collective-permute-start.17 = (bf16[2,2,64,320]{3,2,1,0:T(8,128)(2,1)}, bf16[2,2,64,320]{3,2,1,0:T(8,128)(2,1)S(1)}, u32[]{:S(2)}, u32[]{:S(2)}) collective-permute-start(bf16[2,2,64,320]{3,2,1,0:T(8,128)(2,1)} %get-tuple-element.197), channel_id=1, source_target_pairs={{16,0},{17,1},{18,2},{19,3},{20,4},{21,5},{22,6},{23,7},{24,8},{25... | collective-permute-start | bytes 491528 | tf_op jit(solution)/shard_map/ppermute | solution.py:225
  57.0 22.8 %collective-permute-start.18 = (bf16[2,2,64,320]{3,2,1,0:T(8,128)(2,1)}, bf16[2,2,64,320]{3,2,1,0:T(8,128)(2,1)S(1)}, u32[]{:S(2)}, u32[]{:S(2)}) collective-permute-start(bf16[2,2,64,320]{3,2,1,0:T(8,128)(2,1)} %get-tuple-element.197), channel_id=1, source_target_pairs={{16,8},{17,9},{18,10},{19,11},{20,12},{21,13},{22,14},{23,15},{24,... | collective-permute-start | bytes 491528 | tf_op jit(solution)/shard_map/ppermute | solution.py:225
  71.0 8.8 %copy-start.2 = (f32[128,384]{1,0:T(8,128)S(1)}, f32[128,384]{1,0:T(8,128)}, u32[]{:S(2)}) copy-start(f32[128,384]{1,0:T(8,128)} %shard_map.67) | copy-start | bytes 589828
  71.0 8.8 %copy-start.5 = (bf16[2,64,1152]{2,1,0:T(8,128)(2,1)S(1)}, bf16[2,64,1152]{2,1,0:T(8,128)(2,1)}, u32[]{:S(2)}) copy-start(bf16[2,64,1152]{2,1,0:T(8,128)(2,1)} %copy-done.4) | copy-start | bytes 884740
  71.0 8.8 %copy-start.8 = (bf16[2,64,1152]{2,1,0:T(8,128)(2,1)S(1)}, bf16[2,64,1152]{2,1,0:T(8,128)(2,1)}, u32[]{:S(2)}) copy-start(bf16[2,64,1152]{2,1,0:T(8,128)(2,1)} %copy-done.7) | copy-start | bytes 884740
  71.0 7.6 %collective-permute-start.3 = (bf16[4,80,1152]{2,1,0:T(8,128)(2,1)}, bf16[4,80,1152]{2,1,0:T(8,128)(2,1)}, u32[]{:S(2)}, u32[]{:S(2)}) collective-permute-start(bf16[4,80,1152]{2,1,0:T(8,128)(2,1)} %get-tuple-element.98), channel_id=1, source_target_pairs={{0,1},{1,0},{2,3},{3,2},{4,5},{5,4},{6,7},{7,6},{8,9},{9,8},{10,11... | collective-permute-start | bytes 2211848 | tf_op jit(solution)/shard_map/cond/branch_0_fun/ppermute | solution.py:225
  73.8 4.8 %collective-permute-start.2 = (bf16[4,64,1152]{2,1,0:T(8,128)(2,1)}, bf16[4,64,1152]{2,1,0:T(8,128)(2,1)S(1)}, u32[]{:S(2)}, u32[]{:S(2)}) collective-permute-start(bf16[4,64,1152]{2,1,0:T(8,128)(2,1)} %get-tuple-element.97), channel_id=1, source_target_pairs={{0,1},{1,0},{2,3},{3,2},{4,5},{5,4},{6,7},{7,6},{8,9},{9,8},{10,11... | collective-permute-start | bytes 1769480 | tf_op jit(solution)/shard_map/cond/branch_0_fun/ppermute | solution.py:225
  79.8 3.0 %copy-start.6 = (bf16[4,64,1152]{2,1,0:T(8,128)(2,1)}, bf16[4,64,1152]{2,1,0:T(8,128)(2,1)S(1)}, u32[]{:S(2)}) copy-start(bf16[4,64,1152]{2,1,0:T(8,128)(2,1)S(1)} %get-tuple-element.122.zero_corner) | copy-start | bytes 1769476 | tf_op jit(solution)/shard_map/cond
  79.8 3.1 %copy-start.10 = (bf16[2,2,64,320]{3,2,1,0:T(8,128)(2,1)}, bf16[2,2,64,320]{3,2,1,0:T(8,128)(2,1)S(1)}, u32[]{:S(2)}) copy-start(bf16[2,2,64,320]{3,2,1,0:T(8,128)(2,1)S(1)} %get-tuple-element.116.cross) | copy-start | bytes 491524 | tf_op jit(solution)/shard_map/cond
  79.8 24.1 %collective-permute-start.9 = (bf16[4,80,1152]{2,1,0:T(8,128)(2,1)}, bf16[4,80,1152]{2,1,0:T(8,128)(2,1)S(1)}, u32[]{:S(2)}, u32[]{:S(2)}) collective-permute-start(bf16[4,80,1152]{2,1,0:T(8,128)(2,1)} %get-tuple-element.128.mine), channel_id=1, source_target_pairs={{0,8},{1,9},{2,10},{3,11},{4,12},{5,13},{6,14},{7,15},{8,0},{9,1},... | collective-permute-start | bytes 2211848 | tf_op jit(solution)/shard_map/cond/branch_0_fun/ppermute | solution.py:225
  89.4 10.3 %collective-permute-start.6 = (bf16[256,640]{1,0:T(8,128)(2,1)S(1)}, bf16[256,640]{1,0:T(8,128)(2,1)S(1)}, u32[]{:S(2)}, u32[]{:S(2)}) collective-permute-start(bf16[256,640]{1,0:T(8,128)(2,1)S(1)} %get-tuple-element.125.here), channel_id=1, source_target_pairs={{1,2},{2,1},{3,4},{4,3},{5,6},{6,5},{9,10},{10,9},{11,12},{12,11},... | collective-permute-start | bytes 983048 | tf_op jit(solution)/shard_map/cond/branch_0_fun/ppermute | solution.py:225
  94.7 5.0 %collective-permute-start.7 = (bf16[256,640]{1,0:T(8,128)(2,1)S(1)}, bf16[256,640]{1,0:T(8,128)(2,1)S(1)}, u32[]{:S(2)}, u32[]{:S(2)}) collective-permute-start(bf16[256,640]{1,0:T(8,128)(2,1)S(1)} %get-tuple-element.125.here), channel_id=1, source_target_pairs={{0,1},{1,0},{2,3},{3,2},{4,5},{5,4},{6,7},{7,6},{8,9},{9,8},{10,11... | collective-permute-start | bytes 983048 | tf_op jit(solution)/shard_map/cond/branch_0_fun/ppermute | solution.py:225
  101.8 5.5 %collective-permute-start.8 = (bf16[2,64,320]{2,1,0:T(8,128)(2,1)S(1)}, bf16[2,64,320]{2,1,0:T(8,128)(2,1)S(1)}, u32[]{:S(2)}, u32[]{:S(2)}) collective-permute-start(bf16[2,64,320]{2,1,0:T(8,128)(2,1)S(1)} %dynamic-slice_bitcast_fusion.1), channel_id=1, source_target_pairs={{0,8},{1,9},{2,10},{3,11},{4,12},{5,13},{6,14},{7,15},{8,0},{9,1},... | collective-permute-start | bytes 245768 | tf_op jit(solution)/shard_map/cond/branch_0_fun/ppermute | solution.py:225
  108.4 0.7 copy-start.9

commit v5 on v4

--- a/solution.py
+++ b/solution.py
@@ -364,13 +364,15 @@
 def attend_kernel(spot, queries, outer, here, inner, bias, out):
     scaling = math.log2(math.e) / math.sqrt(HD)
     tokens = bias.shape[0]
-    images = out.shape[0] // tokens
+    images = queries.shape[0] // tokens
     parts = (outer, here, inner)
     key_lanes = queries.shape[1]
     first_key = here.shape[1] - key_lanes
-    heads = out.shape[1] // SLOT
+    width = out.shape[1] // images
+    heads = width // SLOT
+    results = []
     pad = key_lanes - heads * SLOT
-    value_lanes = (out.shape[1] + 127) // 128 * 128
+    value_lanes = (width + 127) // 128 * 128
     query_lane = lax.broadcasted_iota(jnp.int32, (tokens, key_lanes), 1) - pad
     value_lane = lax.broadcasted_iota(jnp.int32, (tokens, value_lanes), 1)
 
@@ -397,7 +399,8 @@
         for head in range(heads):
             part = blended[head * tokens : (head + 1) * tokens] * sums[head]
             total = jnp.where(within(value_lane, head), part, total)
-        out[rows, :] = total[:, : out.shape[1]].astype(out.dtype)
+        results.append(total[:, :width])
+    out[...] = jnp.concatenate(results, axis=1).astype(out.dtype)
 
 
 def head_rows_kernel(index, spot, mine, other, out, outs, done):
@@ -416,7 +419,7 @@
     row, link, core = (spot[1], spot[2], spot[3])
     images, tokens, _ = own.shape
     tile = images * tokens
-    width = near.shape[3]
+    width = near.shape[2] // images
     for block, at in ((out_mine, core), (out_other, 1 - core)):
         arrange_heads(link, block, at * width, w_out)
     shard = w_zero.shape[0] // 8
@@ -433,7 +436,10 @@
     arrange_queries(spot, first, first_other, 2, weight)
 
     def ordered(ref):
-        return jnp.concatenate([ref[i, s] for s in (row, 1 - row) for i in range(images)], axis=0)
+        parts = [
+            ref[s][:, i * width : (i + 1) * width] for s in (row, 1 - row) for i in range(images)
+        ]
+        return jnp.concatenate(parts, axis=0)
 
     def stacked(one, two):
         parts = [ref[i] for ref in (one, two) for i in range(images)]
@@ -466,9 +472,13 @@
 def final_kernel(spot, attended, side, head_rows, own, more, mod, out, result, done):
     row = spot[1]
     images = out.shape[0]
-    width = side.shape[2]
-    near = jnp.concatenate([attended[i, row] for i in range(images)], axis=0)
-    far = jnp.concatenate([side[i] for i in range(images)], axis=0)
+    width = side.shape[1] // images
+
+    def flat(block):
+        parts = [block[:, i * width : (i + 1) * width] for i in range(images)]
+        return jnp.concatenate(parts, axis=0)
+
+    near, far = (flat(attended[row]), flat(side[...]))
     projected = jnp.dot(
         near, head_rows[rows_at(row * width, width), :], preferred_element_type=jnp.float32
     )
@@ -528,7 +538,8 @@
         return tuple(kernel_call(unset_kernel, [out], (spot,), copies=1, stay=True)[0] for out in outs)
 
     tile_shape = (images, tile, D)
-    head_shape = ((images, 2, tile, half), jnp.bfloat16)
+    head_shape = ((2, tile, images * half), jnp.bfloat16)
+    half_head_shape = ((tile, images * half), jnp.bfloat16)
     stack_shape = ((4, SLOT, D), jnp.bfloat16)
     shared_shape = ((4, SHARED, D), jnp.bfloat16)
     rows_shape = ((2 * half, D), jnp.bfloat16)
@@ -583,14 +594,14 @@
 
     def neighborhood(query, keyval, outer, inner):
         (attended,) = kernel_call(
-            attend_kernel, [((tokens, half), jnp.bfloat16)],
+            attend_kernel, [((2 * tile, images * half), jnp.bfloat16)],
             (spot, query, outer, keyval, inner, bias),
             micros=8, near=True,
         )
-        return attended.reshape(images, 2, tile, half)
+        return attended.reshape(2, tile, images * half)
 
     def their_heads(attended, joins):
-        theirs = lax.dynamic_index_in_dim(attended, 1 - row, 1, keepdims=False)
+        theirs = lax.dynamic_index_in_dim(attended, 1 - row, 0, keepdims=False)
         return swap_rows(theirs, joins)
 
     def head_rows(index, mine, other):
@@ -623,8 +634,7 @@
     def control_finish():
         rows = head_rows(3, swap_cores(head_stack, control_only), head_stack)
         side_heads = their_heads(attended, control_only)
-        out = finished(attended, side_heads, rows, far, modulation[1])
-        return unset(shared_shape, stack_shape, stack_shape) + (out,)
+        return unset(shared_shape, stack_shape, stack_shape) + (rows, side_heads)
 
     def base_prepare():
         third = jnp.where(
@@ -632,9 +642,9 @@
         )
         zero_corner = swap_cores(zero_side, base_only)
         out_other = swap_cores(out_mine, base_only)
-        return (zero_corner, out_other, third) + unset((tile_shape, jnp.bfloat16))
-
-    zero_corner, out_other, third, control = lax.cond(
+        return (zero_corner, out_other, third) + unset(rows_shape, half_head_shape)
+
+    zero_corner, out_other, third, rows, side_heads = lax.cond(
         is_control, control_finish, base_prepare
     )
 
@@ -658,9 +668,13 @@
         outer, inner = halos(keyval, base_only)
         attended = neighborhood(query, keyval, outer, inner)
         side_heads = their_heads(attended, base_only)
-        return finished(attended, side_heads, head_rows(1, third, other), residue, modulation[0])
-
-    out = lax.cond(is_control, lambda: control, base_finish)
+        return attended, side_heads, head_rows(1, third, other), residue
+
+    attended, side_heads, rows, more = lax.cond(
+        is_control, lambda: (attended, side_heads, rows, far), base_finish
+    )
+    mod = jnp.where(is_control, modulation[1], modulation[0])
+    out = finished(attended, side_heads, rows, more, mod)
     return out.reshape(latent.shape)
 
 

time: 110 us -> 107 us (0.973)
  waiting for transfers between devices: 51.4 us -> 47.2 us
  Pallas kernels: 16.7 us -> 20.1 us
    ppermute x17, waiting for transfers between devices: 51.4 us -> 47.2 us  [send(): return lax.ppermute(block, AXES, routes(sizes, move))]
    pallas_call x9 -> x10, Pallas kernels: 16.7 us -> 20.1 us  [kernel_call(): pl.pallas_call(body, out_shape=[jax.ShapeDtypeStruct(shape, kind) for sha...]
    unnamed x21 -> x15, local copies, waits for them, and re-layouts: 2.35 us -> 0.98 us
  transfers between devices with their start and end apart: 17 -> 17, of which waited for: 10 -> 6; matrix products, arithmetic and copies ran while one was open for 2% -> 3% of each run, Pallas kernels for 13% -> 15%
where the time goes in v5:
time: 107 us; the launch traced here: 106 us
  waiting for transfers between devices  47.2 us (44%)
  starting transfers between devices  32.4 us (30%)
  Pallas kernels  20.1 us (19%)
  other arithmetic  4.6 us (4%)
  local copies, waits for them, and re-layouts  1.74 us (2%)
    ppermute x17, waiting for transfers between devices, send(): return lax.ppermute(block, AXES, routes(sizes, move))  47.2 us
    ppermute x17, starting transfers between devices, send(): return lax.ppermute(block, AXES, routes(sizes, move))  32.4 us
    pallas_call x10, Pallas kernels, kernel_call(): pl.pallas_call(body, out_shape=[jax.ShapeDtypeStruct(shape, kind) for sha...  20.1 us
    select_n x1, other arithmetic, base_prepare(): jnp.where(is_query, first_other[:, 2 * SLOT:], after(first, attended)[:,...  2.38 us
  transfers between devices with their start and end apart: 17, of which 6 were waited for; matrix products, arithmetic and copies ran while one was open for 3% of the time, Pallas kernels for 15%

profile of v5, /device:TPU:1, one launch (start us, length us, event | category | flops | bytes accessed | tf_op | source)
XLA Modules:
  0.0 106.4 jit_solution(2770039137368035353)
XLA Ops:
  1.0 1.0 bitcast_select_fusion.1
  2.0 1.1 %bitcast_select_fusion = (bf16[80,1152]{1,0:T(8,128)(2,1)S(1)}, bf16[80,1152]{1,0:T(8,128)(2,1)S(1)}) fusion(bf16[1152,144]{0,1:T(8,128)(2,1)} %param.17, s32[]{:T(128)S(6)} %select_n.74, pred[]{:T(512)S(6)} %eq.8, bf16[72,1152]{1,0:T(8,128)(2,1)S(1)} %bitcast_select_fusion.1, bf16[72,1152]{1,0:T(8,128)(2,1)} %bitcast.48), kind=kLoop, calls=%fused_computation.10 | loop fusion | flops 184320 | bytes 884741 | tf_op jit(solution)/shard_map/jit(_where)/select_n | solution.py:560
  3.2 4.2 %collective-permute-start.13 = (bf16[240,1152]{1,0:T(8,128)(2,1)S(1)}, bf16[240,1152]{1,0:T(8,128)(2,1)S(1)}, u32[]{:S(2)}, u32[]{:S(2)}) collective-permute-start(bf16[240,1152]{1,0:T(8,128)(2,1)S(1)} %fusion.2.one), channel_id=1, source_target_pairs={{0,6},{1,7},{2,4},{3,5},{4,2},{5,3},{6,0},{7,1},{8,14},{9,15},{10,... | collective-permute-start | bytes 1658888 | tf_op jit(solution)/shard_map/ppermute | solution.py:225
  7.4 1.2 %collective-permute-start.10 = (bf16[2,64,1152]{2,1,0:T(8,128)(2,1)S(1)}, bf16[2,64,1152]{2,1,0:T(8,128)(2,1)S(1)}, u32[]{:S(2)}, u32[]{:S(2)}) collective-permute-start(bf16[2,64,1152]{2,1,0:T(8,128)(2,1)S(1)} %bitcast.40), channel_id=1, source_target_pairs={{0,16},{1,17},{2,18},{3,19},{4,20},{5,21},{6,22},{7,23},{8,24},{9,... | collective-permute-start | bytes 884744 | tf_op jit(solution)/shard_map/ppermute | solution.py:225
  8.6 1.3 %collective-permute-start.12 = (bf16[2,64,1152]{2,1,0:T(8,128)(2,1)S(1)}, bf16[2,64,1152]{2,1,0:T(8,128)(2,1)S(1)}, u32[]{:S(2)}, u32[]{:S(2)}) collective-permute-start(bf16[2,64,1152]{2,1,0:T(8,128)(2,1)S(1)} %bitcast.41), channel_id=1, source_target_pairs={{16,8},{17,9},{18,10},{19,11},{20,12},{21,13},{22,14},{23,15},{24,... | collective-permute-start | bytes 884744 | tf_op jit(solution)/shard_map/ppermute | solution.py:225
  10.7 10.6 %collective-permute-done.10.far = bf16[2,64,1152]{2,1,0:T(8,128)(2,1)S(1)} collective-permute-done((bf16[2,64,1152]{2,1,0:T(8,128)(2,1)S(1)}, bf16[2,64,1152]{2,1,0:T(8,128)(2,1)S(1)}, u32[]{:S(2)}, u32[]{:S(2)}) %collective-permute-start.10) | collective-permute-done | bytes 294944 | tf_op jit(solution)/shard_map/ppermute | solution.py:225
  22.1 1.3 %collective-permute-start.11 = (bf16[2,64,1152]{2,1,0:T(8,128)(2,1)S(1)}, bf16[2,64,1152]{2,1,0:T(8,128)(2,1)}, u32[]{:S(2)}, u32[]{:S(2)}) collective-permute-start(bf16[2,64,1152]{2,1,0:T(8,128)(2,1)S(1)} %broadcast_select_fusion), channel_id=1, source_target_pairs={{0,8},{1,9},{2,10},{3,11},{4,12},{5,13},{6,14},{7,15},{8,0},{9,1},... | collective-permute-start | bytes 884744 | tf_op jit(solution)/shard_map/ppermute | solution.py:225
  23.4 1.3 %shard_map.65 = f32[128,384]{1,0:T(8,128)} custom-call(s32[5]{0:T(128)S(1)} %stack.26.spot), custom_call_target="tpu_custom_call" | custom-call | bytes 1 | tf_op jit(solution)/shard_map/pallas_call | solution.py:239
  24.8 7.6 %collective-permute-done.14.three = bf16[240,1152]{1,0:T(8,128)(2,1)S(1)} collective-permute-done((bf16[240,1152]{1,0:T(8,128)(2,1)S(1)}, bf16[240,1152]{1,0:T(8,128)(2,1)S(1)}, u32[]{:S(2)}, u32[]{:S(2)}) %collective-permute-start.14) | collective-permute-done | bytes 552992 | tf_op jit(solution)/shard_map/ppermute | solution.py:225
  32.7 13.2 %collective-permute-done.15.four = bf16[240,1152]{1,0:T(8,128)(2,1)S(1)} collective-permute-done((bf16[240,1152]{1,0:T(8,128)(2,1)S(1)}, bf16[240,1152]{1,0:T(8,128)(2,1)S(1)}, u32[]{:S(2)}, u32[]{:S(2)}) %collective-permute-start.15) | collective-permute-done | bytes 552992 | tf_op jit(solution)/shard_map/ppermute | solution.py:225
  46.0 2.0 %shard_map.66 = (bf16[4,240,1152]{2,1,0:T(8,128)(2,1)}, bf16[4,80,1152]{2,1,0:T(8,128)(2,1)}, bf16[4,64,1152]{2,1,0:T(8,128)(2,1)S(1)}) custom-call(s32[5]{0:T(128)S(1)} %stack.26.spot, bf16[240,1152]{1,0:T(8,128)(2,1)S(1)} %fusion.2.one, bf16[240,1152]{1,0:T(8,128)(2,1)S(1)} %collective-permute-done.13.two, ...), custom_call_target="tpu_custom_call" | custom-call | bytes 1 | tf_op jit(solution)/shard_map/pallas_call | solution.py:239
  47.9 1.4 %collective-permute-start.16 = (bf16[4,240,1152]{2,1,0:T(8,128)(2,1)}, bf16[4,240,1152]{2,1,0:T(8,128)(2,1)}, u32[]{:S(2)}, u32[]{:S(2)}) collective-permute-start(bf16[4,240,1152]{2,1,0:T(8,128)(2,1)} %get-tuple-element.147), channel_id=1, source_target_pairs={{0,1},{1,0},{2,3},{3,2},{4,5},{5,4},{6,7},{7,6},{8,9},{9,8},{10,11... | collective-permute-start | bytes 6635528 | tf_op jit(solution)/shard_map/ppermute | solution.py:225
  49.3 1.3 %collective-permute-start.19 = (bf16[4,80,1152]{2,1,0:T(8,128)(2,1)}, bf16[4,80,1152]{2,1,0:T(8,128)(2,1)}, u32[]{:S(2)}, u32[]{:S(2)}) collective-permute-start(bf16[4,80,1152]{2,1,0:T(8,128)(2,1)} %get-tuple-element.149), channel_id=1, source_target_pairs={{16,0},{17,1},{18,2},{19,3},{20,4},{21,5},{22,6},{23,7},{24,8},{25... | collective-permute-start | bytes 2211848 | tf_op jit(solution)/shard_map/ppermute | solution.py:225
  50.6 3.1 %collective-permute-start.20 = (bf16[4,64,1152]{2,1,0:T(8,128)(2,1)S(1)}, bf16[4,64,1152]{2,1,0:T(8,128)(2,1)}, u32[]{:S(2)}, u32[]{:S(2)}) collective-permute-start(bf16[4,64,1152]{2,1,0:T(8,128)(2,1)S(1)} %get-tuple-element.150), channel_id=1, source_target_pairs={{0,8},{1,9},{2,10},{3,11},{4,12},{5,13},{6,14},{7,15},{8,0},{9,1},... | collective-permute-start | bytes 1769480 | tf_op jit(solution)/shard_map/ppermute | solution.py:225
  54.4 1.3 %collective-permute-start.17 = (bf16[2,64,640]{2,1,0:T(8,128)(2,1)S(1)}, bf16[2,64,640]{2,1,0:T(8,128)(2,1)S(1)}, u32[]{:S(2)}, u32[]{:S(2)}) collective-permute-start(bf16[2,64,640]{2,1,0:T(8,128)(2,1)S(1)} %get-tuple-element.201), channel_id=1, source_target_pairs={{16,0},{17,1},{18,2},{19,3},{20,4},{21,5},{22,6},{23,7},{24,8},{25... | collective-permute-start | bytes 491528 | tf_op jit(solution)/shard_map/ppermute | solution.py:225
  55.7 1.3 %collective-permute-start.18 = (bf16[2,64,640]{2,1,0:T(8,128)(2,1)S(1)}, bf16[2,64,640]{2,1,0:T(8,128)(2,1)S(1)}, u32[]{:S(2)}, u32[]{:S(2)}) collective-permute-start(bf16[2,64,640]{2,1,0:T(8,128)(2,1)S(1)} %get-tuple-element.201), channel_id=1, source_target_pairs={{16,8},{17,9},{18,10},{19,11},{20,12},{21,13},{22,14},{23,15},{24,... | collective-permute-start | bytes 491528 | tf_op jit(solution)/shard_map/ppermute | solution.py:225
  57.0 10.6 %collective-permute-done.20 = bf16[4,64,1152]{2,1,0:T(8,128)(2,1)} collective-permute-done((bf16[4,64,1152]{2,1,0:T(8,128)(2,1)S(1)}, bf16[4,64,1152]{2,1,0:T(8,128)(2,1)}, u32[]{:S(2)}, u32[]{:S(2)}) %collective-permute-start.20) | collective-permute-done | bytes 589856 | tf_op jit(solution)/shard_map/ppermute | solution.py:225
  67.6 2.1 %collective-permute-done.19 = bf16[4,80,1152]{2,1,0:T(8,128)(2,1)} collective-permute-done((bf16[4,80,1152]{2,1,0:T(8,128)(2,1)}, bf16[4,80,1152]{2,1,0:T(8,128)(2,1)}, u32[]{:S(2)}, u32[]{:S(2)}) %collective-permute-start.19) | collective-permute-done | bytes 737312 | tf_op jit(solution)/shard_map/ppermute | solution.py:225
  69.6 8.3 %conditional.4 = (bf16[4,64,1152]{2,1,0:T(8,128)(2,1)}, bf16[4,80,1152]{2,1,0:T(8,128)(2,1)}, bf16[4,80,1152]{2,1,0:T(8,128)(2,1)}, bf16[640,1152]{1,0:T(8,128)(2,1)}, bf16[64,640]{1,0:T(8,128)(2,1)}) conditional(s32[]{:T(128)} %convert_element_type.9, (bf16[4,64,1152]{2,1,0:T(8,128)(2,1)}, bf16[4,80,1152]{2,1,0:T(8,128)(2,1)}, pred[]{:T(512)}, ...), branch_computations={%region_2.3_spmd, %region_3.4_spmd} | conditional | flops 368640 | bytes 7520379 | solution.py:647
  69.6 2.8 %collective-permute-start.3 = (bf16[4,80,1152]{2,1,0:T(8,128)(2,1)}, bf16[4,80,1152]{2,1,0:T(8,128)(2,1)}, u32[]{:S(2)}, u32[]{:S(2)}) collective-permute-start(bf16[4,80,1152]{2,1,0:T(8,128)(2,1)} %get-tuple-element.93), channel_id=1, source_target_pairs={{0,1},{1,0},{2,3},{3,2},{4,5},{5,4},{6,7},{7,6},{8,9},{9,8},{10,11... | collective-permute-start | bytes 2211848 | tf_op jit(solution)/shard_map/cond/branch_0_fun/ppermute | solution.py:225
  72.5 1.9 %collective-permute-start.2 = (bf16[4,64,1152]{2,1,0:T(8,128)(2,1)}, bf16[4,64,1152]{2,1,0:T(8,128)(2,1)}, u32[]{:S(2)}, u32[]{:S(2)}) collective-permute-start(bf16[4,64,1152]{2,1,0:T(8,128)(2,1)} %get-tuple-element.92), channel_id=1, source_target_pairs={{0,1},{1,0},{2,3},{3,2},{4,5},{5,4},{6,7},{7,6},{8,9},{9,8},{10,11... | collective-permute-start | bytes 1769480 | tf_op jit(solution)/shard_map/cond/branch_0_fun/ppermute | solution.py:225
  75.5 2.4 %slice_select_fusion = bf16[4,80,1152]{2,1,0:T(8,128)(2,1)} fusion(bf16[4,240,1152]{2,1,0:T(8,128)(2,1)} %get-tuple-element.96, bf16[4,240,1152]{2,1,0:T(8,128)(2,1)} %get-tuple-element.95, pred[]{:T(512)} %get-tuple-element.94), kind=kLoop, calls=%fused_computation | loop fusion | flops 368640 | bytes 2211841 | tf_op jit(solution)/shard_map/cond/branch_0_fun/jit(_where)/select_n | solution.py:640
  78.0 25.8 %conditional.5 = (bf16[2,64,640]{2,1,0:T(8,128)(2,1)S(1)}, bf16[64,640]{1,0:T(8,128)(2,1)S(1)}, bf16[640,1152]{1,0:T(8,128)(2,1)}, bf16[2,64,1152]{2,1,0:T(8,128)(2,1)}) conditional(s32[]{:T(128)} %convert_element_type.9, (f32[2,3,1152]{2,0,1:T(2,128)S(1)}, s32[5]{0:T(128)S(1)}, bf16[2,64,1152]{2,1,0:T(8,128)(2,1)S(1)}, ...), branch_computations={%region_4.5_spmd, %region_5.6_spmd} | conditional | flops 4 | bytes 65372912 | solution.py:673
  78.0 3.1 %collective-permute-start.9 = (bf16[4,80,1152]{2,1,0:T(8,128)(2,1)}, bf16[4,80,1152]{2,1,0:T(8,128)(2,1)S(1)}, u32[]{:S(2)}, u32[]{:S(2)}) collective-permute-start(bf16[4,80,1152]{2,1,0:T(8,128)(2,1)} %get-tuple-element.120.mine), channel_id=1, source_target_pairs={{0,8},{1,9},{2,10},{3,11},{4,12},{5,13},{6,14},{7,15},{8,0},{9,1},... | collective-permute-start | bytes 2211848 | tf_op jit(solution)/shard_map/cond/branch_0_fun/ppermute | solution.py:225
  81.1 6.6 %branch_0_fun.9 = (bf16[2,64,1152]{2,1,0:T(8,128)(2,1)}, bf16[256,640]{1,0:T(8,128)(2,1)S(1)}, bf16[256,384]{1,0:T(8,128)(2,1)S(1)}) custom-call(s32[5]{0:T(128)S(1)} %get-tuple-element.102.spot, bf16[2,64,1152]{2,1,0:T(8,128)(2,1)S(1)} %get-tuple-element.103.own, bf16[2,64,1152]{2,1,0:T(8,128)(2,1)S(1)} %get-tuple-element.104.far, ...), custom_call_target="tpu_custom_call" | custom-call | bytes 29600000 | tf_op jit(solution)/shard_map/cond/branch_0_fun/pallas_call | solution.py:239
  87.7 3.7 %collective-permute-start.6 = (bf16[256,640]{1,0:T(8,128)(2,1)S(1)}, bf16[256,640]{1,0:T(8,128)(2,1)S(1)}, u32[]{:S(2)}, u32[]{:S(2)}) collective-permute-start(bf16[256,640]{1,0:T(8,128)(2,1)S(1)} %get-tuple-element.117.here), channel_id=1, source_target_pairs={{1,2},{2,1},{3,4},{4,3},{5,6},{6,5},{9,10},{10,9},{11,12},{12,11},... | collective-permute-start | bytes 983048 | tf_op jit(solution)/shard_map/cond/branch_0_fun/ppermute | solution.py:225
  91.4 1.9 %collective-permute-start.7 = (bf16[256,640]{1,0:T(8,128)(2,1)S(1)}, bf16[256,640]{1,0:T(8,128)(2,1)S(1)}, u32[]{:S(2)}, u32[]{:S(2)}) collective-permute-start(bf16[256,640]{1,0:T(8,128)(2,1)S(1)} %get-tuple-element.117.here), channel_id=1, source_target_pairs={{0,1},{1,0},{2,3},{3,2},{4,5},{5,4},{6,7},{7,6},{8,9},{9,8},{10,11... | collective-permute-start | bytes 983048 | tf_op jit(solution)/shard_map/cond/branch_0_fun/ppermute | solution.py:225
  93.3 3.1 %collective-permute-done.6.outer = bf16[256,640]{1,0:T(8,128)(2,1)S(1)} collective-permute-done((bf16[256,640]{1,0:T(8,128)(2,1)S(1)}, bf16[256,640]{1,0:T(8,128)(2,1)S(1)}, u32[]{:S(2)}, u32[]{:S(2)}) %collective-permute-start.6) | collective-permute-done | bytes 327712 | tf_op jit(solution)/shard_map/cond/branch_0_fun/ppermute | solution.py:225
  96.4 2.1 %branch_0_fun.10 = bf16[128,640]{1,0:T(8,128)(2,1)S(1)} custom-call(s32[5]{0:T(128)S(1)} %get-tuple-element.102.spot, bf16[256,384]{1,0:T(8,128)(2,1)S(1)} %get-tuple-element.116.queries, bf16[256,640]{1,0:T(8,128)(2,1)S(1)} %collective-permute-done.6.outer, bf16[256,640]{1,0:T(8,128)(2,1)S(1)} %get-tuple-element.117.here, ...), custom_call_target="tpu_custom_call" | custom-call | bytes 29600000 | tf_op jit(solution)/shard_map/cond/branch_0_fun/pallas_call | solution.py:239
  98.6 2.2 %collective-permute-start.8 = (bf16[64,640]{1,0:T(8,128)(2,1)S(1)}, bf16[64,640]{1,0:T(8,128)(2,1)S(1)}, u32[]{:S(2)}, u32[]{:S(2)}) collective-permute-start(bf16[64,640]{1,0:T(8,128)(2,1)S(1)} %dynamic-slice_bitcast_fusion.1), channel_id=1, source_target_pairs={{0,8},{1,9},{2,10},{3,11},{4,12},{5,13},{6,14},{7,15},{8,0},{9,1},... | collective-permute-start | bytes 245768 | tf_op jit(solution)/shard_map/cond/branch_0_fun/ppermute | solution.py:225
  100.8 3.0 %branch_0_fun.11 = bf16[640,1152]{1,0:T(8,128)(2,1)} custom-call(s32[5]{0:T(128)S(1)} %get-tuple-element.102.spot, bf16[4,80,1152]{2,1,0:T(8,128)(2,1)} %get-tuple-element.120.mine, bf16[4,80,1152]{2,1,0:T(8,128)(2,1)S(1)} %collective-permute-done.9.other), custom_call_target="tpu_custom_call" | custom-call | bytes 1 | tf_op jit(solution)/shard_map/cond/branch_0_fun/pallas_call | solution.py:239
  103.8 2.7 %shard_map.67 = bf16[2,64,1152]{2,1,0:T(8,128)(2,1)} custom-call(s32[5]{0:T(128)S(1)} %stack.26.spot, bf16[2,64,640]{2,1,0:T(8,128)(2,1)S(1)} %get-tuple-element.156.attended, bf16[64,640]{1,0:T(8,128)(2,1)S(1)} %get-tuple-element.157.side, bf16[640,1152]{1,0:T(8,128)(2,1)} %get-tuple-element.158.head_rows, bf16[2,64,1152]{2,1,0:T(8,128)(2,1)S(1)} %bitcast.44, ...), custom_call_target="tpu_custom_call" | custom-call | bytes 1 | tf_op jit(solution)/shard_map/pallas_call | solution.py:239
  (42 shorter events, 5.3 us)
Async XLA Ops:
  0.0 1.0 copy-start
  0.0 7.4 %copy-start.1 = (bf16[1,2,8,8,1152]{4,3,2,1,0:T(8,128)(2,1)S(1)}, bf16[1,2,8,8,1152]{4,3,2,1,0:T(8,128)(2,1)}, u32[]{:S(2)}) copy-start(bf16[1,2,8,8,1152]{4,3,2,1,0:T(8,128)(2,1)} %param.12) | copy-start | bytes 884740
  0.0 9.9 %copy-start.6 = (f32[2,3,1152]{2,0,1:T(2,128)S(1)}, f32[2,3,1152]{2,0,1:T(2,128)}, u32[]{:S(2)}) copy-start(f32[2,3,1152]{2,0,1:T(2,128)} %param.13) | copy-start | bytes 82948
  3.2 21.6 %collective-permute-start.13 = (bf16[240,1152]{1,0:T(8,128)(2,1)S(1)}, bf16[240,1152]{1,0:T(8,128)(2,1)S(1)}, u32[]{:S(2)}, u32[]{:S(2)}) collective-permute-start(bf16[240,1152]{1,0:T(8,128)(2,1)S(1)} %fusion.2.one), channel_id=1, source_target_pairs={{0,6},{1,7},{2,4},{3,5},{4,2},{5,3},{6,0},{7,1},{8,14},{9,15},{10,... | collective-permute-start | bytes 1658888 | tf_op jit(solution)/shard_map/ppermute | solution.py:225
  7.4 24.9 %collective-permute-start.14 = (bf16[240,1152]{1,0:T(8,128)(2,1)S(1)}, bf16[240,1152]{1,0:T(8,128)(2,1)S(1)}, u32[]{:S(2)}, u32[]{:S(2)}) collective-permute-start(bf16[240,1152]{1,0:T(8,128)(2,1)S(1)} %fusion.2.one), channel_id=1, source_target_pairs={{0,2},{1,3},{2,0},{3,1},{4,6},{5,7},{6,4},{7,5},{8,10},{9,11},{10,... | collective-permute-start | bytes 1658888 | tf_op jit(solution)/shard_map/ppermute | solution.py:225
  7.4 13.9 %collective-permute-start.10 = (bf16[2,64,1152]{2,1,0:T(8,128)(2,1)S(1)}, bf16[2,64,1152]{2,1,0:T(8,128)(2,1)S(1)}, u32[]{:S(2)}, u32[]{:S(2)}) collective-permute-start(bf16[2,64,1152]{2,1,0:T(8,128)(2,1)S(1)} %bitcast.40), channel_id=1, source_target_pairs={{0,16},{1,17},{2,18},{3,19},{4,20},{5,21},{6,22},{7,23},{8,24},{9,... | collective-permute-start | bytes 884744 | tf_op jit(solution)/shard_map/ppermute | solution.py:225
  8.6 16.1 %collective-permute-start.12 = (bf16[2,64,1152]{2,1,0:T(8,128)(2,1)S(1)}, bf16[2,64,1152]{2,1,0:T(8,128)(2,1)S(1)}, u32[]{:S(2)}, u32[]{:S(2)}) collective-permute-start(bf16[2,64,1152]{2,1,0:T(8,128)(2,1)S(1)} %bitcast.41), channel_id=1, source_target_pairs={{16,8},{17,9},{18,10},{19,11},{20,12},{21,13},{22,14},{23,15},{24,... | collective-permute-start | bytes 884744 | tf_op jit(solution)/shard_map/ppermute | solution.py:225
  22.1 10.2 %collective-permute-start.11 = (bf16[2,64,1152]{2,1,0:T(8,128)(2,1)S(1)}, bf16[2,64,1152]{2,1,0:T(8,128)(2,1)}, u32[]{:S(2)}, u32[]{:S(2)}) collective-permute-start(bf16[2,64,1152]{2,1,0:T(8,128)(2,1)S(1)} %broadcast_select_fusion), channel_id=1, source_target_pairs={{0,8},{1,9},{2,10},{3,11},{4,12},{5,13},{6,14},{7,15},{8,0},{9,1},... | collective-permute-start | bytes 884744 | tf_op jit(solution)/shard_map/ppermute | solution.py:225
  24.8 8.0 %copy-start.4 = (bf16[2,64,1152]{2,1,0:T(8,128)(2,1)}, bf16[2,64,1152]{2,1,0:T(8,128)(2,1)S(1)}, u32[]{:S(2)}) copy-start(bf16[2,64,1152]{2,1,0:T(8,128)(2,1)S(1)} %collective-permute-done.12) | copy-start | bytes 884740
  32.3 13.6 %collective-permute-start.15 = (bf16[240,1152]{1,0:T(8,128)(2,1)S(1)}, bf16[240,1152]{1,0:T(8,128)(2,1)S(1)}, u32[]{:S(2)}, u32[]{:S(2)}) collective-permute-start(bf16[240,1152]{1,0:T(8,128)(2,1)S(1)} %collective-permute-done.13.two), channel_id=1, source_target_pairs={{0,2},{1,3},{2,0},{3,1},{4,6},{5,7},{6,4},{7,5},{8,10},{9,11},{10,... | collective-permute-start | bytes 1658888 | tf_op jit(solution)/shard_map/ppermute | solution.py:225
  47.9 5.8 %collective-permute-start.16 = (bf16[4,240,1152]{2,1,0:T(8,128)(2,1)}, bf16[4,240,1152]{2,1,0:T(8,128)(2,1)}, u32[]{:S(2)}, u32[]{:S(2)}) collective-permute-start(bf16[4,240,1152]{2,1,0:T(8,128)(2,1)} %get-tuple-element.147), channel_id=1, source_target_pairs={{0,1},{1,0},{2,3},{3,2},{4,5},{5,4},{6,7},{7,6},{8,9},{9,8},{10,11... | collective-permute-start | bytes 6635528 | tf_op jit(solution)/shard_map/ppermute | solution.py:225
  49.3 20.3 %collective-permute-start.19 = (bf16[4,80,1152]{2,1,0:T(8,128)(2,1)}, bf16[4,80,1152]{2,1,0:T(8,128)(2,1)}, u32[]{:S(2)}, u32[]{:S(2)}) collective-permute-start(bf16[4,80,1152]{2,1,0:T(8,128)(2,1)} %get-tuple-element.149), channel_id=1, source_target_pairs={{16,0},{17,1},{18,2},{19,3},{20,4},{21,5},{22,6},{23,7},{24,8},{25... | collective-permute-start | bytes 2211848 | tf_op jit(solution)/shard_map/ppermute | solution.py:225
  50.6 16.9 %collective-permute-start.20 = (bf16[4,64,1152]{2,1,0:T(8,128)(2,1)S(1)}, bf16[4,64,1152]{2,1,0:T(8,128)(2,1)}, u32[]{:S(2)}, u32[]{:S(2)}) collective-permute-start(bf16[4,64,1152]{2,1,0:T(8,128)(2,1)S(1)} %get-tuple-element.150), channel_id=1, source_target_pairs={{0,8},{1,9},{2,10},{3,11},{4,12},{5,13},{6,14},{7,15},{8,0},{9,1},... | collective-permute-start | bytes 1769480 | tf_op jit(solution)/shard_map/ppermute | solution.py:225
  53.8 3.2 %copy-start.7 = (f32[1,3,1152]{2,0,1:T(1,128)S(1)}, f32[1,3,1152]{2,0,1:T(1,128)}, u32[]{:S(2)}) copy-start(f32[1,3,1152]{2,0,1:T(1,128)} %get-tuple-element.181) | copy-start | bytes 41476
  54.4 23.6 %collective-permute-start.17 = (bf16[2,64,640]{2,1,0:T(8,128)(2,1)S(1)}, bf16[2,64,640]{2,1,0:T(8,128)(2,1)S(1)}, u32[]{:S(2)}, u32[]{:S(2)}) collective-permute-start(bf16[2,64,640]{2,1,0:T(8,128)(2,1)S(1)} %get-tuple-element.201), channel_id=1, source_target_pairs={{16,0},{17,1},{18,2},{19,3},{20,4},{21,5},{22,6},{23,7},{24,8},{25... | collective-permute-start | bytes 491528 | tf_op jit(solution)/shard_map/ppermute | solution.py:225
  55.7 22.3 %collective-permute-start.18 = (bf16[2,64,640]{2,1,0:T(8,128)(2,1)S(1)}, bf16[2,64,640]{2,1,0:T(8,128)(2,1)S(1)}, u32[]{:S(2)}, u32[]{:S(2)}) collective-permute-start(bf16[2,64,640]{2,1,0:T(8,128)(2,1)S(1)} %get-tuple-element.201), channel_id=1, source_target_pairs={{16,8},{17,9},{18,10},{19,11},{20,12},{21,13},{22,14},{23,15},{24,... | collective-permute-start | bytes 491528 | tf_op jit(solution)/shard_map/ppermute | solution.py:225
  69.6 8.3 %copy-start.2 = (f32[128,384]{1,0:T(8,128)S(1)}, f32[128,384]{1,0:T(8,128)}, u32[]{:S(2)}) copy-start(f32[128,384]{1,0:T(8,128)} %shard_map.65) | copy-start | bytes 589828
  69.6 8.3 %copy-start.5 = (bf16[2,64,1152]{2,1,0:T(8,128)(2,1)S(1)}, bf16[2,64,1152]{2,1,0:T(8,128)(2,1)}, u32[]{:S(2)}) copy-start(bf16[2,64,1152]{2,1,0:T(8,128)(2,1)} %copy-done.4) | copy-start | bytes 884740
  69.6 8.3 %collective-permute-start.3 = (bf16[4,80,1152]{2,1,0:T(8,128)(2,1)}, bf16[4,80,1152]{2,1,0:T(8,128)(2,1)}, u32[]{:S(2)}, u32[]{:S(2)}) collective-permute-start(bf16[4,80,1152]{2,1,0:T(8,128)(2,1)} %get-tuple-element.93), channel_id=1, source_target_pairs={{0,1},{1,0},{2,3},{3,2},{4,5},{5,4},{6,7},{7,6},{8,9},{9,8},{10,11... | collective-permute-start | bytes 2211848 | tf_op jit(solution)/shard_map/cond/branch_0_fun/ppermute | solution.py:225
  72.5 5.4 %collective-permute-start.2 = (bf16[4,64,1152]{2,1,0:T(8,128)(2,1)}, bf16[4,64,1152]{2,1,0:T(8,128)(2,1)}, u32[]{:S(2)}, u32[]{:S(2)}) collective-permute-start(bf16[4,64,1152]{2,1,0:T(8,128)(2,1)} %get-tuple-element.92), channel_id=1, source_target_pairs={{0,1},{1,0},{2,3},{3,2},{4,5},{5,4},{6,7},{7,6},{8,9},{9,8},{10,11... | collective-permute-start | bytes 1769480 | tf_op jit(solution)/shard_map/cond/branch_0_fun/ppermute | solution.py:225
  78.0 22.8 %collective-permute-start.9 = (bf16[4,80,1152]{2,1,0:T(8,128)(2,1)}, bf16[4,80,1152]{2,1,0:T(8,128)(2,1)S(1)}, u32[]{:S(2)}, u32[]{:S(2)}) collective-permute-start(bf16[4,80,1152]{2,1,0:T(8,128)(2,1)} %get-tuple-element.120.mine), channel_id=1, source_target_pairs={{0,8},{1,9},{2,10},{3,11},{4,12},{5,13},{6,14},{7,15},{8,0},{9,1},... | collective-permute-start | bytes 2211848 | tf_op jit(solution)/shard_map/cond/branch_0_fun/ppermute | solution.py:225
  87.7 8.7 %collective-permute-start.6 = (bf16[256,640]{1,0:T(8,128)(2,1)S(1)}, bf16[256,640]{1,0:T(8,128)(2,1)S(1)}, u32[]{:S(2)}, u32[]{:S(2)}) collective-permute-start(bf16[256,640]{1,0:T(8,128)(2,1)S(1)} %get-tuple-element.117.here), channel_id=1, source_target_pairs={{1,2},{2,1},{3,4},{4,3},{5,6},{6,5},{9,10},{10,9},{11,12},{12,11},... | collective-permute-start | bytes 983048 | tf_op jit(solution)/shard_map/cond/branch_0_fun/ppermute | solution.py:225
  91.4 5.0 %collective-permute-start.7 = (bf16[256,640]{1,0:T(8,128)(2,1)S(1)}, bf16[256,640]{1,0:T(8,128)(2,1)S(1)}, u32[]{:S(2)}, u32[]{:S(2)}) collective-permute-start(bf16[256,640]{1,0:T(8,128)(2,1)S(1)} %get-tuple-element.117.here), channel_id=1, source_target_pairs={{0,1},{1,0},{2,3},{3,2},{4,5},{5,4},{6,7},{7,6},{8,9},{9,8},{10,11... | collective-permute-start | bytes 983048 | tf_op jit(solution)/shard_map/cond/branch_0_fun/ppermute | solution.py:225
  98.6 5.2 %collective-permute-start.8 = (bf16[64,640]{1,0:T(8,128)(2,1)S(1)}, bf16[64,640]{1,0:T(8,128)(2,1)S(1)}, u32[]{:S(2)}, u32[]{:S(2)}) collective-permute-start(bf16[64,640]{1,0:T(8,128)(2,1)S(1)} %dynamic-slice_bitcast_fusion.1), channel_id=1, source_target_pairs={{0,8},{1,9},{2,10},{3,11},{4,12},{5,13},{6,14},{7,15},{8,0},{9,1},... | collective-permute-start | bytes 245768 | tf_op jit(solution)/shard_map/cond/branch_0_fun/ppermute | solution.py:225

commit v6 on v5

--- a/solution.py
+++ b/solution.py
@@ -314,7 +314,7 @@
     bias[...] = jnp.where(inside, 0.0, -1e30)
 
 
-def unset_kernel(spot, out, done):
+def unset_kernel(*refs):
     pass
 
 
@@ -535,7 +535,7 @@
         return jnp.concatenate([block, other], axis=0)
 
     def unset(*outs):
-        return tuple(kernel_call(unset_kernel, [out], (spot,), copies=1, stay=True)[0] for out in outs)
+        return tuple(kernel_call(unset_kernel, list(outs), (spot,), copies=1, stay=True))
 
     tile_shape = (images, tile, D)
     head_shape = ((2, tile, images * half), jnp.bfloat16)
@@ -563,20 +563,20 @@
         axis=0,
     )
     first = [piece, swap_links(piece, ORDER[1]), swap_links(piece, ORDER[2])]
-    started = after(own, piece)
+    (bias,) = kernel_call(
+        functools.partial(bias_kernel, 2 * tile_rows, sizes[2] * tile_cols),
+        [((2 * tile, 6 * tile), jnp.float32)], (spot,), copies=1,
+    )
+    started = after(own, piece, bias)
     far = send(started, sizes, lambda b, r, t: (1 - b, r, t))
     corner = send(started, sizes, lambda b, r, t: (0, 1 - r, t) if b == 1 else None)
     (normed,) = kernel_call(
         norm_kernel, [(tile_shape, jnp.bfloat16)], (spot, own, far, modulation[1]),
         near=True,
     )
-    (bias,) = kernel_call(
-        functools.partial(bias_kernel, 2 * tile_rows, sizes[2] * tile_cols),
-        [((2 * tile, 6 * tile), jnp.float32)], (spot,), copies=1,
-    )
     side = swap_rows(jnp.where(is_control, normed, own))
+    first.append(swap_links(first[1], ORDER[2]))
     side, corner, bias, *first = lax.optimization_barrier((side, corner, bias, *first))
-    first.append(swap_links(first[1], ORDER[2]))
     first, head_stack, shared = kernel_call(
         stack_kernel, [triple_shape, stack_shape, shared_shape], (spot, *first),
         copies=8, stay=True,
@@ -625,26 +625,27 @@
             scratch=[((2 * half + lanes, D), jnp.bfloat16), both_shape], micros=5, near=True, room=24,
         )
         attended = neighborhood(query, keyval, *halos(keyval, control_only))
-        return attended
-
-    attended = lax.cond(is_control, control_attention, lambda: unset(head_shape)[0])
+        return (attended,) + unset(stack_shape)
+
+    def base_third():
+        third = jnp.where(is_query, first_other[:, 2 * SLOT :], first[:, 2 * SLOT :])
+        return unset(head_shape) + (third,)
+
+    attended, third = lax.cond(is_control, control_attention, base_third)
     near = send(attended, sizes, lambda b, r, t: (0, r, t) if b == 1 else None)
     cross = send(attended, sizes, lambda b, r, t: (0, 1 - r, t) if b == 1 else None)
 
     def control_finish():
         rows = head_rows(3, swap_cores(head_stack, control_only), head_stack)
         side_heads = their_heads(attended, control_only)
-        return unset(shared_shape, stack_shape, stack_shape) + (rows, side_heads)
+        return unset(shared_shape, stack_shape) + (rows, side_heads)
 
     def base_prepare():
-        third = jnp.where(
-            is_query, first_other[:, 2 * SLOT :], after(first, attended)[:, 2 * SLOT :]
-        )
         zero_corner = swap_cores(zero_side, base_only)
         out_other = swap_cores(out_mine, base_only)
-        return (zero_corner, out_other, third) + unset(rows_shape, half_head_shape)
-
-    zero_corner, out_other, third, rows, side_heads = lax.cond(
+        return (zero_corner, out_other) + unset(rows_shape, half_head_shape)
+
+    zero_corner, out_other, rows, side_heads = lax.cond(
         is_control, control_finish, base_prepare
     )
 

time: 107 us -> 105 us (0.981)
  waiting for transfers between devices: 47.2 us -> 36.9 us
  starting transfers between devices: 32.4 us -> 41 us
    ppermute x17, waiting for transfers between devices: 47.2 us -> 36.9 us  [send(): return lax.ppermute(block, AXES, routes(sizes, move))]
    ppermute x17, starting transfers between devices: 32.4 us -> 41 us  [send(): return lax.ppermute(block, AXES, routes(sizes, move))]
    pallas_call x10 -> x9, Pallas kernels: 20.1 us -> 19.5 us  [kernel_call(): pl.pallas_call(body, out_shape=[jax.ShapeDtypeStruct(shape, kind) for sha...]
  transfers between devices with their start and end apart: 17 -> 17, of which waited for: 6 -> 10; matrix products, arithmetic and copies ran while one was open for 3% -> 3% of each run, Pallas kernels for 15% -> 14%
where the time goes in v6:
time: 105 us
  starting transfers between devices  41 us (39%)
  waiting for transfers between devices  36.9 us (35%)
  Pallas kernels  19.5 us (19%)
  other arithmetic  4.63 us (4%)
  local copies, waits for them, and re-layouts  2.47 us (2%)
    ppermute x17, starting transfers between devices, send(): return lax.ppermute(block, AXES, routes(sizes, move))  41 us
    ppermute x17, waiting for transfers between devices, send(): return lax.ppermute(block, AXES, routes(sizes, move))  36.9 us
    pallas_call x9, Pallas kernels, kernel_call(): pl.pallas_call(body, out_shape=[jax.ShapeDtypeStruct(shape, kind) for sha...  19.5 us
    select_n x1, other arithmetic, base_third(): third = jnp.where(is_query, first_other[:, 2 * SLOT:], first[:, 2 * SLOT:])  2.37 us
  transfers between devices with their start and end apart: 17, of which 10 were waited for; matrix products, arithmetic and copies ran while one was open for 3% of the time, Pallas kernels for 14%

profile of v6, /device:TPU:1, one launch (start us, length us, event | category | flops | bytes accessed | tf_op | source)
XLA Modules:
  0.0 104.9 jit_solution(6908740117897648020)
XLA Ops:
  3.2 4.2 %collective-permute-start.13 = (bf16[240,1152]{1,0:T(8,128)(2,1)S(1)}, bf16[240,1152]{1,0:T(8,128)(2,1)S(1)}, u32[]{:S(2)}, u32[]{:S(2)}) collective-permute-start(bf16[240,1152]{1,0:T(8,128)(2,1)S(1)} %fusion.2.one), channel_id=1, source_target_pairs={{0,6},{1,7},{2,4},{3,5},{4,2},{5,3},{6,0},{7,1},{8,14},{9,15},{10,... | collective-permute-start | bytes 1658888 | tf_op jit(solution)/shard_map/ppermute | solution.py:225
  7.5 1.3 %shard_map.64 = f32[128,384]{1,0:T(8,128)} custom-call(s32[5]{0:T(128)S(1)} %stack.23.spot), custom_call_target="tpu_custom_call" | custom-call | bytes 1 | tf_op jit(solution)/shard_map/pallas_call | solution.py:239
  8.9 1.3 %collective-permute-start.10 = (bf16[2,64,1152]{2,1,0:T(8,128)(2,1)S(1)}, bf16[2,64,1152]{2,1,0:T(8,128)(2,1)S(1)}, u32[]{:S(2)}, u32[]{:S(2)}) collective-permute-start(bf16[2,64,1152]{2,1,0:T(8,128)(2,1)S(1)} %bitcast.40), channel_id=1, source_target_pairs={{0,16},{1,17},{2,18},{3,19},{4,20},{5,21},{6,22},{7,23},{8,24},{9,... | collective-permute-start | bytes 884744 | tf_op jit(solution)/shard_map/ppermute | solution.py:225
  10.2 1.3 %collective-permute-start.12 = (bf16[2,64,1152]{2,1,0:T(8,128)(2,1)S(1)}, bf16[2,64,1152]{2,1,0:T(8,128)(2,1)S(1)}, u32[]{:S(2)}, u32[]{:S(2)}) collective-permute-start(bf16[2,64,1152]{2,1,0:T(8,128)(2,1)S(1)} %bitcast.41), channel_id=1, source_target_pairs={{16,8},{17,9},{18,10},{19,11},{20,12},{21,13},{22,14},{23,15},{24,... | collective-permute-start | bytes 884744 | tf_op jit(solution)/shard_map/ppermute | solution.py:225
  12.1 10.7 %collective-permute-done.10.far = bf16[2,64,1152]{2,1,0:T(8,128)(2,1)S(1)} collective-permute-done((bf16[2,64,1152]{2,1,0:T(8,128)(2,1)S(1)}, bf16[2,64,1152]{2,1,0:T(8,128)(2,1)S(1)}, u32[]{:S(2)}, u32[]{:S(2)}) %collective-permute-start.10) | collective-permute-done | bytes 294944 | tf_op jit(solution)/shard_map/ppermute | solution.py:225
  23.6 7.2 %collective-permute-start.15 = (bf16[240,1152]{1,0:T(8,128)(2,1)S(1)}, bf16[240,1152]{1,0:T(8,128)(2,1)S(1)}, u32[]{:S(2)}, u32[]{:S(2)}) collective-permute-start(bf16[240,1152]{1,0:T(8,128)(2,1)S(1)} %collective-permute-done.13.two), channel_id=1, source_target_pairs={{0,2},{1,3},{2,0},{3,1},{4,6},{5,7},{6,4},{7,5},{8,10},{9,11},{10,... | collective-permute-start | bytes 1658888 | tf_op jit(solution)/shard_map/ppermute | solution.py:225
  32.4 5.4 %collective-permute-done.11 = bf16[2,64,1152]{2,1,0:T(8,128)(2,1)S(1)} collective-permute-done((bf16[2,64,1152]{2,1,0:T(8,128)(2,1)S(1)}, bf16[2,64,1152]{2,1,0:T(8,128)(2,1)S(1)}, u32[]{:S(2)}, u32[]{:S(2)}) %collective-permute-start.11) | collective-permute-done | bytes 294944 | tf_op jit(solution)/shard_map/ppermute | solution.py:225
  38.5 4.6 %collective-permute-done.15.four = bf16[240,1152]{1,0:T(8,128)(2,1)S(1)} collective-permute-done((bf16[240,1152]{1,0:T(8,128)(2,1)S(1)}, bf16[240,1152]{1,0:T(8,128)(2,1)S(1)}, u32[]{:S(2)}, u32[]{:S(2)}) %collective-permute-start.15) | collective-permute-done | bytes 552992 | tf_op jit(solution)/shard_map/ppermute | solution.py:225
  43.1 2.0 %shard_map.66 = (bf16[4,240,1152]{2,1,0:T(8,128)(2,1)}, bf16[4,80,1152]{2,1,0:T(8,128)(2,1)}, bf16[4,64,1152]{2,1,0:T(8,128)(2,1)S(1)}) custom-call(s32[5]{0:T(128)S(1)} %stack.23.spot, bf16[240,1152]{1,0:T(8,128)(2,1)S(1)} %fusion.2.one, bf16[240,1152]{1,0:T(8,128)(2,1)S(1)} %collective-permute-done.13.two, ...), custom_call_target="tpu_custom_call" | custom-call | bytes 1 | tf_op jit(solution)/shard_map/pallas_call | solution.py:239
  45.1 1.7 %collective-permute-start.16 = (bf16[4,240,1152]{2,1,0:T(8,128)(2,1)}, bf16[4,240,1152]{2,1,0:T(8,128)(2,1)}, u32[]{:S(2)}, u32[]{:S(2)}) collective-permute-start(bf16[4,240,1152]{2,1,0:T(8,128)(2,1)} %get-tuple-element.152), channel_id=1, source_target_pairs={{0,1},{1,0},{2,3},{3,2},{4,5},{5,4},{6,7},{7,6},{8,9},{9,8},{10,11... | collective-permute-start | bytes 6635528 | tf_op jit(solution)/shard_map/ppermute | solution.py:225
  46.8 1.3 %collective-permute-start.19 = (bf16[4,80,1152]{2,1,0:T(8,128)(2,1)}, bf16[4,80,1152]{2,1,0:T(8,128)(2,1)}, u32[]{:S(2)}, u32[]{:S(2)}) collective-permute-start(bf16[4,80,1152]{2,1,0:T(8,128)(2,1)} %get-tuple-element.155), channel_id=1, source_target_pairs={{16,0},{17,1},{18,2},{19,3},{20,4},{21,5},{22,6},{23,7},{24,8},{25... | collective-permute-start | bytes 2211848 | tf_op jit(solution)/shard_map/ppermute | solution.py:225
  48.1 3.1 %collective-permute-start.20 = (bf16[4,64,1152]{2,1,0:T(8,128)(2,1)S(1)}, bf16[4,64,1152]{2,1,0:T(8,128)(2,1)S(1)}, u32[]{:S(2)}, u32[]{:S(2)}) collective-permute-start(bf16[4,64,1152]{2,1,0:T(8,128)(2,1)S(1)} %get-tuple-element.156), channel_id=1, source_target_pairs={{0,8},{1,9},{2,10},{3,11},{4,12},{5,13},{6,14},{7,15},{8,0},{9,1},... | collective-permute-start | bytes 1769480 | tf_op jit(solution)/shard_map/ppermute | solution.py:225
  51.2 2.9 %conditional.3 = (bf16[2,64,640]{2,1,0:T(8,128)(2,1)S(1)}, bf16[4,80,1152]{2,1,0:T(8,128)(2,1)}) conditional(s32[]{:T(128)} %convert_element_type.9, (s32[5]{0:T(128)S(1)}, pred[]{:T(512)}, bf16[4,240,1152]{2,1,0:T(8,128)(2,1)}, bf16[4,240,1152]{2,1,0:T(8,128)(2,1)}) %tuple.32, (s32[5]{0:T(128)S(1)}, bf16[2,64,1152]{2,1,0:T(8,128)(2,1)S(1)}, ...), branch_computations={%region_0.1_spmd, %region_1.2_spmd} | conditional | flops 368640 | bytes 51507996 | solution.py:634
  51.2 2.4 %slice_select_fusion = bf16[4,80,1152]{2,1,0:T(8,128)(2,1)} fusion(bf16[4,240,1152]{2,1,0:T(8,128)(2,1)} %get-tuple-element.84, bf16[4,240,1152]{2,1,0:T(8,128)(2,1)} %get-tuple-element.83, pred[]{:T(512)} %get-tuple-element.82), kind=kLoop, calls=%fused_computation | loop fusion | flops 368640 | bytes 2211841 | tf_op jit(solution)/shard_map/cond/branch_0_fun/jit(_where)/select_n | solution.py:631
  54.2 1.3 %collective-permute-start.17 = (bf16[2,64,640]{2,1,0:T(8,128)(2,1)S(1)}, bf16[2,64,640]{2,1,0:T(8,128)(2,1)S(1)}, u32[]{:S(2)}, u32[]{:S(2)}) collective-permute-start(bf16[2,64,640]{2,1,0:T(8,128)(2,1)S(1)} %get-tuple-element.154), channel_id=1, source_target_pairs={{16,0},{17,1},{18,2},{19,3},{20,4},{21,5},{22,6},{23,7},{24,8},{25... | collective-permute-start | bytes 491528 | tf_op jit(solution)/shard_map/ppermute | solution.py:225
  55.5 1.3 %collective-permute-start.18 = (bf16[2,64,640]{2,1,0:T(8,128)(2,1)S(1)}, bf16[2,64,640]{2,1,0:T(8,128)(2,1)S(1)}, u32[]{:S(2)}, u32[]{:S(2)}) collective-permute-start(bf16[2,64,640]{2,1,0:T(8,128)(2,1)S(1)} %get-tuple-element.154), channel_id=1, source_target_pairs={{16,8},{17,9},{18,10},{19,11},{20,12},{21,13},{22,14},{23,15},{24,... | collective-permute-start | bytes 491528 | tf_op jit(solution)/shard_map/ppermute | solution.py:225
  56.8 8.2 %collective-permute-done.20 = bf16[4,64,1152]{2,1,0:T(8,128)(2,1)S(1)} collective-permute-done((bf16[4,64,1152]{2,1,0:T(8,128)(2,1)S(1)}, bf16[4,64,1152]{2,1,0:T(8,128)(2,1)S(1)}, u32[]{:S(2)}, u32[]{:S(2)}) %collective-permute-start.20) | collective-permute-done | bytes 589856 | tf_op jit(solution)/shard_map/ppermute | solution.py:225
  65.0 2.1 %collective-permute-done.19 = bf16[4,80,1152]{2,1,0:T(8,128)(2,1)} collective-permute-done((bf16[4,80,1152]{2,1,0:T(8,128)(2,1)}, bf16[4,80,1152]{2,1,0:T(8,128)(2,1)}, u32[]{:S(2)}, u32[]{:S(2)}) %collective-permute-start.19) | collective-permute-done | bytes 737312 | tf_op jit(solution)/shard_map/ppermute | solution.py:225
  67.1 6.9 %conditional.4 = (bf16[4,64,1152]{2,1,0:T(8,128)(2,1)}, bf16[4,80,1152]{2,1,0:T(8,128)(2,1)}, bf16[640,1152]{1,0:T(8,128)(2,1)}, bf16[64,640]{1,0:T(8,128)(2,1)}) conditional(s32[]{:T(128)} %convert_element_type.9, (bf16[4,64,1152]{2,1,0:T(8,128)(2,1)S(1)}, bf16[4,80,1152]{2,1,0:T(8,128)(2,1)}, s32[5]{0:T(128)S(1)}) %tuple.34, (s32[5]{0:T(128)S(1)}, ...), branch_computations={%region_2.3_spmd, %region_3.4_spmd} | conditional | flops 4 | bytes 5308529 | solution.py:648
  67.1 2.8 %collective-permute-start.3 = (bf16[4,80,1152]{2,1,0:T(8,128)(2,1)}, bf16[4,80,1152]{2,1,0:T(8,128)(2,1)}, u32[]{:S(2)}, u32[]{:S(2)}) collective-permute-start(bf16[4,80,1152]{2,1,0:T(8,128)(2,1)} %get-tuple-element.94), channel_id=1, source_target_pairs={{0,1},{1,0},{2,3},{3,2},{4,5},{5,4},{6,7},{7,6},{8,9},{9,8},{10,11... | collective-permute-start | bytes 2211848 | tf_op jit(solution)/shard_map/cond/branch_0_fun/ppermute | solution.py:225
  69.9 1.9 %collective-permute-start.2 = (bf16[4,64,1152]{2,1,0:T(8,128)(2,1)S(1)}, bf16[4,64,1152]{2,1,0:T(8,128)(2,1)}, u32[]{:S(2)}, u32[]{:S(2)}) collective-permute-start(bf16[4,64,1152]{2,1,0:T(8,128)(2,1)S(1)} %get-tuple-element.93), channel_id=1, source_target_pairs={{0,1},{1,0},{2,3},{3,2},{4,5},{5,4},{6,7},{7,6},{8,9},{9,8},{10,11... | collective-permute-start | bytes 1769480 | tf_op jit(solution)/shard_map/cond/branch_0_fun/ppermute | solution.py:225
  72.4 1.5 %collective-permute-done.2 = bf16[4,64,1152]{2,1,0:T(8,128)(2,1)} collective-permute-done((bf16[4,64,1152]{2,1,0:T(8,128)(2,1)S(1)}, bf16[4,64,1152]{2,1,0:T(8,128)(2,1)}, u32[]{:S(2)}, u32[]{:S(2)}) %collective-permute-start.2) | collective-permute-done | bytes 589856 | tf_op jit(solution)/shard_map/cond/branch_0_fun/ppermute | solution.py:225
  74.9 27.2 %conditional.5 = (bf16[2,64,640]{2,1,0:T(8,128)(2,1)S(1)}, bf16[64,640]{1,0:T(8,128)(2,1)S(1)}, bf16[640,1152]{1,0:T(8,128)(2,1)}, bf16[2,64,1152]{2,1,0:T(8,128)(2,1)}) conditional(s32[]{:T(128)} %convert_element_type.9, (f32[2,3,1152]{2,0,1:T(2,128)S(1)}, s32[5]{0:T(128)S(1)}, bf16[2,64,1152]{2,1,0:T(8,128)(2,1)S(1)}, ...), branch_computations={%region_4.5_spmd, %region_5.6_spmd} | conditional | flops 4 | bytes 66028300 | solution.py:674
  75.0 3.1 %collective-permute-start.9 = (bf16[4,80,1152]{2,1,0:T(8,128)(2,1)}, bf16[4,80,1152]{2,1,0:T(8,128)(2,1)S(1)}, u32[]{:S(2)}, u32[]{:S(2)}) collective-permute-start(bf16[4,80,1152]{2,1,0:T(8,128)(2,1)} %get-tuple-element.122.mine), channel_id=1, source_target_pairs={{0,8},{1,9},{2,10},{3,11},{4,12},{5,13},{6,14},{7,15},{8,0},{9,1},... | collective-permute-start | bytes 2211848 | tf_op jit(solution)/shard_map/cond/branch_0_fun/ppermute | solution.py:225
  78.1 6.5 %branch_0_fun.7 = (bf16[2,64,1152]{2,1,0:T(8,128)(2,1)}, bf16[256,640]{1,0:T(8,128)(2,1)S(1)}, bf16[256,384]{1,0:T(8,128)(2,1)S(1)}) custom-call(s32[5]{0:T(128)S(1)} %get-tuple-element.104.spot, bf16[2,64,1152]{2,1,0:T(8,128)(2,1)S(1)} %get-tuple-element.105.own, bf16[2,64,1152]{2,1,0:T(8,128)(2,1)S(1)} %get-tuple-element.106.far, ...), custom_call_target="tpu_custom_call" | custom-call | bytes 29600000 | tf_op jit(solution)/shard_map/cond/branch_0_fun/pallas_call | solution.py:239
  84.7 5.1 %collective-permute-start.6 = (bf16[256,640]{1,0:T(8,128)(2,1)S(1)}, bf16[256,640]{1,0:T(8,128)(2,1)S(1)}, u32[]{:S(2)}, u32[]{:S(2)}) collective-permute-start(bf16[256,640]{1,0:T(8,128)(2,1)S(1)} %get-tuple-element.119.here), channel_id=1, source_target_pairs={{1,2},{2,1},{3,4},{4,3},{5,6},{6,5},{9,10},{10,9},{11,12},{12,11},... | collective-permute-start | bytes 983048 | tf_op jit(solution)/shard_map/cond/branch_0_fun/ppermute | solution.py:225
  89.8 1.9 %collective-permute-start.7 = (bf16[256,640]{1,0:T(8,128)(2,1)S(1)}, bf16[256,640]{1,0:T(8,128)(2,1)S(1)}, u32[]{:S(2)}, u32[]{:S(2)}) collective-permute-start(bf16[256,640]{1,0:T(8,128)(2,1)S(1)} %get-tuple-element.119.here), channel_id=1, source_target_pairs={{0,1},{1,0},{2,3},{3,2},{4,5},{5,4},{6,7},{7,6},{8,9},{9,8},{10,11... | collective-permute-start | bytes 983048 | tf_op jit(solution)/shard_map/cond/branch_0_fun/ppermute | solution.py:225
  91.7 3.1 %collective-permute-done.6.outer = bf16[256,640]{1,0:T(8,128)(2,1)S(1)} collective-permute-done((bf16[256,640]{1,0:T(8,128)(2,1)S(1)}, bf16[256,640]{1,0:T(8,128)(2,1)S(1)}, u32[]{:S(2)}, u32[]{:S(2)}) %collective-permute-start.6) | collective-permute-done | bytes 327712 | tf_op jit(solution)/shard_map/cond/branch_0_fun/ppermute | solution.py:225
  94.9 2.1 %branch_0_fun.8 = bf16[128,640]{1,0:T(8,128)(2,1)S(1)} custom-call(s32[5]{0:T(128)S(1)} %get-tuple-element.104.spot, bf16[256,384]{1,0:T(8,128)(2,1)S(1)} %get-tuple-element.118.queries, bf16[256,640]{1,0:T(8,128)(2,1)S(1)} %collective-permute-done.6.outer, bf16[256,640]{1,0:T(8,128)(2,1)S(1)} %get-tuple-element.119.here, ...), custom_call_target="tpu_custom_call" | custom-call | bytes 29600000 | tf_op jit(solution)/shard_map/cond/branch_0_fun/pallas_call | solution.py:239
  97.0 2.1 %collective-permute-start.8 = (bf16[64,640]{1,0:T(8,128)(2,1)S(1)}, bf16[64,640]{1,0:T(8,128)(2,1)S(1)}, u32[]{:S(2)}, u32[]{:S(2)}) collective-permute-start(bf16[64,640]{1,0:T(8,128)(2,1)S(1)} %dynamic-slice_bitcast_fusion.1), channel_id=1, source_target_pairs={{0,8},{1,9},{2,10},{3,11},{4,12},{5,13},{6,14},{7,15},{8,0},{9,1},... | collective-permute-start | bytes 245768 | tf_op jit(solution)/shard_map/cond/branch_0_fun/ppermute | solution.py:225
  99.2 2.9 %branch_0_fun.9 = bf16[640,1152]{1,0:T(8,128)(2,1)} custom-call(s32[5]{0:T(128)S(1)} %get-tuple-element.104.spot, bf16[4,80,1152]{2,1,0:T(8,128)(2,1)} %get-tuple-element.122.mine, bf16[4,80,1152]{2,1,0:T(8,128)(2,1)S(1)} %collective-permute-done.9.other), custom_call_target="tpu_custom_call" | custom-call | bytes 1 | tf_op jit(solution)/shard_map/cond/branch_0_fun/pallas_call | solution.py:239
  102.2 2.7 %shard_map.67 = bf16[2,64,1152]{2,1,0:T(8,128)(2,1)} custom-call(s32[5]{0:T(128)S(1)} %stack.23.spot, bf16[2,64,640]{2,1,0:T(8,128)(2,1)S(1)} %get-tuple-element.162.attended, bf16[64,640]{1,0:T(8,128)(2,1)S(1)} %get-tuple-element.163.side, bf16[640,1152]{1,0:T(8,128)(2,1)} %get-tuple-element.164.head_rows, bf16[2,64,1152]{2,1,0:T(8,128)(2,1)S(1)} %bitcast.44, ...), custom_call_target="tpu_custom_call" | custom-call | bytes 1 | tf_op jit(solution)/shard_map/pallas_call | solution.py:239
  (47 shorter events, 9.2 us)
Async XLA Ops:
  0.0 1.0 copy-start
  1.0 7.9 %copy-start.1 = (bf16[1,2,8,8,1152]{4,3,2,1,0:T(8,128)(2,1)S(1)}, bf16[1,2,8,8,1152]{4,3,2,1,0:T(8,128)(2,1)}, u32[]{:S(2)}) copy-start(bf16[1,2,8,8,1152]{4,3,2,1,0:T(8,128)(2,1)} %param.12) | copy-start | bytes 884740
  1.0 10.5 %copy-start.8 = (f32[2,3,1152]{2,0,1:T(2,128)S(1)}, f32[2,3,1152]{2,0,1:T(2,128)}, u32[]{:S(2)}) copy-start(f32[2,3,1152]{2,0,1:T(2,128)} %param.13) | copy-start | bytes 82948
  3.2 20.4 %collective-permute-start.13 = (bf16[240,1152]{1,0:T(8,128)(2,1)S(1)}, bf16[240,1152]{1,0:T(8,128)(2,1)S(1)}, u32[]{:S(2)}, u32[]{:S(2)}) collective-permute-start(bf16[240,1152]{1,0:T(8,128)(2,1)S(1)} %fusion.2.one), channel_id=1, source_target_pairs={{0,6},{1,7},{2,4},{3,5},{4,2},{5,3},{6,0},{7,1},{8,14},{9,15},{10,... | collective-permute-start | bytes 1658888 | tf_op jit(solution)/shard_map/ppermute | solution.py:225
  7.4 24.9 %collective-permute-start.14 = (bf16[240,1152]{1,0:T(8,128)(2,1)S(1)}, bf16[240,1152]{1,0:T(8,128)(2,1)S(1)}, u32[]{:S(2)}, u32[]{:S(2)}) collective-permute-start(bf16[240,1152]{1,0:T(8,128)(2,1)S(1)} %fusion.2.one), channel_id=1, source_target_pairs={{0,2},{1,3},{2,0},{3,1},{4,6},{5,7},{6,4},{7,5},{8,10},{9,11},{10,... | collective-permute-start | bytes 1658888 | tf_op jit(solution)/shard_map/ppermute | solution.py:225
  8.9 13.9 %collective-permute-start.10 = (bf16[2,64,1152]{2,1,0:T(8,128)(2,1)S(1)}, bf16[2,64,1152]{2,1,0:T(8,128)(2,1)S(1)}, u32[]{:S(2)}, u32[]{:S(2)}) collective-permute-start(bf16[2,64,1152]{2,1,0:T(8,128)(2,1)S(1)} %bitcast.40), channel_id=1, source_target_pairs={{0,16},{1,17},{2,18},{3,19},{4,20},{5,21},{6,22},{7,23},{8,24},{9,... | collective-permute-start | bytes 884744 | tf_op jit(solution)/shard_map/ppermute | solution.py:225
  10.2 22.0 %collective-permute-start.12 = (bf16[2,64,1152]{2,1,0:T(8,128)(2,1)S(1)}, bf16[2,64,1152]{2,1,0:T(8,128)(2,1)S(1)}, u32[]{:S(2)}, u32[]{:S(2)}) collective-permute-start(bf16[2,64,1152]{2,1,0:T(8,128)(2,1)S(1)} %bitcast.41), channel_id=1, source_target_pairs={{16,8},{17,9},{18,10},{19,11},{20,12},{21,13},{22,14},{23,15},{24,... | collective-permute-start | bytes 884744 | tf_op jit(solution)/shard_map/ppermute | solution.py:225
  23.6 19.5 %collective-permute-start.15 = (bf16[240,1152]{1,0:T(8,128)(2,1)S(1)}, bf16[240,1152]{1,0:T(8,128)(2,1)S(1)}, u32[]{:S(2)}, u32[]{:S(2)}) collective-permute-start(bf16[240,1152]{1,0:T(8,128)(2,1)S(1)} %collective-permute-done.13.two), channel_id=1, source_target_pairs={{0,2},{1,3},{2,0},{3,1},{4,6},{5,7},{6,4},{7,5},{8,10},{9,11},{10,... | collective-permute-start | bytes 1658888 | tf_op jit(solution)/shard_map/ppermute | solution.py:225
  30.9 6.9 %collective-permute-start.11 = (bf16[2,64,1152]{2,1,0:T(8,128)(2,1)S(1)}, bf16[2,64,1152]{2,1,0:T(8,128)(2,1)S(1)}, u32[]{:S(2)}, u32[]{:S(2)}) collective-permute-start(bf16[2,64,1152]{2,1,0:T(8,128)(2,1)S(1)} %broadcast_select_fusion), channel_id=1, source_target_pairs={{0,8},{1,9},{2,10},{3,11},{4,12},{5,13},{6,14},{7,15},{8,0},{9,1},... | collective-permute-start | bytes 884744 | tf_op jit(solution)/shard_map/ppermute | solution.py:225
  32.2 15.9 %copy-start.6 = (bf16[2,64,1152]{2,1,0:T(8,128)(2,1)}, bf16[2,64,1152]{2,1,0:T(8,128)(2,1)S(1)}, u32[]{:S(2)}) copy-start(bf16[2,64,1152]{2,1,0:T(8,128)(2,1)S(1)} %collective-permute-done.12) | copy-start | bytes 884740
  37.8 0.7 copy-start.4
  45.1 6.1 %collective-permute-start.16 = (bf16[4,240,1152]{2,1,0:T(8,128)(2,1)}, bf16[4,240,1152]{2,1,0:T(8,128)(2,1)}, u32[]{:S(2)}, u32[]{:S(2)}) collective-permute-start(bf16[4,240,1152]{2,1,0:T(8,128)(2,1)} %get-tuple-element.152), channel_id=1, source_target_pairs={{0,1},{1,0},{2,3},{3,2},{4,5},{5,4},{6,7},{7,6},{8,9},{9,8},{10,11... | collective-permute-start | bytes 6635528 | tf_op jit(solution)/shard_map/ppermute | solution.py:225
  46.8 20.3 %collective-permute-start.19 = (bf16[4,80,1152]{2,1,0:T(8,128)(2,1)}, bf16[4,80,1152]{2,1,0:T(8,128)(2,1)}, u32[]{:S(2)}, u32[]{:S(2)}) collective-permute-start(bf16[4,80,1152]{2,1,0:T(8,128)(2,1)} %get-tuple-element.155), channel_id=1, source_target_pairs={{16,0},{17,1},{18,2},{19,3},{20,4},{21,5},{22,6},{23,7},{24,8},{25... | collective-permute-start | bytes 2211848 | tf_op jit(solution)/shard_map/ppermute | solution.py:225
  48.1 16.9 %collective-permute-start.20 = (bf16[4,64,1152]{2,1,0:T(8,128)(2,1)S(1)}, bf16[4,64,1152]{2,1,0:T(8,128)(2,1)S(1)}, u32[]{:S(2)}, u32[]{:S(2)}) collective-permute-start(bf16[4,64,1152]{2,1,0:T(8,128)(2,1)S(1)} %get-tuple-element.156), channel_id=1, source_target_pairs={{0,8},{1,9},{2,10},{3,11},{4,12},{5,13},{6,14},{7,15},{8,0},{9,1},... | collective-permute-start | bytes 1769480 | tf_op jit(solution)/shard_map/ppermute | solution.py:225
  51.2 5.6 %copy-start.10 = (f32[1,3,1152]{2,0,1:T(1,128)S(1)}, f32[1,3,1152]{2,0,1:T(1,128)}, u32[]{:S(2)}) copy-start(f32[1,3,1152]{2,0,1:T(1,128)} %get-tuple-element.187) | copy-start | bytes 41476
  54.2 20.7 %collective-permute-start.17 = (bf16[2,64,640]{2,1,0:T(8,128)(2,1)S(1)}, bf16[2,64,640]{2,1,0:T(8,128)(2,1)S(1)}, u32[]{:S(2)}, u32[]{:S(2)}) collective-permute-start(bf16[2,64,640]{2,1,0:T(8,128)(2,1)S(1)} %get-tuple-element.154), channel_id=1, source_target_pairs={{16,0},{17,1},{18,2},{19,3},{20,4},{21,5},{22,6},{23,7},{24,8},{25... | collective-permute-start | bytes 491528 | tf_op jit(solution)/shard_map/ppermute | solution.py:225
  55.5 19.4 %collective-permute-start.18 = (bf16[2,64,640]{2,1,0:T(8,128)(2,1)S(1)}, bf16[2,64,640]{2,1,0:T(8,128)(2,1)S(1)}, u32[]{:S(2)}, u32[]{:S(2)}) collective-permute-start(bf16[2,64,640]{2,1,0:T(8,128)(2,1)S(1)} %get-tuple-element.154), channel_id=1, source_target_pairs={{16,8},{17,9},{18,10},{19,11},{20,12},{21,13},{22,14},{23,15},{24,... | collective-permute-start | bytes 491528 | tf_op jit(solution)/shard_map/ppermute | solution.py:225
  67.1 7.8 %copy-start.2 = (f32[128,384]{1,0:T(8,128)S(1)}, f32[128,384]{1,0:T(8,128)}, u32[]{:S(2)}) copy-start(f32[128,384]{1,0:T(8,128)} %shard_map.64) | copy-start | bytes 589828
  67.1 7.8 %copy-start.5 = (bf16[2,64,1152]{2,1,0:T(8,128)(2,1)S(1)}, bf16[2,64,1152]{2,1,0:T(8,128)(2,1)}, u32[]{:S(2)}) copy-start(bf16[2,64,1152]{2,1,0:T(8,128)(2,1)} %copy-done.4) | copy-start | bytes 884740
  67.1 7.9 %copy-start.9 = (f32[2,3,1152]{2,0,1:T(2,128)S(1)}, f32[2,3,1152]{2,0,1:T(2,128)}, u32[]{:S(2)}) copy-start(f32[2,3,1152]{2,0,1:T(2,128)} %param.13) | copy-start | bytes 82948
  67.1 6.9 %collective-permute-start.3 = (bf16[4,80,1152]{2,1,0:T(8,128)(2,1)}, bf16[4,80,1152]{2,1,0:T(8,128)(2,1)}, u32[]{:S(2)}, u32[]{:S(2)}) collective-permute-start(bf16[4,80,1152]{2,1,0:T(8,128)(2,1)} %get-tuple-element.94), channel_id=1, source_target_pairs={{0,1},{1,0},{2,3},{3,2},{4,5},{5,4},{6,7},{7,6},{8,9},{9,8},{10,11... | collective-permute-start | bytes 2211848 | tf_op jit(solution)/shard_map/cond/branch_0_fun/ppermute | solution.py:225
  69.9 4.0 %collective-permute-start.2 = (bf16[4,64,1152]{2,1,0:T(8,128)(2,1)S(1)}, bf16[4,64,1152]{2,1,0:T(8,128)(2,1)}, u32[]{:S(2)}, u32[]{:S(2)}) collective-permute-start(bf16[4,64,1152]{2,1,0:T(8,128)(2,1)S(1)} %get-tuple-element.93), channel_id=1, source_target_pairs={{0,1},{1,0},{2,3},{3,2},{4,5},{5,4},{6,7},{7,6},{8,9},{9,8},{10,11... | collective-permute-start | bytes 1769480 | tf_op jit(solution)/shard_map/cond/branch_0_fun/ppermute | solution.py:225
  75.0 3.2 %copy-start.7 = (bf16[2,64,640]{2,1,0:T(8,128)(2,1)}, bf16[2,64,640]{2,1,0:T(8,128)(2,1)S(1)}, u32[]{:S(2)}) copy-start(bf16[2,64,640]{2,1,0:T(8,128)(2,1)S(1)} %get-tuple-element.110.cross) | copy-start | bytes 491524 | tf_op jit(solution)/shard_map/cond
  75.0 24.2 %collective-permute-start.9 = (bf16[4,80,1152]{2,1,0:T(8,128)(2,1)}, bf16[4,80,1152]{2,1,0:T(8,128)(2,1)S(1)}, u32[]{:S(2)}, u32[]{:S(2)}) collective-permute-start(bf16[4,80,1152]{2,1,0:T(8,128)(2,1)} %get-tuple-element.122.mine), channel_id=1, source_target_pairs={{0,8},{1,9},{2,10},{3,11},{4,12},{5,13},{6,14},{7,15},{8,0},{9,1},... | collective-permute-start | bytes 2211848 | tf_op jit(solution)/shard_map/cond/branch_0_fun/ppermute | solution.py:225
  84.7 10.2 %collective-permute-start.6 = (bf16[256,640]{1,0:T(8,128)(2,1)S(1)}, bf16[256,640]{1,0:T(8,128)(2,1)S(1)}, u32[]{:S(2)}, u32[]{:S(2)}) collective-permute-start(bf16[256,640]{1,0:T(8,128)(2,1)S(1)} %get-tuple-element.119.here), channel_id=1, source_target_pairs={{1,2},{2,1},{3,4},{4,3},{5,6},{6,5},{9,10},{10,9},{11,12},{12,11},... | collective-permute-start | bytes 983048 | tf_op jit(solution)/shard_map/cond/branch_0_fun/ppermute | solution.py:225
  89.8 5.0 %collective-permute-start.7 = (bf16[256,640]{1,0:T(8,128)(2,1)S(1)}, bf16[256,640]{1,0:T(8,128)(2,1)S(1)}, u32[]{:S(2)}, u32[]{:S(2)}) collective-permute-start(bf16[256,640]{1,0:T(8,128)(2,1)S(1)} %get-tuple-element.119.here), channel_id=1, source_target_pairs={{0,1},{1,0},{2,3},{3,2},{4,5},{5,4},{6,7},{7,6},{8,9},{9,8},{10,11... | collective-permute-start | bytes 983048 | tf_op jit(solution)/shard_map/cond/branch_0_fun/ppermute | solution.py:225
  97.0 5.2 %collective-permute-start.8 = (bf16[64,640]{1,0:T(8,128)(2,1)S(1)}, bf16[64,640]{1,0:T(8,128)(2,1)S(1)}, u32[]{:S(2)}, u32[]{:S(2)}) collective-permute-start(bf16[64,640]{1,0:T(8,128)(2,1)S(1)} %dynamic-slice_bitcast_fusion.1), channel_id=1, source_target_pairs={{0,8},{1,9},{2,10},{3,11},{4,12},{5,13},{6,14},{7,15},{8,0},{9,1},... | collective-permute-start | bytes 245768 | tf_op jit(solution)/shard_map/cond/branch_0_fun/ppermute | solution.py:225

commit v7 on v6

--- a/solution.py
+++ b/solution.py
@@ -229,7 +229,7 @@
     return lax.optimization_barrier((block,) + earlier)[0]
 
 
-def kernel_call(body, outs, args, scratch=(), copies=0, stay=False, micros=0, near=False, room=16):
+def kernel_call(body, outs, args, scratch=(), copies=0, stay=False, micros=0, near=False, room=16, keep=()):
     def space(a):
         if a.dtype == jnp.int32:
             return pltpu.SMEM
@@ -241,6 +241,7 @@
         out_shape=[jax.ShapeDtypeStruct(shape, kind) for shape, kind in outs],
         in_specs=[pl.BlockSpec(memory_space=space(a)) for a in args],
         out_specs=[pl.BlockSpec(memory_space=pl.ANY if stay else pltpu.VMEM) for _ in outs],
+        input_output_aliases=dict(keep),
         scratch_shapes=buffers + ([pltpu.SemaphoreType.DMA((copies,))] if copies else []),
         compiler_params=pltpu.CompilerParams(vmem_limit_bytes=room * 1024 * 1024),
         cost_estimate=pl.CostEstimate(
@@ -271,13 +272,14 @@
     return pl.ds(pl.multiple_of(start, 16), count)
 
 
-def stack_kernel(spot, one, two, three, four, stacked, heads, shared, done):
-    pieces = (one, two, three, four)
-    started = begin([(piece, stacked.at[n]) for n, piece in enumerate(pieces)], done)
+def stack_kernel(first_index, count, spot, *refs):
+    pieces = list(enumerate(refs[:count], first_index))
+    stacked, heads, shared, done = refs[-4:]
+    started = begin([(piece, stacked.at[n]) for n, piece in pieces], done)
 
     def part(first, target):
         rows = slice(first, first + target.shape[1])
-        finish(begin([(piece.at[rows], target.at[n]) for n, piece in enumerate(pieces)], done, 4))
+        finish(begin([(piece.at[rows], target.at[n]) for n, piece in pieces], done, count))
 
     is_control = spot[0] == 1
     is_query = spot[3] == spot[1]
@@ -575,11 +577,15 @@
         near=True,
     )
     side = swap_rows(jnp.where(is_control, normed, own))
-    first.append(swap_links(first[1], ORDER[2]))
-    side, corner, bias, *first = lax.optimization_barrier((side, corner, bias, *first))
+    last = swap_links(first[1], ORDER[2])
+    parts = [triple_shape, stack_shape, shared_shape]
+    begun = kernel_call(
+        functools.partial(stack_kernel, 0, 3), parts, (spot, *first), copies=6, stay=True
+    )
+    side, corner, bias, last, *begun = lax.optimization_barrier((side, corner, bias, last, *begun))
     first, head_stack, shared = kernel_call(
-        stack_kernel, [triple_shape, stack_shape, shared_shape], (spot, *first),
-        copies=8, stay=True,
+        functools.partial(stack_kernel, 3, 1), parts, (spot, last, *begun),
+        copies=2, stay=True, keep=((2, 0), (3, 1), (4, 2)),
     )
     first_other = swap_cores(first)
     out_mine = send(head_stack, sizes, lambda b, r, t: (0, r, t) if b == 1 else None)

time: 105 us -> 105 us (level)
  local copies, waits for them, and re-layouts: 2.47 us -> 1.17 us
  Pallas kernels: 19.5 us -> 20.7 us
    pallas_call x9 -> x10, Pallas kernels: 19.5 us -> 20.7 us  [kernel_call(): pl.pallas_call(body, out_shape=[jax.ShapeDtypeStruct(shape, kind) for sha...]
  transfers between devices with their start and end apart: 17 -> 17, of which waited for: 10 -> 9; matrix products, arithmetic and copies ran while one was open for 3% -> 2% of each run, Pallas kernels for 14% -> 16%
where the time goes in v7:
time: 105 us; the launch traced here: 104 us
  starting transfers between devices  41.2 us (39%)
  waiting for transfers between devices  36.2 us (34%)
  Pallas kernels  20.7 us (20%)
  other arithmetic  4.63 us (4%)
  local copies, waits for them, and re-layouts  1.17 us (1%)
    ppermute x17, starting transfers between devices, send(): return lax.ppermute(block, AXES, routes(sizes, move))  41.2 us
    ppermute x17, waiting for transfers between devices, send(): return lax.ppermute(block, AXES, routes(sizes, move))  36.2 us
    pallas_call x10, Pallas kernels, kernel_call(): pl.pallas_call(body, out_shape=[jax.ShapeDtypeStruct(shape, kind) for sha...  20.7 us
    select_n x1, other arithmetic, base_third(): third = jnp.where(is_query, first_other[:, 2 * SLOT:], first[:, 2 * SLOT:])  2.39 us
  transfers between devices with their start and end apart: 17, of which 9 were waited for; matrix products, arithmetic and copies ran while one was open for 2% of the time, Pallas kernels for 16%

profile of v7, /device:TPU:1, one launch (start us, length us, event | category | flops | bytes accessed | tf_op | source)
XLA Modules:
  0.0 104.3 jit_solution(444978620968796147)
XLA Ops:
  3.2 4.2 %collective-permute-start.13 = (bf16[240,1152]{1,0:T(8,128)(2,1)S(1)}, bf16[240,1152]{1,0:T(8,128)(2,1)S(1)}, u32[]{:S(2)}, u32[]{:S(2)}) collective-permute-start(bf16[240,1152]{1,0:T(8,128)(2,1)S(1)} %fusion.2.refs_0_), channel_id=1, source_target_pairs={{0,6},{1,7},{2,4},{3,5},{4,2},{5,3},{6,0},{7,1},{8,14},{9,15},{10,... | collective-permute-start | bytes 1658888 | tf_op jit(solution)/shard_map/ppermute | solution.py:225
  7.5 1.3 %shard_map.64 = f32[128,384]{1,0:T(8,128)} custom-call(s32[5]{0:T(128)S(1)} %stack.23.spot), custom_call_target="tpu_custom_call" | custom-call | bytes 1 | tf_op jit(solution)/shard_map/pallas_call | solution.py:239
  8.9 1.3 %collective-permute-start.10 = (bf16[2,64,1152]{2,1,0:T(8,128)(2,1)S(1)}, bf16[2,64,1152]{2,1,0:T(8,128)(2,1)S(1)}, u32[]{:S(2)}, u32[]{:S(2)}) collective-permute-start(bf16[2,64,1152]{2,1,0:T(8,128)(2,1)S(1)} %bitcast.40), channel_id=1, source_target_pairs={{0,16},{1,17},{2,18},{3,19},{4,20},{5,21},{6,22},{7,23},{8,24},{9,... | collective-permute-start | bytes 884744 | tf_op jit(solution)/shard_map/ppermute | solution.py:225
  10.2 1.3 %collective-permute-start.12 = (bf16[2,64,1152]{2,1,0:T(8,128)(2,1)S(1)}, bf16[2,64,1152]{2,1,0:T(8,128)(2,1)S(1)}, u32[]{:S(2)}, u32[]{:S(2)}) collective-permute-start(bf16[2,64,1152]{2,1,0:T(8,128)(2,1)S(1)} %bitcast.41), channel_id=1, source_target_pairs={{16,8},{17,9},{18,10},{19,11},{20,12},{21,13},{22,14},{23,15},{24,... | collective-permute-start | bytes 884744 | tf_op jit(solution)/shard_map/ppermute | solution.py:225
  11.5 11.3 %collective-permute-done.10.far = bf16[2,64,1152]{2,1,0:T(8,128)(2,1)S(1)} collective-permute-done((bf16[2,64,1152]{2,1,0:T(8,128)(2,1)S(1)}, bf16[2,64,1152]{2,1,0:T(8,128)(2,1)S(1)}, u32[]{:S(2)}, u32[]{:S(2)}) %collective-permute-start.10) | collective-permute-done | bytes 294944 | tf_op jit(solution)/shard_map/ppermute | solution.py:225
  23.6 7.2 %collective-permute-start.14 = (bf16[240,1152]{1,0:T(8,128)(2,1)S(1)}, bf16[240,1152]{1,0:T(8,128)(2,1)S(1)}, u32[]{:S(2)}, u32[]{:S(2)}) collective-permute-start(bf16[240,1152]{1,0:T(8,128)(2,1)S(1)} %collective-permute-done.13.refs_1_), channel_id=1, source_target_pairs={{0,2},{1,3},{2,0},{3,1},{4,6},{5,7},{6,4},{7,5},{8,10},{9,11},{10,... | collective-permute-start | bytes 1658888 | tf_op jit(solution)/shard_map/ppermute | solution.py:225
  32.4 1.8 %shard_map.66 = (bf16[4,240,1152]{2,1,0:T(8,128)(2,1)}, bf16[4,80,1152]{2,1,0:T(8,128)(2,1)}, bf16[4,64,1152]{2,1,0:T(8,128)(2,1)S(1)}) custom-call(s32[5]{0:T(128)S(1)} %stack.23.spot, bf16[240,1152]{1,0:T(8,128)(2,1)S(1)} %fusion.2.refs_0_, bf16[240,1152]{1,0:T(8,128)(2,1)S(1)} %collective-permute-done.13.refs_1_, ...), custom_call_target="tpu_custom_call" | custom-call | bytes 1 | tf_op jit(solution)/shard_map/pallas_call | solution.py:239
  34.2 3.7 %collective-permute-done.11 = bf16[2,64,1152]{2,1,0:T(8,128)(2,1)S(1)} collective-permute-done((bf16[2,64,1152]{2,1,0:T(8,128)(2,1)S(1)}, bf16[2,64,1152]{2,1,0:T(8,128)(2,1)S(1)}, u32[]{:S(2)}, u32[]{:S(2)}) %collective-permute-start.11) | collective-permute-done | bytes 294944 | tf_op jit(solution)/shard_map/ppermute | solution.py:225
  37.8 5.3 %collective-permute-done.14.refs_0_ = bf16[240,1152]{1,0:T(8,128)(2,1)S(1)} collective-permute-done((bf16[240,1152]{1,0:T(8,128)(2,1)S(1)}, bf16[240,1152]{1,0:T(8,128)(2,1)S(1)}, u32[]{:S(2)}, u32[]{:S(2)}) %collective-permute-start.14) | collective-permute-done | bytes 552992 | tf_op jit(solution)/shard_map/ppermute | solution.py:225
  43.1 1.4 %shard_map.67 = (bf16[4,240,1152]{2,1,0:T(8,128)(2,1)}, bf16[4,80,1152]{2,1,0:T(8,128)(2,1)}, bf16[4,64,1152]{2,1,0:T(8,128)(2,1)S(1)}) custom-call(s32[5]{0:T(128)S(1)} %stack.23.spot, bf16[240,1152]{1,0:T(8,128)(2,1)S(1)} %collective-permute-done.14.refs_0_, ...), custom_call_target="tpu_custom_call", output_to_operand_aliasing={{0}: (2, {}), {1}: (3, {}), {2}: (4, {})} | custom-call | bytes 1 | tf_op jit(solution)/shard_map/pallas_call | solution.py:239
  44.5 1.7 %collective-permute-start.16 = (bf16[4,240,1152]{2,1,0:T(8,128)(2,1)}, bf16[4,240,1152]{2,1,0:T(8,128)(2,1)}, u32[]{:S(2)}, u32[]{:S(2)}) collective-permute-start(bf16[4,240,1152]{2,1,0:T(8,128)(2,1)} %get-tuple-element.158), channel_id=1, source_target_pairs={{0,1},{1,0},{2,3},{3,2},{4,5},{5,4},{6,7},{7,6},{8,9},{9,8},{10,11... | collective-permute-start | bytes 6635528 | tf_op jit(solution)/shard_map/ppermute | solution.py:225
  47.5 3.1 %collective-permute-start.20 = (bf16[4,64,1152]{2,1,0:T(8,128)(2,1)S(1)}, bf16[4,64,1152]{2,1,0:T(8,128)(2,1)}, u32[]{:S(2)}, u32[]{:S(2)}) collective-permute-start(bf16[4,64,1152]{2,1,0:T(8,128)(2,1)S(1)} %get-tuple-element.162), channel_id=1, source_target_pairs={{0,8},{1,9},{2,10},{3,11},{4,12},{5,13},{6,14},{7,15},{8,0},{9,1},... | collective-permute-start | bytes 1769480 | tf_op jit(solution)/shard_map/ppermute | solution.py:225
  50.6 3.0 %conditional.3 = (bf16[2,64,640]{2,1,0:T(8,128)(2,1)S(1)}, bf16[4,80,1152]{2,1,0:T(8,128)(2,1)}) conditional(s32[]{:T(128)} %convert_element_type.9, (s32[5]{0:T(128)S(1)}, pred[]{:T(512)}, bf16[4,240,1152]{2,1,0:T(8,128)(2,1)}, bf16[4,240,1152]{2,1,0:T(8,128)(2,1)}) %tuple.32, (s32[5]{0:T(128)S(1)}, bf16[2,64,1152]{2,1,0:T(8,128)(2,1)S(1)}, ...), branch_computations={%region_0.1_spmd, %region_1.2_spmd} | conditional | flops 368640 | bytes 50721536 | solution.py:640
  50.6 2.4 %slice_select_fusion = bf16[4,80,1152]{2,1,0:T(8,128)(2,1)} fusion(bf16[4,240,1152]{2,1,0:T(8,128)(2,1)} %get-tuple-element.84, bf16[4,240,1152]{2,1,0:T(8,128)(2,1)} %get-tuple-element.83, pred[]{:T(512)} %get-tuple-element.82), kind=kLoop, calls=%fused_computation | loop fusion | flops 368640 | bytes 2211841 | tf_op jit(solution)/shard_map/cond/branch_0_fun/jit(_where)/select_n | solution.py:637
  53.6 1.3 %collective-permute-start.17 = (bf16[2,64,640]{2,1,0:T(8,128)(2,1)S(1)}, bf16[2,64,640]{2,1,0:T(8,128)(2,1)S(1)}, u32[]{:S(2)}, u32[]{:S(2)}) collective-permute-start(bf16[2,64,640]{2,1,0:T(8,128)(2,1)S(1)} %get-tuple-element.160), channel_id=1, source_target_pairs={{16,0},{17,1},{18,2},{19,3},{20,4},{21,5},{22,6},{23,7},{24,8},{25... | collective-permute-start | bytes 491528 | tf_op jit(solution)/shard_map/ppermute | solution.py:225
  54.9 1.3 %collective-permute-start.18 = (bf16[2,64,640]{2,1,0:T(8,128)(2,1)S(1)}, bf16[2,64,640]{2,1,0:T(8,128)(2,1)}, u32[]{:S(2)}, u32[]{:S(2)}) collective-permute-start(bf16[2,64,640]{2,1,0:T(8,128)(2,1)S(1)} %get-tuple-element.160), channel_id=1, source_target_pairs={{16,8},{17,9},{18,10},{19,11},{20,12},{21,13},{22,14},{23,15},{24,... | collective-permute-start | bytes 491528 | tf_op jit(solution)/shard_map/ppermute | solution.py:225
  56.2 8.2 %collective-permute-done.20 = bf16[4,64,1152]{2,1,0:T(8,128)(2,1)} collective-permute-done((bf16[4,64,1152]{2,1,0:T(8,128)(2,1)S(1)}, bf16[4,64,1152]{2,1,0:T(8,128)(2,1)}, u32[]{:S(2)}, u32[]{:S(2)}) %collective-permute-start.20) | collective-permute-done | bytes 589856 | tf_op jit(solution)/shard_map/ppermute | solution.py:225
  64.4 2.1 %collective-permute-done.19 = bf16[4,80,1152]{2,1,0:T(8,128)(2,1)} collective-permute-done((bf16[4,80,1152]{2,1,0:T(8,128)(2,1)}, bf16[4,80,1152]{2,1,0:T(8,128)(2,1)}, u32[]{:S(2)}, u32[]{:S(2)}) %collective-permute-start.19) | collective-permute-done | bytes 737312 | tf_op jit(solution)/shard_map/ppermute | solution.py:225
  66.5 7.1 %conditional.4 = (bf16[4,64,1152]{2,1,0:T(8,128)(2,1)}, bf16[4,80,1152]{2,1,0:T(8,128)(2,1)}, bf16[640,1152]{1,0:T(8,128)(2,1)}, bf16[64,640]{1,0:T(8,128)(2,1)}) conditional(s32[]{:T(128)} %convert_element_type.9, (bf16[4,64,1152]{2,1,0:T(8,128)(2,1)}, bf16[4,80,1152]{2,1,0:T(8,128)(2,1)}, s32[5]{0:T(128)S(1)}) %tuple.34, (s32[5]{0:T(128)S(1)}, ...), branch_computations={%region_2.3_spmd, %region_3.4_spmd} | conditional | flops 4 | bytes 5308529 | solution.py:654
  66.5 2.8 %collective-permute-start.3 = (bf16[4,80,1152]{2,1,0:T(8,128)(2,1)}, bf16[4,80,1152]{2,1,0:T(8,128)(2,1)}, u32[]{:S(2)}, u32[]{:S(2)}) collective-permute-start(bf16[4,80,1152]{2,1,0:T(8,128)(2,1)} %get-tuple-element.94), channel_id=1, source_target_pairs={{0,1},{1,0},{2,3},{3,2},{4,5},{5,4},{6,7},{7,6},{8,9},{9,8},{10,11... | collective-permute-start | bytes 2211848 | tf_op jit(solution)/shard_map/cond/branch_0_fun/ppermute | solution.py:225
  69.3 1.9 %collective-permute-start.2 = (bf16[4,64,1152]{2,1,0:T(8,128)(2,1)}, bf16[4,64,1152]{2,1,0:T(8,128)(2,1)}, u32[]{:S(2)}, u32[]{:S(2)}) collective-permute-start(bf16[4,64,1152]{2,1,0:T(8,128)(2,1)} %get-tuple-element.93), channel_id=1, source_target_pairs={{0,1},{1,0},{2,3},{3,2},{4,5},{5,4},{6,7},{7,6},{8,9},{9,8},{10,11... | collective-permute-start | bytes 1769480 | tf_op jit(solution)/shard_map/cond/branch_0_fun/ppermute | solution.py:225
  71.8 1.8 %collective-permute-done.2 = bf16[4,64,1152]{2,1,0:T(8,128)(2,1)} collective-permute-done((bf16[4,64,1152]{2,1,0:T(8,128)(2,1)}, bf16[4,64,1152]{2,1,0:T(8,128)(2,1)}, u32[]{:S(2)}, u32[]{:S(2)}) %collective-permute-start.2) | collective-permute-done | bytes 589856 | tf_op jit(solution)/shard_map/cond/branch_0_fun/ppermute | solution.py:225
  74.1 27.5 %conditional.5 = (bf16[2,64,640]{2,1,0:T(8,128)(2,1)S(1)}, bf16[64,640]{1,0:T(8,128)(2,1)S(1)}, bf16[640,1152]{1,0:T(8,128)(2,1)}, bf16[2,64,1152]{2,1,0:T(8,128)(2,1)}) conditional(s32[]{:T(128)} %convert_element_type.9, (f32[2,3,1152]{2,0,1:T(2,128)S(1)}, s32[5]{0:T(128)S(1)}, bf16[2,64,1152]{2,1,0:T(8,128)(2,1)S(1)}, ...), branch_computations={%region_4.5_spmd, %region_5.6_spmd} | conditional | flops 4 | bytes 66028300 | solution.py:680
  74.2 3.1 %collective-permute-start.9 = (bf16[4,80,1152]{2,1,0:T(8,128)(2,1)}, bf16[4,80,1152]{2,1,0:T(8,128)(2,1)S(1)}, u32[]{:S(2)}, u32[]{:S(2)}) collective-permute-start(bf16[4,80,1152]{2,1,0:T(8,128)(2,1)} %get-tuple-element.122.mine), channel_id=1, source_target_pairs={{0,8},{1,9},{2,10},{3,11},{4,12},{5,13},{6,14},{7,15},{8,0},{9,1},... | collective-permute-start | bytes 2211848 | tf_op jit(solution)/shard_map/cond/branch_0_fun/ppermute | solution.py:225
  77.3 6.7 %branch_0_fun.7 = (bf16[2,64,1152]{2,1,0:T(8,128)(2,1)}, bf16[256,640]{1,0:T(8,128)(2,1)S(1)}, bf16[256,384]{1,0:T(8,128)(2,1)S(1)}) custom-call(s32[5]{0:T(128)S(1)} %get-tuple-element.104.spot, bf16[2,64,1152]{2,1,0:T(8,128)(2,1)S(1)} %get-tuple-element.105.own, bf16[2,64,1152]{2,1,0:T(8,128)(2,1)S(1)} %get-tuple-element.106.far, ...), custom_call_target="tpu_custom_call" | custom-call | bytes 29600000 | tf_op jit(solution)/shard_map/cond/branch_0_fun/pallas_call | solution.py:239
  84.0 5.2 %collective-permute-start.6 = (bf16[256,640]{1,0:T(8,128)(2,1)S(1)}, bf16[256,640]{1,0:T(8,128)(2,1)S(1)}, u32[]{:S(2)}, u32[]{:S(2)}) collective-permute-start(bf16[256,640]{1,0:T(8,128)(2,1)S(1)} %get-tuple-element.119.here), channel_id=1, source_target_pairs={{1,2},{2,1},{3,4},{4,3},{5,6},{6,5},{9,10},{10,9},{11,12},{12,11},... | collective-permute-start | bytes 983048 | tf_op jit(solution)/shard_map/cond/branch_0_fun/ppermute | solution.py:225
  89.2 1.9 %collective-permute-start.7 = (bf16[256,640]{1,0:T(8,128)(2,1)S(1)}, bf16[256,640]{1,0:T(8,128)(2,1)S(1)}, u32[]{:S(2)}, u32[]{:S(2)}) collective-permute-start(bf16[256,640]{1,0:T(8,128)(2,1)S(1)} %get-tuple-element.119.here), channel_id=1, source_target_pairs={{0,1},{1,0},{2,3},{3,2},{4,5},{5,4},{6,7},{7,6},{8,9},{9,8},{10,11... | collective-permute-start | bytes 983048 | tf_op jit(solution)/shard_map/cond/branch_0_fun/ppermute | solution.py:225
  91.2 3.1 %collective-permute-done.6.outer = bf16[256,640]{1,0:T(8,128)(2,1)S(1)} collective-permute-done((bf16[256,640]{1,0:T(8,128)(2,1)S(1)}, bf16[256,640]{1,0:T(8,128)(2,1)S(1)}, u32[]{:S(2)}, u32[]{:S(2)}) %collective-permute-start.6) | collective-permute-done | bytes 327712 | tf_op jit(solution)/shard_map/cond/branch_0_fun/ppermute | solution.py:225
  94.3 2.1 %branch_0_fun.8 = bf16[128,640]{1,0:T(8,128)(2,1)S(1)} custom-call(s32[5]{0:T(128)S(1)} %get-tuple-element.104.spot, bf16[256,384]{1,0:T(8,128)(2,1)S(1)} %get-tuple-element.118.queries, bf16[256,640]{1,0:T(8,128)(2,1)S(1)} %collective-permute-done.6.outer, bf16[256,640]{1,0:T(8,128)(2,1)S(1)} %get-tuple-element.119.here, ...), custom_call_target="tpu_custom_call" | custom-call | bytes 29600000 | tf_op jit(solution)/shard_map/cond/branch_0_fun/pallas_call | solution.py:239
  96.4 2.2 %collective-permute-start.8 = (bf16[64,640]{1,0:T(8,128)(2,1)S(1)}, bf16[64,640]{1,0:T(8,128)(2,1)S(1)}, u32[]{:S(2)}, u32[]{:S(2)}) collective-permute-start(bf16[64,640]{1,0:T(8,128)(2,1)S(1)} %dynamic-slice_bitcast_fusion.1), channel_id=1, source_target_pairs={{0,8},{1,9},{2,10},{3,11},{4,12},{5,13},{6,14},{7,15},{8,0},{9,1},... | collective-permute-start | bytes 245768 | tf_op jit(solution)/shard_map/cond/branch_0_fun/ppermute | solution.py:225
  98.6 3.0 %branch_0_fun.9 = bf16[640,1152]{1,0:T(8,128)(2,1)} custom-call(s32[5]{0:T(128)S(1)} %get-tuple-element.104.spot, bf16[4,80,1152]{2,1,0:T(8,128)(2,1)} %get-tuple-element.122.mine, bf16[4,80,1152]{2,1,0:T(8,128)(2,1)S(1)} %collective-permute-done.9.other), custom_call_target="tpu_custom_call" | custom-call | bytes 1 | tf_op jit(solution)/shard_map/cond/branch_0_fun/pallas_call | solution.py:239
  101.6 2.7 %shard_map.68 = bf16[2,64,1152]{2,1,0:T(8,128)(2,1)} custom-call(s32[5]{0:T(128)S(1)} %stack.23.spot, bf16[2,64,640]{2,1,0:T(8,128)(2,1)S(1)} %get-tuple-element.168.attended, bf16[64,640]{1,0:T(8,128)(2,1)S(1)} %get-tuple-element.169.side, bf16[640,1152]{1,0:T(8,128)(2,1)} %get-tuple-element.170.head_rows, bf16[2,64,1152]{2,1,0:T(8,128)(2,1)S(1)} %bitcast.44, ...), custom_call_target="tpu_custom_call" | custom-call | bytes 1 | tf_op jit(solution)/shard_map/pallas_call | solution.py:239
  (46 shorter events, 8.7 us)
Async XLA Ops:
  0.0 1.0 copy-start
  1.0 7.9 %copy-start.1 = (bf16[1,2,8,8,1152]{4,3,2,1,0:T(8,128)(2,1)S(1)}, bf16[1,2,8,8,1152]{4,3,2,1,0:T(8,128)(2,1)}, u32[]{:S(2)}) copy-start(bf16[1,2,8,8,1152]{4,3,2,1,0:T(8,128)(2,1)} %param.12) | copy-start | bytes 884740
  1.0 10.5 %copy-start.8 = (f32[2,3,1152]{2,0,1:T(2,128)S(1)}, f32[2,3,1152]{2,0,1:T(2,128)}, u32[]{:S(2)}) copy-start(f32[2,3,1152]{2,0,1:T(2,128)} %param.13) | copy-start | bytes 82948
  3.2 20.4 %collective-permute-start.13 = (bf16[240,1152]{1,0:T(8,128)(2,1)S(1)}, bf16[240,1152]{1,0:T(8,128)(2,1)S(1)}, u32[]{:S(2)}, u32[]{:S(2)}) collective-permute-start(bf16[240,1152]{1,0:T(8,128)(2,1)S(1)} %fusion.2.refs_0_), channel_id=1, source_target_pairs={{0,6},{1,7},{2,4},{3,5},{4,2},{5,3},{6,0},{7,1},{8,14},{9,15},{10,... | collective-permute-start | bytes 1658888 | tf_op jit(solution)/shard_map/ppermute | solution.py:225
  7.4 24.9 %collective-permute-start.15 = (bf16[240,1152]{1,0:T(8,128)(2,1)S(1)}, bf16[240,1152]{1,0:T(8,128)(2,1)S(1)}, u32[]{:S(2)}, u32[]{:S(2)}) collective-permute-start(bf16[240,1152]{1,0:T(8,128)(2,1)S(1)} %fusion.2.refs_0_), channel_id=1, source_target_pairs={{0,2},{1,3},{2,0},{3,1},{4,6},{5,7},{6,4},{7,5},{8,10},{9,11},{10,... | collective-permute-start | bytes 1658888 | tf_op jit(solution)/shard_map/ppermute | solution.py:225
  8.9 13.9 %collective-permute-start.10 = (bf16[2,64,1152]{2,1,0:T(8,128)(2,1)S(1)}, bf16[2,64,1152]{2,1,0:T(8,128)(2,1)S(1)}, u32[]{:S(2)}, u32[]{:S(2)}) collective-permute-start(bf16[2,64,1152]{2,1,0:T(8,128)(2,1)S(1)} %bitcast.40), channel_id=1, source_target_pairs={{0,16},{1,17},{2,18},{3,19},{4,20},{5,21},{6,22},{7,23},{8,24},{9,... | collective-permute-start | bytes 884744 | tf_op jit(solution)/shard_map/ppermute | solution.py:225
  10.2 24.0 %collective-permute-start.12 = (bf16[2,64,1152]{2,1,0:T(8,128)(2,1)S(1)}, bf16[2,64,1152]{2,1,0:T(8,128)(2,1)S(1)}, u32[]{:S(2)}, u32[]{:S(2)}) collective-permute-start(bf16[2,64,1152]{2,1,0:T(8,128)(2,1)S(1)} %bitcast.41), channel_id=1, source_target_pairs={{16,8},{17,9},{18,10},{19,11},{20,12},{21,13},{22,14},{23,15},{24,... | collective-permute-start | bytes 884744 | tf_op jit(solution)/shard_map/ppermute | solution.py:225
  23.6 19.5 %collective-permute-start.14 = (bf16[240,1152]{1,0:T(8,128)(2,1)S(1)}, bf16[240,1152]{1,0:T(8,128)(2,1)S(1)}, u32[]{:S(2)}, u32[]{:S(2)}) collective-permute-start(bf16[240,1152]{1,0:T(8,128)(2,1)S(1)} %collective-permute-done.13.refs_1_), channel_id=1, source_target_pairs={{0,2},{1,3},{2,0},{3,1},{4,6},{5,7},{6,4},{7,5},{8,10},{9,11},{10,... | collective-permute-start | bytes 1658888 | tf_op jit(solution)/shard_map/ppermute | solution.py:225
  30.9 6.9 %collective-permute-start.11 = (bf16[2,64,1152]{2,1,0:T(8,128)(2,1)S(1)}, bf16[2,64,1152]{2,1,0:T(8,128)(2,1)S(1)}, u32[]{:S(2)}, u32[]{:S(2)}) collective-permute-start(bf16[2,64,1152]{2,1,0:T(8,128)(2,1)S(1)} %broadcast_select_fusion), channel_id=1, source_target_pairs={{0,8},{1,9},{2,10},{3,11},{4,12},{5,13},{6,14},{7,15},{8,0},{9,1},... | collective-permute-start | bytes 884744 | tf_op jit(solution)/shard_map/ppermute | solution.py:225
  34.1 10.3 %copy-start.5 = (bf16[2,64,1152]{2,1,0:T(8,128)(2,1)}, bf16[2,64,1152]{2,1,0:T(8,128)(2,1)S(1)}, u32[]{:S(2)}) copy-start(bf16[2,64,1152]{2,1,0:T(8,128)(2,1)S(1)} %collective-permute-done.12) | copy-start | bytes 884740
  37.8 9.7 %copy-start.3 = (bf16[2,64,1152]{2,1,0:T(8,128)(2,1)}, bf16[2,64,1152]{2,1,0:T(8,128)(2,1)S(1)}, u32[]{:S(2)}) copy-start(bf16[2,64,1152]{2,1,0:T(8,128)(2,1)S(1)} %collective-permute-done.11) | copy-start | bytes 884740
  43.1 7.5 %copy-start.2 = (f32[128,384]{1,0:T(8,128)S(1)}, f32[128,384]{1,0:T(8,128)}, u32[]{:S(2)}) copy-start(f32[128,384]{1,0:T(8,128)} %shard_map.64) | copy-start | bytes 589828
  44.5 6.1 %collective-permute-start.16 = (bf16[4,240,1152]{2,1,0:T(8,128)(2,1)}, bf16[4,240,1152]{2,1,0:T(8,128)(2,1)}, u32[]{:S(2)}, u32[]{:S(2)}) collective-permute-start(bf16[4,240,1152]{2,1,0:T(8,128)(2,1)} %get-tuple-element.158), channel_id=1, source_target_pairs={{0,1},{1,0},{2,3},{3,2},{4,5},{5,4},{6,7},{7,6},{8,9},{9,8},{10,11... | collective-permute-start | bytes 6635528 | tf_op jit(solution)/shard_map/ppermute | solution.py:225
  46.2 20.3 %collective-permute-start.19 = (bf16[4,80,1152]{2,1,0:T(8,128)(2,1)}, bf16[4,80,1152]{2,1,0:T(8,128)(2,1)}, u32[]{:S(2)}, u32[]{:S(2)}) collective-permute-start(bf16[4,80,1152]{2,1,0:T(8,128)(2,1)} %get-tuple-element.161), channel_id=1, source_target_pairs={{16,0},{17,1},{18,2},{19,3},{20,4},{21,5},{22,6},{23,7},{24,8},{25... | collective-permute-start | bytes 2211848 | tf_op jit(solution)/shard_map/ppermute | solution.py:225
  47.5 16.9 %collective-permute-start.20 = (bf16[4,64,1152]{2,1,0:T(8,128)(2,1)S(1)}, bf16[4,64,1152]{2,1,0:T(8,128)(2,1)}, u32[]{:S(2)}, u32[]{:S(2)}) collective-permute-start(bf16[4,64,1152]{2,1,0:T(8,128)(2,1)S(1)} %get-tuple-element.162), channel_id=1, source_target_pairs={{0,8},{1,9},{2,10},{3,11},{4,12},{5,13},{6,14},{7,15},{8,0},{9,1},... | collective-permute-start | bytes 1769480 | tf_op jit(solution)/shard_map/ppermute | solution.py:225
  53.6 20.5 %collective-permute-start.17 = (bf16[2,64,640]{2,1,0:T(8,128)(2,1)S(1)}, bf16[2,64,640]{2,1,0:T(8,128)(2,1)S(1)}, u32[]{:S(2)}, u32[]{:S(2)}) collective-permute-start(bf16[2,64,640]{2,1,0:T(8,128)(2,1)S(1)} %get-tuple-element.160), channel_id=1, source_target_pairs={{16,0},{17,1},{18,2},{19,3},{20,4},{21,5},{22,6},{23,7},{24,8},{25... | collective-permute-start | bytes 491528 | tf_op jit(solution)/shard_map/ppermute | solution.py:225
  54.9 19.2 %collective-permute-start.18 = (bf16[2,64,640]{2,1,0:T(8,128)(2,1)S(1)}, bf16[2,64,640]{2,1,0:T(8,128)(2,1)}, u32[]{:S(2)}, u32[]{:S(2)}) collective-permute-start(bf16[2,64,640]{2,1,0:T(8,128)(2,1)S(1)} %get-tuple-element.160), channel_id=1, source_target_pairs={{16,8},{17,9},{18,10},{19,11},{20,12},{21,13},{22,14},{23,15},{24,... | collective-permute-start | bytes 491528 | tf_op jit(solution)/shard_map/ppermute | solution.py:225
  66.5 7.6 %copy-start.4 = (bf16[2,64,1152]{2,1,0:T(8,128)(2,1)S(1)}, bf16[2,64,1152]{2,1,0:T(8,128)(2,1)}, u32[]{:S(2)}) copy-start(bf16[2,64,1152]{2,1,0:T(8,128)(2,1)} %copy-done.3) | copy-start | bytes 884740
  66.5 7.6 %copy-start.6 = (bf16[2,64,1152]{2,1,0:T(8,128)(2,1)S(1)}, bf16[2,64,1152]{2,1,0:T(8,128)(2,1)}, u32[]{:S(2)}) copy-start(bf16[2,64,1152]{2,1,0:T(8,128)(2,1)} %copy-done.5) | copy-start | bytes 884740
  66.5 7.1 %collective-permute-start.3 = (bf16[4,80,1152]{2,1,0:T(8,128)(2,1)}, bf16[4,80,1152]{2,1,0:T(8,128)(2,1)}, u32[]{:S(2)}, u32[]{:S(2)}) collective-permute-start(bf16[4,80,1152]{2,1,0:T(8,128)(2,1)} %get-tuple-element.94), channel_id=1, source_target_pairs={{0,1},{1,0},{2,3},{3,2},{4,5},{5,4},{6,7},{7,6},{8,9},{9,8},{10,11... | collective-permute-start | bytes 2211848 | tf_op jit(solution)/shard_map/cond/branch_0_fun/ppermute | solution.py:225
  69.3 4.2 %collective-permute-start.2 = (bf16[4,64,1152]{2,1,0:T(8,128)(2,1)}, bf16[4,64,1152]{2,1,0:T(8,128)(2,1)}, u32[]{:S(2)}, u32[]{:S(2)}) collective-permute-start(bf16[4,64,1152]{2,1,0:T(8,128)(2,1)} %get-tuple-element.93), channel_id=1, source_target_pairs={{0,1},{1,0},{2,3},{3,2},{4,5},{5,4},{6,7},{7,6},{8,9},{9,8},{10,11... | collective-permute-start | bytes 1769480 | tf_op jit(solution)/shard_map/cond/branch_0_fun/ppermute | solution.py:225
  74.1 3.2 %copy-start.7 = (bf16[2,64,640]{2,1,0:T(8,128)(2,1)}, bf16[2,64,640]{2,1,0:T(8,128)(2,1)S(1)}, u32[]{:S(2)}) copy-start(bf16[2,64,640]{2,1,0:T(8,128)(2,1)S(1)} %get-tuple-element.109.near) | copy-start | bytes 491524 | tf_op jit(solution)/shard_map/cond
  74.2 24.4 %collective-permute-start.9 = (bf16[4,80,1152]{2,1,0:T(8,128)(2,1)}, bf16[4,80,1152]{2,1,0:T(8,128)(2,1)S(1)}, u32[]{:S(2)}, u32[]{:S(2)}) collective-permute-start(bf16[4,80,1152]{2,1,0:T(8,128)(2,1)} %get-tuple-element.122.mine), channel_id=1, source_target_pairs={{0,8},{1,9},{2,10},{3,11},{4,12},{5,13},{6,14},{7,15},{8,0},{9,1},... | collective-permute-start | bytes 2211848 | tf_op jit(solution)/shard_map/cond/branch_0_fun/ppermute | solution.py:225
  84.0 10.3 %collective-permute-start.6 = (bf16[256,640]{1,0:T(8,128)(2,1)S(1)}, bf16[256,640]{1,0:T(8,128)(2,1)S(1)}, u32[]{:S(2)}, u32[]{:S(2)}) collective-permute-start(bf16[256,640]{1,0:T(8,128)(2,1)S(1)} %get-tuple-element.119.here), channel_id=1, source_target_pairs={{1,2},{2,1},{3,4},{4,3},{5,6},{6,5},{9,10},{10,9},{11,12},{12,11},... | collective-permute-start | bytes 983048 | tf_op jit(solution)/shard_map/cond/branch_0_fun/ppermute | solution.py:225
  89.2 5.0 %collective-permute-start.7 = (bf16[256,640]{1,0:T(8,128)(2,1)S(1)}, bf16[256,640]{1,0:T(8,128)(2,1)S(1)}, u32[]{:S(2)}, u32[]{:S(2)}) collective-permute-start(bf16[256,640]{1,0:T(8,128)(2,1)S(1)} %get-tuple-element.119.here), channel_id=1, source_target_pairs={{0,1},{1,0},{2,3},{3,2},{4,5},{5,4},{6,7},{7,6},{8,9},{9,8},{10,11... | collective-permute-start | bytes 983048 | tf_op jit(solution)/shard_map/cond/branch_0_fun/ppermute | solution.py:225
  96.4 5.2 %collective-permute-start.8 = (bf16[64,640]{1,0:T(8,128)(2,1)S(1)}, bf16[64,640]{1,0:T(8,128)(2,1)S(1)}, u32[]{:S(2)}, u32[]{:S(2)}) collective-permute-start(bf16[64,640]{1,0:T(8,128)(2,1)S(1)} %dynamic-slice_bitcast_fusion.1), channel_id=1, source_target_pairs={{0,8},{1,9},{2,10},{3,11},{4,12},{5,13},{6,14},{7,15},{8,0},{9,1},... | collective-permute-start | bytes 245768 | tf_op jit(solution)/shard_map/cond/branch_0_fun/ppermute | solution.py:225
